TPU v7x, 32 devices: a whole 2x2x4 slice. The times are simulated.
32 devices in a mesh: groups: 2 (over y), image: 16 (over z, x, core).
Axes of the slice: x: 2, y: 2, z: 4, core: 2. Of those that a mesh axis runs over, the one named last changes fastest.
Arguments:
- vision: bfloat16 [32, 256, 8192], P(('groups', 'image')), parts along dimension 0, may hold values from -6 to 6
- queries: bfloat16 [32, 4096], P(('groups', 'image')), parts along dimension 0, may hold values from -480 to 480
- text_request: int32 [32], P(('groups', 'image')), parts along dimension 0, may hold values from 0 to 7, never falling along the last dimension, each value on 1 to 4 neighbouring positions
- key_weight: bfloat16 [8192, 512], P('image'), may hold values from -0.0625 to 0.0625
- value_weight: bfloat16 [8192, 512], P('image'), may hold values from -0.0625 to 0.0625
- key_gain: float32 [128], replicated, may hold values from 0.25 to 1.75
- down_pages: bfloat16 [8192, 256], P('image'), may hold values from -0.0625 to 0.0625
- up_pages: bfloat16 [16, 16, 512], replicated, may hold values from -1.5 to 1.5
- image_request: int32 [32, 1], P(('groups', 'image')), parts along dimension 0, may hold values from 0 to 7
- image_tiles: int32 [32], P(('groups', 'image')), parts along dimension 0, may hold values from 1 to 4
- request_tenant: int32 [16], P('groups'), parts along dimension 0, may hold values from 0 to 15
- tenant_page: int32 [16], replicated, may hold values from 0 to 15, each once
Outputs:
- attended: bfloat16 [32, 4096], P(('groups', 'image')), parts along dimension 0
There are 2 independent parts, one for each index of `groups`. A program takes and returns all parts, laid end to end along the dimension named above; an argument that names none is the same for every part. Nothing has to cross between parts.
Inputs may be any that keep to these rules, and one draw needn't show every extreme that they name: `text_request`: each request's text tokens are consecutive, 1 to 4 of them, requests in increasing order. `image_request`: every request owns at least one image. `tenant_page`: each page once.
All inputs are finite; a program needn't handle non-finite values.
Results may differ from a plain program's by a relative error of at most 0.012.
The roundings to bfloat16 on the way count: a program that leaves them out, or rounds other values in their place, can miss the bound.
Values may be sent and summed in bfloat16 or wider, within the bound.
No kernel may reach another device: no remote copies, remote signals or barrier semaphores. Data moves between devices by JAX's collectives and lax.ppermute only.
A program may use at most 128 MiB of HBM per device.

v0:
```python
import jax
import jax.numpy as jnp
from jax import lax
from jax.sharding import PartitionSpec as P

HEAD = 128
KV_HEADS = 4
TILES = 4


epsilon = 1e-05
masked_score = -1e30


def select_entry(table, position):
    matches = jnp.arange(table.shape[0], dtype=jnp.int32) == position
    return jnp.sum(jnp.where(matches, table, 0))


def local(
    vision,
    queries,
    text_request,
    key_weight,
    value_weight,
    key_gain,
    down_pages,
    up_pages,
    image_request,
    image_tiles,
    request_tenant,
    tenant_page,
):
    image_tokens = vision[0]
    key_count = image_tokens.shape[0]
    kv_width = key_weight.shape[1]
    low_rank = up_pages.shape[1]
    owner_id = image_request[0, 0]
    tenant_id = select_entry(request_tenant, owner_id)
    page_id = select_entry(tenant_page, tenant_id)

    def token_columns():
        return image_tokens

    pieces = (
        lax.all_gather(key_weight, "image", axis=0, tiled=True),
        lax.all_gather(value_weight, "image", axis=0, tiled=True),
    )
    columns = token_columns()
    key_raw = jnp.dot(columns, pieces[0], preferred_element_type=jnp.float32)
    value_raw = jnp.dot(columns, pieces[1], preferred_element_type=jnp.float32)
    columns = token_columns()
    lowrank_sum = jnp.dot(
        columns,
        lax.dynamic_slice_in_dim(
            lax.all_gather(down_pages, "image", axis=0, tiled=True), page_id * low_rank, low_rank, 1
        ),
        preferred_element_type=jnp.float32,
    )
    lowrank = lowrank_sum.astype(jnp.bfloat16)
    up_factor = lax.dynamic_index_in_dim(up_pages, page_id, 0, keepdims=False)
    value_block = (
        value_raw + jnp.dot(lowrank, up_factor, preferred_element_type=jnp.float32)
    ).astype(jnp.bfloat16)
    key_heads = key_raw.reshape(key_count, KV_HEADS, HEAD)
    inverse_rms = lax.rsqrt(jnp.mean(key_heads * key_heads, axis=-1, keepdims=True) + epsilon)
    key_block = (
        (key_heads * inverse_rms * key_gain).reshape(key_count, kv_width).astype(jnp.bfloat16)
    )
    every_query, every_request = (
        lax.all_gather(queries, "image", axis=0, tiled=True),
        lax.all_gather(text_request, "image", axis=0, tiled=True),
    )
    text_total = every_query.shape[0]
    own_count = queries.shape[0]
    window = min(4 * own_count, text_total)
    head_group = every_query.shape[1] // kv_width
    q_count = KV_HEADS * head_group
    first_token = jnp.sum((every_request < owner_id).astype(jnp.int32))
    first_token = jnp.minimum(first_token, text_total - window)
    window_query = lax.dynamic_slice_in_dim(every_query, first_token, window, 0)
    window_request = lax.dynamic_slice_in_dim(every_request, first_token, window, 0)
    query_heads = window_query.reshape(window, KV_HEADS, head_group, HEAD)
    positions = jnp.arange(key_count, dtype=jnp.int32)
    usable = (window_request[:, None] == owner_id) & (
        positions[None, :] < image_tiles[0] * (key_count // TILES)
    )
    scores = jnp.einsum(
        "tkgd,vkd->tkgv",
        query_heads,
        key_block.reshape(key_count, KV_HEADS, HEAD),
        preferred_element_type=jnp.float32,
    ) * HEAD ** (-0.5)
    scores = jnp.where(usable[:, None, None, :], scores, masked_score)
    window_max = jnp.max(scores, axis=-1).reshape(window, q_count)
    every_max = lax.dynamic_update_slice_in_dim(
        jnp.full((text_total, q_count), masked_score, jnp.float32), window_max, first_token, 0
    )
    top_score = lax.pmax(every_max, "image")
    window_top = lax.dynamic_slice_in_dim(top_score, first_token, window, 0).reshape(
        window, KV_HEADS, head_group
    )
    weights = jnp.where(
        usable[:, None, None, :], jnp.exp(scores - window_top[..., None]), 0.0
    ).astype(jnp.bfloat16)
    totals = jnp.sum(weights, axis=-1, dtype=jnp.float32).reshape(window, q_count)
    numerator = jnp.einsum(
        "tkgv,vkd->tkgd",
        weights,
        value_block.reshape(key_count, KV_HEADS, HEAD),
        preferred_element_type=jnp.float32,
    ).reshape(window, q_count * HEAD)
    my_first = lax.axis_index("image") * own_count
    own_tokens = my_first + jnp.arange(own_count, dtype=jnp.int32)
    window_slots = jnp.arange(window, dtype=jnp.int32)
    start_value = first_token.astype(jnp.float32).reshape(1)
    pieces = (
        lax.all_gather(numerator, "image", axis=0, tiled=True),
        lax.all_gather(totals, "image", axis=0, tiled=True),
        lax.all_gather(start_value, "image", axis=0, tiled=True),
    )
    piece_count = pieces[2].shape[0]
    starts = pieces[2].astype(jnp.int32)
    offsets = own_tokens[None, :] - starts[:, None]
    chooser = (window_slots[None, None, :] == offsets[:, :, None]).astype(jnp.float32)
    numer_piece = pieces[0].reshape(piece_count, window, -1)
    totals_piece = pieces[1].reshape(piece_count, window, -1)
    numer_own = jnp.einsum("jrw,jwc->rc", chooser, numer_piece, precision=lax.Precision.HIGHEST)
    totals_own = jnp.einsum("jrw,jwc->rc", chooser, totals_piece, precision=lax.Precision.HIGHEST)
    attended = numer_own.reshape(own_count, -1, HEAD) / totals_own[..., None]
    return attended.reshape(own_count, -1).astype(jnp.bfloat16)


def solution(mesh):
    in_specs = (
        P(("groups", "image"), None, None),
        P(("groups", "image"), None),
        P(("groups", "image")),
        P("image", None),
        P("image", None),
        P(),
        P("image", None),
        P(),
        P(("groups", "image"), None),
        P(("groups", "image")),
        P("groups"),
        P(),
    )
    out_specs = P(("groups", "image"), None)
    return jax.shard_map(local, mesh=mesh, in_specs=in_specs, out_specs=out_specs, check_vma=False)
```

profile of v0, /device:TPU:0, one launch (start us, length us, event | category | flops | bytes accessed | tf_op | source)
XLA Modules:
  0.0 311.2 jit_solution(8050046615734723408)
XLA Ops:
  6.5 0.0 copy-start
  6.5 0.0 all-gather.12.cloned.1.call-start
  6.5 0.7 all-gather.12.cloned.1.call-update
  7.3 0.0 all-gather.8.cloned.1.call-start
  7.3 0.7 all-gather.8.cloned.1.call-update
  8.0 0.0 all-gather.10.cloned.1.call-start
  8.1 0.7 all-gather.10.cloned.1.call-update
  8.7 0.0 all-gather.14.cloned.1.call-start
  9.4 1.3 dynamic-slice
  10.8 0.8 dynamic-update-slice
  11.5 14.3 %all-reduce = s32[16]{0:T(128)S(1)} all-reduce(s32[16]{0:T(128)S(1)} %dynamic-update-slice), channel_id=1, replica_groups=mesh['groups'=2,'image'=16] {'image'}, use_global_device_ids=true, to_apply=%add | all-reduce | flops 16 | bytes 128
  26.5 1.4 fusion.38
  27.8 2.0 fusion.39
  31.5 0.7 fusion.37
  34.1 19.0 %all-gather = bf16[16,1,4096]{2,1,0:T(2,128)(2,1)S(1)} all-gather(bf16[1,1,4096]{2,1,0:T(2,128)(2,1)} %bitcast.79), channel_id=1, replica_groups=mesh['groups'=2,'image'=16] {'image'}, dimensions={0}, use_global_device_ids=true | all-gather | bytes 139264 | tf_op jit(solution)/shard_map/all_gather | solution.py:71
  53.2 0.2 dynamic-slice_reduce_fusion
  53.4 0.1 dynamic-slice_compare_fusion
  53.4 0.1 broadcast_and_fusion
  53.5 34.3 %all-gather.12.cloned.1.call-done = bf16[8192,512]{1,0:T(8,128)(2,1)} async-done(((bf16[512,512]{1,0:T(8,128)(2,1)}), bf16[8192,512]{1,0:T(8,128)(2,1)}) %all-gather.12.cloned.1.call-update) | async-done | bytes 8388624 | tf_op jit(solution)/shard_map/all_gather | solution.py:46
  87.8 11.4 %copy.23 = bf16[512,8192]{1,0:T(8,128)(2,1)} copy(bf16[512,8192]{0,1:T(8,128)(2,1)} %bitcast.73) | data formatting | bytes 16777216 | tf_op jit(solution)/shard_map/dot_general | solution.py:50
  99.2 7.1 %multiply_reduce_fusion = (f32[256,4]{0,1:T(4,128)S(1)}, f32[256,4,128]{0,2,1:T(8,128)S(1)}) fusion(bf16[4,128,8192]{2,1,0:T(8,128)(2,1)} %bitcast.74, bf16[1,256,8192]{2,1,0:T(8,128)(2,1)} %param.12), kind=kOutput, calls=%fused_computation.18 | convolution fusion | flops 2147744768 | bytes 13111296 | tf_op jit(solution)/shard_map/dot_general | solution.py:50
  106.3 57.1 %all-gather.8.cloned.1.call-done = bf16[8192,512]{1,0:T(8,128)(2,1)} async-done(((bf16[512,512]{1,0:T(8,128)(2,1)}), bf16[8192,512]{1,0:T(8,128)(2,1)}) %all-gather.8.cloned.1.call-update) | async-done | bytes 8388624 | tf_op jit(solution)/shard_map/all_gather | solution.py:47
  163.4 7.0 %fusion.4 = f32[256,512]{1,0:T(8,128)S(1)} fusion(bf16[8192,512]{1,0:T(8,128)(2,1)} %all-gather.8.cloned.1.call-done, bf16[1,256,8192]{2,1,0:T(8,128)(2,1)} %param.12), kind=kOutput, calls=%fused_computation.4 | convolution fusion | flops 2147483648 | bytes 13107200 | tf_op jit(solution)/shard_map/dot_general | solution.py:51
  170.3 0.0 copy-start.1
  170.3 44.0 %all-gather.10.cloned.1.call-done = bf16[8192,256]{1,0:T(8,128)(2,1)} async-done(((bf16[512,256]{1,0:T(8,128)(2,1)}), bf16[8192,256]{1,0:T(8,128)(2,1)}) %all-gather.10.cloned.1.call-update) | async-done | bytes 4194320 | tf_op jit(solution)/shard_map/all_gather | solution.py:56
  214.4 0.0 copy-done
  214.4 5.2 %fusion.7 = bf16[256,512]{1,0:T(8,128)(2,1)S(1)} fusion(f32[256,512]{1,0:T(8,128)S(1)} %fusion.4, bf16[1,256,8192]{2,1,0:T(8,128)(2,1)} %param.12, bf16[8192,256]{1,0:T(8,128)(2,1)} %all-gather.10.cloned.1.call-done, s32[]{:T(128)S(6)} %select_n.30, bf16[16,16,512]{2,1,0:T(8,128)(2,1)S(1)} %copy-done, s32[]{:T(128)S(6)} %select_n.31), kind=kOutput, calls=%fused_computation.8 | convolution fusion | flops 71569408 | bytes 7094280 | tf_op jit(solution)/shard_map/dot_general | solution.py:63
  219.6 0.1 reshape.168
  219.6 0.0 copy-done.1
  219.7 0.3 fusion.41
  220.0 0.1 reshape.170
  220.1 0.1 dynamic_update_slice.3
  220.2 31.7 %pmax.7 = f32[16,32]{1,0:T(8,128)S(1)} all-reduce(f32[16,32]{1,0:T(8,128)S(1)} %dynamic_update_slice.3), channel_id=1, replica_groups=mesh['groups'=2,'image'=16] {'image'}, use_global_device_ids=true, to_apply=%region_5.6 | all-reduce | flops 512 | bytes 4096 | tf_op jit(solution)/shard_map/pmax | solution.py:99
  251.9 0.1 sub.21
  252.0 0.2 convolution_bitcast_fusion
  252.2 0.6 reshape.183
  252.8 0.0 all-gather.14.cloned.1.call-update
  252.9 0.8 dynamic-update-slice.1
  253.6 29.6 %all-reduce.1 = f32[16]{0:T(128)S(1)} all-reduce(f32[16]{0:T(128)S(1)} %dynamic-update-slice.1), channel_id=1, replica_groups=mesh['groups'=2,'image'=16] {'image'}, use_global_device_ids=true, to_apply=%add.1 | all-reduce | flops 16 | bytes 128
  283.3 0.2 convert_reduce_fusion
  283.5 0.1 reshape.185
  283.6 17.2 %all-gather.2 = f32[16,4,32]{2,1,0:T(4,128)S(1)} all-gather(f32[1,4,32]{2,1,0:T(4,128)S(1)} %reshape.185), channel_id=1, replica_groups=mesh['groups'=2,'image'=16] {'image'}, dimensions={0}, use_global_device_ids=true | all-gather | bytes 8704 | tf_op jit(solution)/shard_map/all_gather | solution.py:119
  300.8 0.2 convolution_bitcast_fusion.1
  301.0 0.0 all-gather.14.cloned.1.call-done
  301.0 2.0 dot_general.41
  302.9 1.1 fusion.19
  304.0 0.1 fusion.30
  304.1 0.6 copy.62
  (12 shorter events, 0.1 us)
Async XLA Ops:
  6.5 207.8 %copy-start = (bf16[16,16,512]{2,1,0:T(8,128)(2,1)S(1)}, bf16[16,16,512]{2,1,0:T(8,128)(2,1)}, u32[]{:S(2)}) copy-start(bf16[16,16,512]{2,1,0:T(8,128)(2,1)} %param.19) | copy-start | bytes 786436
  6.5 81.3 %all-gather.12.cloned.1.call-start = ((), (), s32[]{:S(2)}) async-start(), calls=%async_computation.2 | async-start | bytes 8912896 | tf_op jit(solution)/shard_map/all_gather | solution.py:46
  7.3 156.1 %all-gather.8.cloned.1.call-start = ((), (), s32[]{:S(2)}) async-start(), calls=%async_computation | async-start | bytes 8912896 | tf_op jit(solution)/shard_map/all_gather | solution.py:47
  8.0 206.4 %all-gather.10.cloned.1.call-start = ((), (), s32[]{:S(2)}) async-start(), calls=%async_computation.1 | async-start | bytes 4456448 | tf_op jit(solution)/shard_map/all_gather | solution.py:56
  8.7 292.2 %all-gather.14.cloned.1.call-start = ((), (), s32[]{:S(2)}) async-start(), calls=%async_computation.3 | async-start | bytes 1114112 | tf_op jit(solution)/shard_map/all_gather | solution.py:118
  170.3 49.3 %copy-start.1 = (f32[128]{0:T(128)S(1)}, f32[128]{0:T(128)}, u32[]{:S(2)}) copy-start(f32[128]{0:T(128)} %param.17) | copy-start | bytes 1540
Sparse Core Ops, SparseCore 0:
  9.5 78.2 all-gather.11
  90.0 73.3 all-gather.7
  165.5 48.7 all-gather.9
  253.0 35.1 all-gather.13
where the time goes:
time: 312 us; the launch traced here: 311 us
  waiting for transfers between devices  138 us (44%)
  blocking collectives  112 us (36%)
  matrix products  21 us (7%)
  between operations  18.2 us (6%)
  local copies, waits for them, and re-layouts  18.1 us (6%)
  other arithmetic  4.51 us (1%)
    all_gather x1, waiting for transfers between devices, local(): lax.all_gather(value_weight, 'image', axis=0, tiled=True)  57.1 us
    all_gather x1, waiting for transfers between devices, local(): lax.all_gather(down_pages, 'image', axis=0, tiled=True)  44 us
    unnamed x2, blocking collectives  43.9 us
    all_gather x1, waiting for transfers between devices, local(): lax.all_gather(key_weight, 'image', axis=0, tiled=True)  34.3 us
    pmax x1, blocking collectives, local(): top_score = lax.pmax(every_max, 'image')  31.7 us
    all_gather x1, blocking collectives, local(): lax.all_gather(queries, 'image', axis=0, tiled=True)  19 us
    all_gather x1, blocking collectives, local(): lax.all_gather(totals, 'image', axis=0, tiled=True)  17.2 us
    dot_general x1, local copies, waits for them, and re-layouts, local(): key_raw = jnp.dot(columns, pieces[0], preferred_element_type=jnp.float32)  11.4 us
  transfers between devices with their start and end apart: 4, of which 3 were waited for; matrix products, arithmetic and copies ran while one was open for 11% of the time, Pallas kernels for 0%

commit v1 on v0

--- a/solution.py
+++ b/solution.py
@@ -1,6 +1,10 @@
+import functools
+
 import jax
 import jax.numpy as jnp
 from jax import lax
+from jax.experimental import pallas as pl
+from jax.experimental.pallas import tpu as pltpu
 from jax.sharding import PartitionSpec as P
 
 HEAD = 128
@@ -17,7 +21,7 @@
     return jnp.sum(jnp.where(matches, table, 0))
 
 
-def local(
+def local_gathered(
     vision,
     queries,
     text_request,
@@ -131,6 +135,469 @@
     return attended.reshape(own_count, -1).astype(jnp.bfloat16)
 
 
+CORES = 2
+COLUMNS = 2
+PLANE = CORES * COLUMNS
+EXTRA = 16
+WINDOW = 4
+MESSAGE = 40
+
+
+def after(value, *others):
+    return lax.optimization_barrier((value,) + others)[0]
+
+
+def whole(count, space=pltpu.VMEM):
+    return [pl.BlockSpec(memory_space=space)] * count
+
+
+def call(kernel, out_shape, in_specs, scratch=(), vmem=16, flops=0, moved=0):
+    outs = out_shape if isinstance(out_shape, (list, tuple)) else [out_shape]
+    specs = [pl.BlockSpec(memory_space=pltpu.VMEM)] * len(outs)
+    return pl.pallas_call(
+        kernel,
+        out_shape=out_shape,
+        in_specs=in_specs,
+        out_specs=specs if isinstance(out_shape, (list, tuple)) else specs[0],
+        scratch_shapes=list(scratch),
+        compiler_params=pltpu.CompilerParams(vmem_limit_bytes=vmem * 2**20),
+        cost_estimate=pl.CostEstimate(flops=flops, bytes_accessed=moved, transcendentals=0),
+    )
+
+
+def split_kernel(place_ref, vision_ref, out_ref):
+    out_ref[...] = vision_ref[...]
+
+
+def split_vision(vision, core, rows):
+    keys, depth = vision.shape
+    shards = depth // rows // CORES
+    return pl.pallas_call(
+        split_kernel,
+        out_shape=jax.ShapeDtypeStruct((keys, shards * rows), vision.dtype),
+        grid_spec=pltpu.PrefetchScalarGridSpec(
+            num_scalar_prefetch=1,
+            grid=(shards,),
+            in_specs=[pl.BlockSpec((keys, rows), lambda i, place: (0, CORES * i + 1 - place[0]))],
+            out_specs=pl.BlockSpec((keys, rows), lambda i, place: (0, i)),
+        ),
+        cost_estimate=pl.CostEstimate(flops=0, bytes_accessed=keys * depth * 2, transcendentals=0),
+    )(core.reshape(1), vision)
+
+
+def prepare_kernel(half, place_ref, text_ref, image_ref, tenant_ref, page_ref, queries_ref, key_ref, out_ref):
+    start = pl.multiple_of(place_ref[0] * half, half)
+    out_ref[0:half, :] = key_ref[pl.ds(start, half), :]
+    width = key_ref.shape[1]
+    owner = image_ref[0, 0]
+    page = page_ref[tenant_ref[owner]]
+    row = lax.broadcasted_iota(jnp.int32, (EXTRA, width), 0)
+    lane = lax.broadcasted_iota(jnp.int32, (EXTRA, width), 1)
+    block = jnp.zeros((EXTRA, width), jnp.float32)
+    for r in range(queries_ref.shape[1] // width):
+        piece = queries_ref[0:1, r * width : (r + 1) * width].astype(jnp.float32)
+        block = jnp.where(row == r, piece, block)
+    for at, number in enumerate((text_ref[0], owner, page)):
+        block = jnp.where((row == 8) & (lane == at), number.astype(jnp.float32), block)
+    out_ref[half : half + EXTRA, :] = block.astype(out_ref.dtype)
+
+
+def project_kernel(pieces, arrays, half, adds, *refs):
+    cols_ref, vision_ref, other_ref = refs[:3]
+    weight_refs = refs[3 : 3 + arrays]
+    before = refs[3 + arrays : 3 + arrays + adds]
+    own_ref, send_ref, slots, sems = refs[3 + arrays + adds :]
+    keys = own_ref.shape[0]
+
+    def copies(p):
+        own_at = pl.multiple_of(cols_ref[0, p] * half, half)
+        other_at = pl.multiple_of(cols_ref[1, p] * half, half)
+        to = p * half
+        return (
+            pltpu.make_async_copy(
+                vision_ref.at[:, pl.ds(own_at, half)], slots.at[0:keys, to : to + half], sems.at[0, p]
+            ),
+            pltpu.make_async_copy(
+                other_ref.at[:, pl.ds(other_at, half)],
+                slots.at[keys : 2 * keys, to : to + half],
+                sems.at[1, p],
+            ),
+        )
+
+    for p in range(len(pieces)):
+        for one in copies(p):
+            one.start()
+    total = [None, None]
+    for p, (which, row) in enumerate(pieces):
+        for one in copies(p):
+            one.wait()
+        weight = weight_refs[which][row : row + half, :]
+        for i in range(2):
+            term = jnp.dot(
+                slots[i * keys : (i + 1) * keys, p * half : (p + 1) * half],
+                weight,
+                preferred_element_type=jnp.float32,
+            )
+            if p == 0 and adds:
+                total[i] = before[i][...] + term
+            else:
+                total[i] = term if total[i] is None else total[i] + term
+    own_ref[...] = total[0]
+    send_ref[...] = total[1]
+
+
+def project(vision, other, arrays, pieces, cols, half, before=()):
+    keys = vision.shape[0]
+    width = arrays[0].shape[1]
+    result = jax.ShapeDtypeStruct((keys, width), jnp.float32)
+    count = len(pieces)
+    return call(
+        functools.partial(project_kernel, pieces, len(arrays), half, len(before)),
+        [result, result],
+        whole(1, pltpu.SMEM) + whole(2, pl.ANY) + whole(len(arrays) + len(before)),
+        scratch=[
+            pltpu.VMEM((2 * keys, count * half), vision.dtype),
+            pltpu.SemaphoreType.DMA((2, count)),
+        ],
+        vmem=24,
+        flops=4 * keys * half * width * count,
+        moved=count * half * (2 * keys + width) * 2,
+    )(cols, vision, other, *arrays, *before)
+
+
+def slot_of(token, me, steps):
+    z, x, core = token // PLANE, token // CORES % COLUMNS, token % CORES
+    mz, mx, mcore = me // PLANE, me // CORES % COLUMNS, me % CORES
+    d = lax.rem(z - mz + steps, steps)
+    across = jnp.where(core == mcore, 0, 1) * COLUMNS + jnp.where(x == mx, 0, 1)
+    return across * steps + d
+
+
+def pick_kernel(total, steps, rank, place_ref, extras_ref, down_ref, out_ref, flat):
+    me = place_ref[1]
+    flat[...] = down_ref[...].T
+    for dest in range(total):
+        at = pl.multiple_of(slot_of(jnp.int32(dest), me, steps) * EXTRA, EXTRA)
+        tile = extras_ref[pl.ds(at, EXTRA), 0:HEAD].astype(jnp.float32)
+        page = tile[8, 2].astype(jnp.int32)
+        out_ref[dest] = flat[pl.ds(pl.multiple_of(page * rank, rank), rank), :]
+
+
+def lowrank_kernel(image_ref, tenant_ref, page_ref, vision_ref, down_ref, up_ref, out_ref):
+    shards, rank, rows = down_ref.shape
+    total = jnp.zeros((vision_ref.shape[0], rank), jnp.float32)
+    for j in range(shards):
+        total = total + lax.dot_general(
+            vision_ref[:, j * rows : (j + 1) * rows],
+            down_ref[j],
+            (((1,), (1,)), ((), ())),
+            preferred_element_type=jnp.float32,
+        )
+    page = page_ref[tenant_ref[image_ref[0, 0]]]
+    out_ref[...] = jnp.dot(
+        total.astype(jnp.bfloat16), up_ref[page], preferred_element_type=jnp.float32
+    )
+
+
+def window_start(extras_ref, owner, text_total):
+    ids = extras_ref[:, 0:HEAD].astype(jnp.float32)
+    row = lax.broadcasted_iota(jnp.int32, ids.shape, 0)
+    lane = lax.broadcasted_iota(jnp.int32, ids.shape, 1)
+    smaller = (row % EXTRA == 8) & (lane == 0) & (ids < owner.astype(jnp.float32))
+    first = jnp.sum(jnp.where(smaller, 1.0, 0.0)).astype(jnp.int32)
+    return jnp.minimum(first, text_total - WINDOW)
+
+
+def select_rows(parts, rows):
+    head = lax.broadcasted_iota(jnp.int32, parts[0].shape, 0) % 8 // 2
+    result = parts[0]
+    for k in range(1, KV_HEADS):
+        result = jnp.where(head == k, parts[k], result)
+    return result
+
+
+def score_kernel(
+    total, steps, place_ref, image_ref, tiles_ref, mine_ref, got_ref, gain_ref, extras_ref,
+    weights_ref, stats_ref, state_ref,
+):
+    me, owner = place_ref[1], image_ref[0, 0]
+    keys = mine_ref.shape[0]
+    first = window_start(extras_ref, owner, total)
+    tiles = []
+    match = []
+    for s in range(WINDOW):
+        at = pl.multiple_of(slot_of(first + s, me, steps) * EXTRA, EXTRA)
+        block = extras_ref[pl.ds(at, EXTRA), :].astype(jnp.float32)
+        tiles += [block[0:8, k * HEAD : (k + 1) * HEAD] for k in range(KV_HEADS)]
+        match.append(block[8, 0].astype(jnp.int32) == owner)
+    query = jnp.concatenate(tiles, axis=0).astype(jnp.bfloat16)
+    key_raw = mine_ref[...] + got_ref[...]
+    gain = gain_ref[...]
+    parts = []
+    for k in range(KV_HEADS):
+        head = key_raw[:, k * HEAD : (k + 1) * HEAD]
+        scale = lax.rsqrt(jnp.mean(head * head, axis=1, keepdims=True) + epsilon)
+        block = (head * scale * gain).astype(jnp.bfloat16)
+        parts.append(
+            lax.dot_general(query, block, (((1,), (1,)), ((), ())), preferred_element_type=jnp.float32)
+        )
+    scores = select_rows(parts, query.shape[0]) * HEAD ** (-0.5)
+    row = lax.broadcasted_iota(jnp.int32, scores.shape, 0) // (8 * KV_HEADS)
+    lane = lax.broadcasted_iota(jnp.int32, scores.shape, 1)
+    limit = jnp.zeros(scores.shape, jnp.int32)
+    slots = tiles_ref[0] * (keys // TILES)
+    for s in range(WINDOW):
+        limit = jnp.where(row == s, jnp.where(match[s], slots, 0), limit)
+    usable = lane < limit
+    scores = jnp.where(usable, scores, masked_score)
+    top = jnp.max(scores, axis=1, keepdims=True)
+    weights = jnp.where(usable, jnp.exp(scores - top), 0.0).astype(jnp.bfloat16)
+    weights_ref[...] = weights
+    sums = jnp.sum(weights.astype(jnp.float32), axis=1, keepdims=True)
+    rows = 8 * KV_HEADS
+    eye = lax.broadcasted_iota(jnp.int32, (rows, HEAD), 0) == lax.broadcasted_iota(jnp.int32, (rows, HEAD), 1)
+    line = lax.broadcasted_iota(jnp.int32, (8, HEAD), 0)
+    for s in range(WINDOW):
+        own = slice(s * rows, (s + 1) * rows)
+        top_row = jnp.sum(jnp.where(eye, top[own], 0.0), axis=0, keepdims=True)
+        sum_row = jnp.sum(jnp.where(eye, sums[own], 0.0), axis=0, keepdims=True)
+        stats_ref[s] = jnp.where(line == 0, top_row, jnp.where(line == 1, sum_row, 0.0))
+        state_ref[1 + s] = match[s].astype(jnp.int32)
+    state_ref[0] = first
+
+
+def value_kernel(
+    steps, place_ref, state_ref, mine_ref, got_ref, lowrank_ref, weights_ref, stats_ref, *refs
+):
+    out_refs, numerators = refs[:-1], refs[-1]
+    me, first = place_ref[1], state_ref[0]
+    value = (mine_ref[...] + got_ref[...] + lowrank_ref[...]).astype(jnp.bfloat16)
+    weights = weights_ref[...]
+    parts = [
+        jnp.dot(weights, value[:, k * HEAD : (k + 1) * HEAD], preferred_element_type=jnp.float32)
+        for k in range(KV_HEADS)
+    ]
+    result = select_rows(parts, weights.shape[0])
+    rows = 8 * KV_HEADS
+    for s in range(WINDOW):
+        numerators[s, 0:rows, :] = result[s * rows : (s + 1) * rows]
+        numerators[s, rows:MESSAGE, :] = stats_ref[s]
+    line = lax.broadcasted_iota(jnp.int32, (MESSAGE, HEAD), 0)
+    empty = jnp.where(line == rows, masked_score, 0.0)
+    group = lax.rem(me, PLANE)
+    for k, out_ref in enumerate(out_refs):
+        core, x = lax.rem(group, CORES), group // CORES
+        to = (x if k < CORES else 1 - x) * CORES + (core if k % CORES == 0 else 1 - core)
+        for z in range(steps):
+            s = z * PLANE + to - first
+            inside = (s >= 0) & (s < WINDOW)
+            s = jnp.clip(s, 0, WINDOW - 1)
+            good = inside & (state_ref[1 + s] == 1)
+            out_ref[z] = jnp.where(good, numerators[s], empty)
+
+
+def merge(blocks):
+    rows = 8 * KV_HEADS
+    tops = [b[rows : rows + 1] for b in blocks]
+    top = functools.reduce(jnp.maximum, tops)
+    eye = lax.broadcasted_iota(jnp.int32, (rows, HEAD), 0) == lax.broadcasted_iota(jnp.int32, (rows, HEAD), 1)
+    numerator, total = 0.0, 0.0
+    for b, t in zip(blocks, tops):
+        scale = jnp.exp(t - top)
+        total = total + scale * b[rows + 1 : rows + 2]
+        column = jnp.sum(jnp.where(eye, scale, 0.0), axis=1, keepdims=True)
+        numerator = numerator + column * b[0:rows]
+    return numerator, top, total, eye
+
+
+def plane_kernel(steps, place_ref, *refs):
+    in_refs, out_refs, merged = refs[:PLANE], refs[PLANE : PLANE + steps], refs[-1]
+    rows = 8 * KV_HEADS
+    line = lax.broadcasted_iota(jnp.int32, (8, HEAD), 0)
+    for z in range(steps):
+        numerator, top, total, _ = merge([ref[z] for ref in in_refs])
+        merged[z, 0:rows, :] = numerator
+        merged[z, rows:MESSAGE, :] = jnp.where(line == 0, top, jnp.where(line == 1, total, 0.0))
+    for d, out_ref in enumerate(out_refs):
+        out_ref[...] = merged[lax.rem(place_ref[1] // PLANE + d, steps)]
+
+
+def final_kernel(*refs):
+    out_ref = refs[-1]
+    numerator, top, total, eye = merge([ref[...] for ref in refs[:-1]])
+    column = jnp.sum(jnp.where(eye, total, 0.0), axis=1, keepdims=True)
+    out = numerator / column
+    for k in range(KV_HEADS):
+        out_ref[:, k * HEAD : (k + 1) * HEAD] = out[8 * k : 8 * k + 8].astype(out_ref.dtype)
+
+
+def local(
+    devices,
+    vision,
+    queries,
+    text_request,
+    key_weight,
+    value_weight,
+    key_gain,
+    down_pages,
+    up_pages,
+    image_request,
+    image_tiles,
+    request_tenant,
+    tenant_page,
+):
+    steps = devices // PLANE
+    me = lax.axis_index("image").astype(jnp.int32)
+    y = lax.axis_index("groups").astype(jnp.int32)
+    z, x, core = me // PLANE, me // CORES % COLUMNS, me % CORES
+    tokens = vision[0]
+    rows, width = key_weight.shape
+    half = rows // 2
+    rank = up_pages.shape[1]
+    place = jnp.stack([y, me])
+    everyone = range(devices)
+
+    def across(value, bits):
+        return lax.ppermute(value, "image", [(i, i ^ bits) for i in everyone])
+
+    def along(value, d):
+        return lax.ppermute(value, "image", [(i, (i - PLANE * d) % devices) for i in everyone])
+
+    def swap(value):
+        return lax.ppermute(value, "groups", [(0, 1), (1, 0)])
+
+    def join(*arrays):
+        return jnp.concatenate(arrays, axis=0)
+
+    key_half = call(
+        functools.partial(prepare_kernel, half),
+        jax.ShapeDtypeStruct((half + EXTRA, width), key_weight.dtype),
+        whole(5, pltpu.SMEM) + whole(2),
+    )(place, text_request, image_request, request_tenant, tenant_page, queries, key_weight)
+    value_half = lax.dynamic_slice_in_dim(value_weight, y * half, half, 0)
+    extra = key_half[half:]
+
+    k_own = across(key_weight, CORES)
+    k1, k3 = along(key_half, 1), along(key_half, 3)
+    k2 = along(after(key_half, k1, k3, k_own), 2)
+    other = across(split_vision(tokens, core, rows), 1)
+    kx = across(after(join(k1, k3, extra), k_own), CORES)
+    ky = swap(after(join(k1[:half], k3[:half]), k_own))
+    kx2 = across(k2, CORES)
+    ky2 = swap(k2)
+    v1, v3 = along(after(value_half, k2), 1), along(after(value_half, k2), 3)
+    v_own = across(after(value_weight, kx, ky), CORES)
+    kd = swap(after(join(kx[:half], kx[half + EXTRA : 2 * half + EXTRA]), ky))
+    kd2 = swap(after(kx2, ky2))
+    v2 = along(after(value_half, v1, v3, v_own, kd), 2)
+    v_pair = join(v1, v3)
+    vx = across(after(v_pair, kx2, v_own), CORES)
+    vy = swap(after(v_pair, kd))
+    vx2 = across(after(v2, v_own), CORES)
+    vy2 = swap(after(v2, kd2))
+    vd = swap(after(vx, vy))
+    vd2 = across(after(vy2, vx), CORES)
+
+    def columns(spots):
+        own, other_at = [], []
+        for d, mirrored, part in spots:
+            pair = lax.rem(z + d, steps) * COLUMNS + (1 - x if mirrored else x)
+            at = part if isinstance(part, int) else jnp.where(part == "near", y, 1 - y)
+            at = {"near": y, "far": 1 - y}.get(part, part)
+            own.append((pair * CORES + core) * 2 + at)
+            other_at.append(pair * 2 + at)
+        return jnp.stack([jnp.stack([jnp.int32(0) + v for v in own]), jnp.stack([jnp.int32(0) + v for v in other_at])])
+
+    step = half + EXTRA
+    spots = [
+        (0, False, 0), (0, False, 1), (0, True, 0), (0, True, 1),
+        (1, False, "near"), (3, False, "near"), (2, False, "near"),
+        (1, True, "near"), (3, True, "near"), (2, True, "near"),
+        (1, False, "far"), (3, False, "far"), (2, False, "far"),
+        (1, True, "far"), (3, True, "far"), (2, True, "far"),
+    ]
+    cols = columns(spots)
+    key_arrays = [key_weight, k_own, k1, k3, k2, kx, kx2, ky, ky2, kd, kd2]
+    key_pieces = [
+        (0, 0), (0, half), (1, 0), (1, half), (2, 0), (3, 0), (4, 0),
+        (5, 0), (5, step), (6, 0), (7, 0), (7, half), (8, 0), (9, 0), (9, half), (10, 0),
+    ]
+    key_mine, key_send = project(tokens, other, key_arrays, tuple(key_pieces), cols, half)
+    key_got = across(key_send, 1)
+
+    near = join(extra, k1[half:], k2[half:], k3[half:], kx[2 * step :], kx[half:step], kx2[half:], kx[step + half : 2 * step])
+    extras = join(near, across(near, 1))
+
+    picked = call(
+        functools.partial(pick_kernel, devices, steps, rank),
+        jax.ShapeDtypeStruct((devices, rank, rows), down_pages.dtype),
+        whole(1, pltpu.SMEM) + whole(2),
+        scratch=[pltpu.VMEM(down_pages.shape[::-1], down_pages.dtype)],
+    )(place, extras, down_pages)
+    picked = lax.all_to_all(picked, "image", 0, 0, tiled=True)
+    lowrank = call(
+        lowrank_kernel,
+        jax.ShapeDtypeStruct((tokens.shape[0], width), jnp.float32),
+        whole(3, pltpu.SMEM) + whole(3),
+        vmem=16,
+        moved=tokens.size * 2,
+    )(image_request, request_tenant, tenant_page, tokens, picked, up_pages)
+
+    heads = WINDOW * 8 * KV_HEADS
+    weights, stats, state = pl.pallas_call(
+        functools.partial(score_kernel, devices, steps),
+        out_shape=[
+            jax.ShapeDtypeStruct((heads, tokens.shape[0]), jnp.bfloat16),
+            jax.ShapeDtypeStruct((WINDOW, 8, HEAD), jnp.float32),
+            jax.ShapeDtypeStruct((WINDOW + 1,), jnp.int32),
+        ],
+        in_specs=whole(3, pltpu.SMEM) + whole(4),
+        out_specs=whole(2) + whole(1, pltpu.SMEM),
+    )(place, image_request, image_tiles, key_mine, key_got, key_gain.reshape(1, HEAD), extras)
+
+    value_arrays = [value_weight, v_own, v1, v3, v2, vx, vx2, vy]
+    value_pieces = [
+        (0, 0), (0, half), (1, 0), (1, half), (2, 0), (3, 0), (4, 0),
+        (5, 0), (5, half), (6, 0), (7, 0), (7, half),
+    ]
+    early = project(tokens, other, value_arrays, tuple(value_pieces), cols[:, :12], half)
+    value_mine, value_send = project(
+        tokens, other, [vy2, vd, vd2], ((0, 0), (1, 0), (1, half), (2, 0)), cols[:, 12:], half, early
+    )
+    value_got = across(value_send, 1)
+
+    message = jax.ShapeDtypeStruct((steps, MESSAGE, HEAD), jnp.float32)
+    messages = call(
+        functools.partial(value_kernel, steps),
+        [message] * PLANE,
+        whole(2, pltpu.SMEM) + whole(5),
+        scratch=[pltpu.VMEM((WINDOW, MESSAGE, HEAD), jnp.float32)],
+    )(place, state, value_mine, value_got, lowrank, weights, stats)
+    arrived = [messages[0]] + [across(messages[k], k) for k in range(1, PLANE)]
+    one = jax.ShapeDtypeStruct((MESSAGE, HEAD), jnp.float32)
+    merged = call(
+        functools.partial(plane_kernel, steps),
+        [one] * steps,
+        whole(1, pltpu.SMEM) + whole(PLANE),
+        scratch=[pltpu.VMEM((steps, MESSAGE, HEAD), jnp.float32)],
+    )(place, *arrived)
+    arrived = [merged[0]] + [along(merged[d], steps - d) for d in range(1, steps)]
+    out = call(
+        final_kernel,
+        jax.ShapeDtypeStruct((8, KV_HEADS * HEAD), jnp.bfloat16),
+        whole(steps),
+    )(*arrived)
+    return out.reshape(queries.shape)
+
+
+def fits(mesh, vision, queries, key_weight):
+    devices = mesh.shape["image"]
+    rows = key_weight.shape[0] // devices
+    own = queries.shape[0] // (mesh.shape["groups"] * devices)
+    one = vision.shape[0] == mesh.shape["groups"] * devices
+    return rows % 256 == 0 and devices == 4 * PLANE and mesh.shape["groups"] == 2 and own == 1 and one
+
+
 def solution(mesh):
     in_specs = (
         P(("groups", "image"), None, None),
@@ -147,4 +614,12 @@
         P(),
     )
     out_specs = P(("groups", "image"), None)
-    return jax.shard_map(local, mesh=mesh, in_specs=in_specs, out_specs=out_specs, check_vma=False)
+
+    def run(*args):
+        if fits(mesh, args[0], args[1], args[3]):
+            body = functools.partial(local, mesh.shape["image"])
+        else:
+            body = local_gathered
+        return jax.shard_map(body, mesh=mesh, in_specs=in_specs, out_specs=out_specs, check_vma=False)(*args)
+
+    return run

time: 312 us -> 157 us (0.50)
  blocking collectives: 112 us -> 0 us
  waiting for transfers between devices: 138 us -> 88.4 us
  starting transfers between devices: 0.12 us -> 31.5 us
  Pallas kernels: 0 us -> 24 us
  matrix products: 21 us -> 0 us
  between operations: 18.2 us -> 2.36 us
  local copies, waits for them, and re-layouts: 18.1 us -> 9.4 us
  other arithmetic: 4.51 us -> 0.2 us
    all_gather x4 -> x0, waiting for transfers between devices: 135 us -> none  [the longest x1 57.1 us: local(): lax.all_gather(value_weight, 'image', axis=0, tiled=True)]
    ppermute x0 -> x30, waiting for transfers between devices: none -> 79.1 us  [the longest x9 41.9 us: along(): lax.ppermute(value, 'image', [(i, (i - PLANE * d) % devices) for i in eve...]
    unnamed x2 -> x0, blocking collectives: 43.9 us -> none
    all_gather x2 -> x0, blocking collectives: 36.2 us -> none  [the longest x1 19 us: local(): lax.all_gather(queries, 'image', axis=0, tiled=True)]
    pmax x1 -> x0, blocking collectives: 31.7 us -> none  [local(): top_score = lax.pmax(every_max, 'image')]
    ppermute x0 -> x30, starting transfers between devices: none -> 27.9 us  [the longest x9 10.5 us: along(): lax.ppermute(value, 'image', [(i, (i - PLANE * d) % devices) for i in eve...]
    pallas_call x0 -> x11, Pallas kernels: none -> 24 us  [the longest x3 10.1 us: project(): call(functools.partial(project_kernel, pieces, len(arrays), half, len(bef...]
    dot_general x7 -> x0, matrix products: 21 us -> none  [the longest x1 7.06 us: local(): key_raw = jnp.dot(columns, pieces[0], preferred_element_type=jnp.float32)]
  transfers between devices with their start and end apart: 4 -> 31, of which waited for: 3 -> 13; matrix products, arithmetic and copies ran while one was open for 11% -> 0% of each run, Pallas kernels for 0% -> 14%
where the time goes in v1:
time: 157 us; the launch traced here: 156 us
  waiting for transfers between devices  88.4 us (56%)
  starting transfers between devices  31.5 us (20%)
  Pallas kernels  24 us (15%)
  local copies, waits for them, and re-layouts  9.4 us (6%)
  between operations  2.36 us (2%)
    ppermute x9, waiting for transfers between devices, along(): lax.ppermute(value, 'image', [(i, (i - PLANE * d) % devices) for i in eve...  41.9 us
    ppermute x7, waiting for transfers between devices, swap(): return lax.ppermute(value, 'groups', [(0, 1), (1, 0)])  32.9 us
    ppermute x9, starting transfers between devices, along(): lax.ppermute(value, 'image', [(i, (i - PLANE * d) % devices) for i in eve...  10.5 us
    pallas_call x3, Pallas kernels, project(): call(functools.partial(project_kernel, pieces, len(arrays), half, len(bef...  10.1 us
    all_to_all x1, waiting for transfers between devices, local(): picked = lax.all_to_all(picked, 'image', 0, 0, tiled=True)  9.36 us
    unnamed x52, local copies, waits for them, and re-layouts  9.01 us
    ppermute x14, starting transfers between devices, across(): return lax.ppermute(value, 'image', [(i, i ^ bits) for i in everyone])  8.79 us
    ppermute x7, starting transfers between devices, swap(): return lax.ppermute(value, 'groups', [(0, 1), (1, 0)])  8.68 us
  transfers between devices with their start and end apart: 31, of which 13 were waited for; matrix products, arithmetic and copies ran while one was open for 0% of the time, Pallas kernels for 14%

profile of v1, /device:TPU:0, one launch (start us, length us, event | category | flops | bytes accessed | tf_op | source)
XLA Modules:
  0.0 155.9 jit_solution(3899770660470398239)
XLA Ops:
  0.0 2.9 %collective-permute-start.1 = (bf16[512,512]{1,0:T(8,128)(2,1)}, bf16[512,512]{1,0:T(8,128)(2,1)S(1)}, u32[]{:S(2)}, u32[]{:S(2)}) collective-permute-start(bf16[512,512]{1,0:T(8,128)(2,1)} %refs_3_.2), channel_id=1, source_target_pairs={{0,2},{1,3},{2,0},{3,1},{4,6},{5,7},{6,4},{7,5},{8,10},{9,11},{10,... | collective-permute-start | bytes 1572872 | tf_op jit(solution)/shard_map/ppermute | solution.py:461
  4.3 1.0 copy-done.2
  5.4 0.7 copy-done.11
  6.1 0.7 copy-done.14
  6.7 0.7 copy-done.16
  7.4 0.6 shard_map.119
  8.0 3.7 %collective-permute-start.2 = (bf16[272,512]{1,0:T(8,128)(2,1)S(1)}, bf16[272,512]{1,0:T(8,128)(2,1)S(1)}, u32[]{:S(2)}, u32[]{:S(2)}) collective-permute-start(bf16[272,512]{1,0:T(8,128)(2,1)S(1)} %shard_map.119), channel_id=1, source_target_pairs={{0,12},{1,13},{2,14},{3,15},{4,0},{5,1},{6,2},{7,3},{8,4},{9,5},{1... | collective-permute-start | bytes 835592 | tf_op jit(solution)/shard_map/ppermute | solution.py:464
  12.0 5.7 %shard_map.118 = bf16[256,4096]{1,0:T(8,128)(2,1)} custom-call(s32[1]{0:T(128)} %bitcast.37.place_ref, bf16[256,8192]{1,0:T(8,128)(2,1)} %bitcast.43), custom_call_target="tpu_custom_call" | custom-call | bytes 4194304 | tf_op jit(solution)/shard_map/pallas_call | solution.py:175
  17.7 6.5 %collective-permute-done.3.refs_6_ = bf16[272,512]{1,0:T(8,128)(2,1)S(1)} collective-permute-done((bf16[272,512]{1,0:T(8,128)(2,1)S(1)}, bf16[272,512]{1,0:T(8,128)(2,1)S(1)}, u32[]{:S(2)}, u32[]{:S(2)}) %collective-permute-start.3) | collective-permute-done | bytes 278560 | tf_op jit(solution)/shard_map/ppermute | solution.py:464
  24.3 0.8 collective-permute-start.4
  25.1 0.6 collective-permute-start.5
  25.7 12.7 %collective-permute-done.4.refs_7_ = bf16[272,512]{1,0:T(8,128)(2,1)S(1)} collective-permute-done((bf16[272,512]{1,0:T(8,128)(2,1)S(1)}, bf16[272,512]{1,0:T(8,128)(2,1)S(1)}, u32[]{:S(2)}, u32[]{:S(2)}) %collective-permute-start.4) | collective-permute-done | bytes 278560 | tf_op jit(solution)/shard_map/ppermute | solution.py:464
  38.4 1.3 collective-permute-start.13
  39.7 0.7 collective-permute-start.14
  41.0 1.5 collective-permute-start.8
  42.5 4.0 %collective-permute-done.13.refs_5_ = bf16[256,512]{1,0:T(8,128)(2,1)S(1)} collective-permute-done((bf16[256,512]{1,0:T(8,128)(2,1)S(1)}, bf16[256,512]{1,0:T(8,128)(2,1)S(1)}, u32[]{:S(2)}, u32[]{:S(2)}) %collective-permute-start.13) | collective-permute-done | bytes 262176 | tf_op jit(solution)/shard_map/ppermute | solution.py:464
  46.5 5.4 %collective-permute-done.14.refs_6_ = bf16[256,512]{1,0:T(8,128)(2,1)S(1)} collective-permute-done((bf16[256,512]{1,0:T(8,128)(2,1)S(1)}, bf16[256,512]{1,0:T(8,128)(2,1)S(1)}, u32[]{:S(2)}, u32[]{:S(2)}) %collective-permute-start.14) | collective-permute-done | bytes 262176 | tf_op jit(solution)/shard_map/ppermute | solution.py:464
  51.9 1.5 collective-permute-start.7
  53.4 0.6 collective-permute-start.10
  54.1 12.6 %collective-permute-done.7.refs_10_ = bf16[512,512]{1,0:T(8,128)(2,1)S(1)} collective-permute-done((bf16[512,512]{1,0:T(8,128)(2,1)S(1)}, bf16[512,512]{1,0:T(8,128)(2,1)S(1)}, u32[]{:S(2)}, u32[]{:S(2)}) %collective-permute-start.7) | collective-permute-done | bytes 524320 | tf_op jit(solution)/shard_map/ppermute | solution.py:467
  66.7 1.5 collective-permute-start.9
  68.8 13.6 %collective-permute-done.9.refs_12_ = bf16[512,512]{1,0:T(8,128)(2,1)S(1)} collective-permute-done((bf16[512,512]{1,0:T(8,128)(2,1)S(1)}, bf16[512,512]{1,0:T(8,128)(2,1)S(1)}, u32[]{:S(2)}, u32[]{:S(2)}) %collective-permute-start.9) | collective-permute-done | bytes 524320 | tf_op jit(solution)/shard_map/ppermute | solution.py:467
  82.9 1.5 collective-permute-start.19
  84.5 11.1 %collective-permute-done.16.refs_7_ = bf16[256,512]{1,0:T(8,128)(2,1)S(1)} collective-permute-done((bf16[256,512]{1,0:T(8,128)(2,1)S(1)}, bf16[256,512]{1,0:T(8,128)(2,1)S(1)}, u32[]{:S(2)}, u32[]{:S(2)}) %collective-permute-start.16) | collective-permute-done | bytes 262176 | tf_op jit(solution)/shard_map/ppermute | solution.py:464
  95.7 1.5 collective-permute-start.17
  98.3 6.7 %collective-permute-done.17.refs_3_ = bf16[256,512]{1,0:T(8,128)(2,1)S(1)} collective-permute-done((bf16[256,512]{1,0:T(8,128)(2,1)S(1)}, bf16[256,512]{1,0:T(8,128)(2,1)S(1)}, u32[]{:S(2)}, u32[]{:S(2)}) %collective-permute-start.17) | collective-permute-done | bytes 262176 | tf_op jit(solution)/shard_map/ppermute | solution.py:467
  105.5 4.7 %shard_map.120 = (f32[256,512]{1,0:T(8,128)S(1)}, f32[256,512]{1,0:T(8,128)S(1)}) custom-call(s32[2,16]{1,0:T(2,128)S(1)} %pad_add_fusion.refs_0_, bf16[256,8192]{1,0:T(8,128)(2,1)S(1)} %bitcast.44, bf16[256,4096]{1,0:T(8,128)(2,1)S(1)} %collective-permute-done.refs_2_, bf16[512,512]{1,0:T(8,128)(2,1)S(1)} %copy-done.3, ...), custom_call_target="tpu_custom_call" | custom-call | flops 2147483648 | bytes 8388608 | tf_op jit(solution)/shard_map/pallas_call | solution.py:254
  110.2 0.8 copy-done.6
  111.0 3.7 %shard_map.122 = (f32[256,512]{1,0:T(8,128)S(1)}, f32[256,512]{1,0:T(8,128)S(1)}) custom-call(s32[2,12]{1,0:T(2,128)S(1)} %bitcast.49, bf16[256,8192]{1,0:T(8,128)(2,1)S(1)} %bitcast.45, bf16[256,4096]{1,0:T(8,128)(2,1)S(1)} %collective-permute-done.refs_2_, bf16[512,512]{1,0:T(8,128)(2,1)S(1)} %copy-done.4, ...), custom_call_target="tpu_custom_call" | custom-call | flops 1610612736 | bytes 6291456 | tf_op jit(solution)/shard_map/pallas_call | solution.py:254
  114.7 1.7 %shard_map.123 = (f32[256,512]{1,0:T(8,128)S(1)}, f32[256,512]{1,0:T(8,128)S(1)}) custom-call(s32[2,4]{1,0:T(2,128)S(1)} %slice.54.refs_0_, bf16[256,8192]{1,0:T(8,128)(2,1)S(1)} %bitcast.46, bf16[256,4096]{1,0:T(8,128)(2,1)S(1)} %collective-permute-done.refs_2_, bf16[256,512]{1,0:T(8,128)(2,1)S(1)} %collective-permute-done.17.refs_3_, ...), custom_call_target="tpu_custom_call" | custom-call | flops 536870912 | bytes 2097152 | tf_op jit(solution)/shard_map/pallas_call | solution.py:254
  117.1 1.4 shard_map.124
  118.6 3.5 %all-to-all-start = ((bf16[16,16,512]{2,1,0:T(8,128)(2,1)}), bf16[16,16,512]{2,1,0:T(8,128)(2,1)S(1)}, u32[]{:S(2)}, u32[]{:S(2)}) async-start(bf16[16,16,512]{2,1,0:T(8,128)(2,1)} %shard_map.124), calls=%async_computation | async-start | bytes 524288 | tf_op jit(solution)/shard_map/all_to_all | solution.py:537
  122.8 9.4 %all-to-all-done.down_ref = bf16[16,16,512]{2,1,0:T(8,128)(2,1)S(1)} async-done(((bf16[16,16,512]{2,1,0:T(8,128)(2,1)}), bf16[16,16,512]{2,1,0:T(8,128)(2,1)S(1)}, u32[]{:S(2)}, u32[]{:S(2)}) %all-to-all-start) | async-done | bytes 262176 | tf_op jit(solution)/shard_map/all_to_all | solution.py:537
  132.1 2.2 %copy-done.1 = bf16[1,256,8192]{2,1,0:T(8,128)(2,1)S(1)} copy-done((bf16[1,256,8192]{2,1,0:T(8,128)(2,1)S(1)}, bf16[1,256,8192]{2,1,0:T(8,128)(2,1)}, u32[]{:S(2)}) %copy-start.1) | copy-done | bytes 4194328
  134.3 2.0 %shard_map.125.lowrank_ref = f32[256,512]{1,0:T(8,128)S(1)} custom-call(s32[1,1]{1,0:T(1,128)S(6)} %copy.31.image_ref, s32[8]{0:T(128)S(1)} %copy-done.15, s32[16]{0:T(128)S(1)} %copy-done.17, bf16[256,8192]{1,0:T(8,128)(2,1)S(1)} %bitcast.47, bf16[16,16,512]{2,1,0:T(8,128)(2,1)S(1)} %all-to-all-done.down_ref, bf16[16,16,512]{2,1,0:T(8,128)(2,1)S(1)} %copy-done.7), custom_call_target="tpu_custom_call" | custom-call | bytes 4194304 | tf_op jit(solution)/shard_map/pallas_call | solution.py:538
  136.4 2.5 %shard_map.121 = (bf16[128,256]{1,0:T(8,128)(2,1)}, f32[4,8,128]{2,1,0:T(8,128)}, s32[5]{0:T(128)}) custom-call(s32[2]{0:T(128)} %copy-done.12, s32[1,1]{1,0:T(1,128)S(6)} %copy.31.image_ref, s32[1]{0:T(128)S(6)} %copy.32.tiles_ref, f32[256,512]{1,0:T(8,128)} %copy-done.6, f32[256,512]{1,0:T(8,128)} %collective-permute-done.11.got_ref, f32[1,128]{1,0:T(1,128)} %bitcast.52, ...), custom_call_target="tpu_custom_call" | custom-call | tf_op jit(solution)/shard_map/pallas_call | solution.py:547
  138.9 0.8 copy-done.9
  139.7 0.7 copy-done.10
  140.4 0.7 copy-done.18
  141.1 0.9 shard_map.126
  142.6 1.4 collective-permute-start.26
  143.9 3.4 %collective-permute-done.25.refs_2_ = f32[4,40,128]{2,1,0:T(8,128)S(1)} collective-permute-done((f32[4,40,128]{2,1,0:T(8,128)S(1)}, f32[4,40,128]{2,1,0:T(8,128)S(1)}, u32[]{:S(2)}, u32[]{:S(2)}) %collective-permute-start.25) | collective-permute-done | bytes 81952 | tf_op jit(solution)/shard_map/ppermute | solution.py:461
  147.4 0.8 collective-permute-done.26.refs_3_
  148.2 0.7 shard_map.127
  149.0 1.4 collective-permute-start.28
  150.4 2.6 %collective-permute-start.29 = (f32[40,128]{1,0:T(8,128)S(1)}, f32[40,128]{1,0:T(8,128)S(1)}, u32[]{:S(2)}, u32[]{:S(2)}) collective-permute-start(f32[40,128]{1,0:T(8,128)S(1)} %get-tuple-element.66), channel_id=1, source_target_pairs={{0,12},{1,13},{2,14},{3,15},{4,0},{5,1},{6,2},{7,3},{8,4},{9,5},{1... | collective-permute-start | bytes 61448 | tf_op jit(solution)/shard_map/ppermute | solution.py:464
  152.9 1.6 %collective-permute-done.27.refs_1_ = f32[40,128]{1,0:T(8,128)S(1)} collective-permute-done((f32[40,128]{1,0:T(8,128)S(1)}, f32[40,128]{1,0:T(8,128)S(1)}, u32[]{:S(2)}, u32[]{:S(2)}) %collective-permute-start.27) | collective-permute-done | bytes 20512 | tf_op jit(solution)/shard_map/ppermute | solution.py:464
  155.2 0.6 copy.13
  (92 shorter events, 5.9 us)
Async XLA Ops:
  0.0 24.3 %collective-permute-start.1 = (bf16[512,512]{1,0:T(8,128)(2,1)}, bf16[512,512]{1,0:T(8,128)(2,1)S(1)}, u32[]{:S(2)}, u32[]{:S(2)}) collective-permute-start(bf16[512,512]{1,0:T(8,128)(2,1)} %refs_3_.2), channel_id=1, source_target_pairs={{0,2},{1,3},{2,0},{3,1},{4,6},{5,7},{6,4},{7,5},{8,10},{9,11},{10,... | collective-permute-start | bytes 1572872 | tf_op jit(solution)/shard_map/ppermute | solution.py:461
  4.3 1.0 copy-start.2
  5.4 0.7 copy-start.11
  7.4 109.7 %copy-start.12 = (s32[2]{0:T(128)}, s32[2]{0:T(128)S(1)}, u32[]{:S(2)}) copy-start(s32[2]{0:T(128)S(1)} %pad_add_fusion.1.place_ref) | copy-start | bytes 28
  7.4 4.4 %copy-start.4 = (bf16[512,512]{1,0:T(8,128)(2,1)S(1)}, bf16[512,512]{1,0:T(8,128)(2,1)}, u32[]{:S(2)}) copy-start(bf16[512,512]{1,0:T(8,128)(2,1)} %refs_3_.3) | copy-start | bytes 1572868
  8.0 16.2 %collective-permute-start.2 = (bf16[272,512]{1,0:T(8,128)(2,1)S(1)}, bf16[272,512]{1,0:T(8,128)(2,1)S(1)}, u32[]{:S(2)}, u32[]{:S(2)}) collective-permute-start(bf16[272,512]{1,0:T(8,128)(2,1)S(1)} %shard_map.119), channel_id=1, source_target_pairs={{0,12},{1,13},{2,14},{3,15},{4,0},{5,1},{6,2},{7,3},{8,4},{9,5},{1... | collective-permute-start | bytes 835592 | tf_op jit(solution)/shard_map/ppermute | solution.py:464
  11.6 12.5 %collective-permute-start.3 = (bf16[272,512]{1,0:T(8,128)(2,1)S(1)}, bf16[272,512]{1,0:T(8,128)(2,1)S(1)}, u32[]{:S(2)}, u32[]{:S(2)}) collective-permute-start(bf16[272,512]{1,0:T(8,128)(2,1)S(1)} %shard_map.119), channel_id=1, source_target_pairs={{0,4},{1,5},{2,6},{3,7},{4,8},{5,9},{6,10},{7,11},{8,12},{9,13},{1... | collective-permute-start | bytes 835592 | tf_op jit(solution)/shard_map/ppermute | solution.py:464
  24.1 22.3 %copy-start.19 = (bf16[256,4096]{1,0:T(8,128)(2,1)S(1)}, bf16[256,4096]{1,0:T(8,128)(2,1)}, u32[]{:S(2)}) copy-start(bf16[256,4096]{1,0:T(8,128)(2,1)} %shard_map.118) | copy-start | bytes 6291460
  24.2 81.3 %copy-start.3 = (bf16[512,512]{1,0:T(8,128)(2,1)S(1)}, bf16[512,512]{1,0:T(8,128)(2,1)}, u32[]{:S(2)}) copy-start(bf16[512,512]{1,0:T(8,128)(2,1)} %refs_3_.2) | copy-start | bytes 1572868
  24.3 14.1 %collective-permute-start.4 = (bf16[272,512]{1,0:T(8,128)(2,1)S(1)}, bf16[272,512]{1,0:T(8,128)(2,1)S(1)}, u32[]{:S(2)}, u32[]{:S(2)}) collective-permute-start(bf16[272,512]{1,0:T(8,128)(2,1)S(1)} %shard_map.119), channel_id=1, source_target_pairs={{0,8},{1,9},{2,10},{3,11},{4,12},{5,13},{6,14},{7,15},{8,0},{9,1},... | collective-permute-start | bytes 835592 | tf_op jit(solution)/shard_map/ppermute | solution.py:464
  25.1 80.4 %copy-start = (bf16[1,256,8192]{2,1,0:T(8,128)(2,1)S(1)}, bf16[1,256,8192]{2,1,0:T(8,128)(2,1)}, u32[]{:S(2)}) copy-start(bf16[1,256,8192]{2,1,0:T(8,128)(2,1)} %param.12) | copy-start | bytes 12582916
  25.1 28.9 %collective-permute-start.5 = (bf16[560,512]{1,0:T(8,128)(2,1)S(1)}, bf16[560,512]{1,0:T(8,128)(2,1)S(1)}, u32[]{:S(2)}, u32[]{:S(2)}) collective-permute-start(bf16[560,512]{1,0:T(8,128)(2,1)S(1)} %pad_maximum_fusion), channel_id=1, source_target_pairs={{0,2},{1,3},{2,0},{3,1},{4,6},{5,7},{6,4},{7,5},{8,10},{9,11},{10,... | collective-permute-start | bytes 1720328 | tf_op jit(solution)/shard_map/ppermute | solution.py:461
  38.4 8.1 %collective-permute-start.13 = (bf16[256,512]{1,0:T(8,128)(2,1)S(1)}, bf16[256,512]{1,0:T(8,128)(2,1)S(1)}, u32[]{:S(2)}, u32[]{:S(2)}) collective-permute-start(bf16[256,512]{1,0:T(8,128)(2,1)S(1)} %constant_dynamic-slice_fusion), channel_id=1, source_target_pairs={{0,12},{1,13},{2,14},{3,15},{4,0},{5,1},{6,2},{7,3},{8,4},{9,5},{1... | collective-permute-start | bytes 786440 | tf_op jit(solution)/shard_map/ppermute | solution.py:464
  39.7 12.1 %collective-permute-start.14 = (bf16[256,512]{1,0:T(8,128)(2,1)S(1)}, bf16[256,512]{1,0:T(8,128)(2,1)S(1)}, u32[]{:S(2)}, u32[]{:S(2)}) collective-permute-start(bf16[256,512]{1,0:T(8,128)(2,1)S(1)} %constant_dynamic-slice_fusion), channel_id=1, source_target_pairs={{0,4},{1,5},{2,6},{3,7},{4,8},{5,9},{6,10},{7,11},{8,12},{9,13},{1... | collective-permute-start | bytes 786440 | tf_op jit(solution)/shard_map/ppermute | solution.py:464
  40.4 13.0 %collective-permute-start.6 = (bf16[272,512]{1,0:T(8,128)(2,1)S(1)}, bf16[272,512]{1,0:T(8,128)(2,1)S(1)}, u32[]{:S(2)}, u32[]{:S(2)}) collective-permute-start(bf16[272,512]{1,0:T(8,128)(2,1)S(1)} %collective-permute-done.4.refs_7_), channel_id=1, source_target_pairs={{0,2},{1,3},{2,0},{3,1},{4,6},{5,7},{6,4},{7,5},{8,10},{9,11},{10,... | collective-permute-start | bytes 835592 | tf_op jit(solution)/shard_map/ppermute | solution.py:461
  41.0 12.5 %collective-permute-start.8 = (bf16[272,512]{1,0:T(8,128)(2,1)S(1)}, bf16[272,512]{1,0:T(8,128)(2,1)S(1)}, u32[]{:S(2)}, u32[]{:S(2)}) collective-permute-start(bf16[272,512]{1,0:T(8,128)(2,1)S(1)} %collective-permute-done.4.refs_7_), channel_id=1, source_target_pairs={{0,16},{16,0},{1,17},{17,1},{2,18},{18,2},{3,19},{19,3},{4,20},{20... | collective-permute-start | bytes 835592 | tf_op jit(solution)/shard_map/ppermute | solution.py:467
  46.5 59.0 %collective-permute-start = (bf16[256,4096]{1,0:T(8,128)(2,1)S(1)}, bf16[256,4096]{1,0:T(8,128)(2,1)S(1)}, u32[]{:S(2)}, u32[]{:S(2)}) collective-permute-start(bf16[256,4096]{1,0:T(8,128)(2,1)S(1)} %copy-done.19), channel_id=1, source_target_pairs={{0,1},{1,0},{2,3},{3,2},{4,5},{5,4},{6,7},{7,6},{8,9},{9,8},{10,11... | collective-permute-start | bytes 6291464 | tf_op jit(solution)/shard_map/ppermute | solution.py:461
  51.9 14.9 %collective-permute-start.7 = (bf16[512,512]{1,0:T(8,128)(2,1)S(1)}, bf16[512,512]{1,0:T(8,128)(2,1)S(1)}, u32[]{:S(2)}, u32[]{:S(2)}) collective-permute-start(bf16[512,512]{1,0:T(8,128)(2,1)S(1)} %pad_maximum_fusion.1), channel_id=1, source_target_pairs={{0,16},{16,0},{1,17},{17,1},{2,18},{18,2},{3,19},{19,3},{4,20},{20... | collective-permute-start | bytes 1572872 | tf_op jit(solution)/shard_map/ppermute | solution.py:467
  53.4 31.0 %collective-permute-start.10 = (bf16[272,512]{1,0:T(8,128)(2,1)S(1)}, bf16[272,512]{1,0:T(8,128)(2,1)S(1)}, u32[]{:S(2)}, u32[]{:S(2)}) collective-permute-start(bf16[272,512]{1,0:T(8,128)(2,1)S(1)} %collective-permute-done.6.refs_9_), channel_id=1, source_target_pairs={{0,16},{16,0},{1,17},{17,1},{2,18},{18,2},{3,19},{19,3},{4,20},{20... | collective-permute-start | bytes 835592 | tf_op jit(solution)/shard_map/ppermute | solution.py:467
  66.7 15.7 %collective-permute-start.9 = (bf16[512,512]{1,0:T(8,128)(2,1)S(1)}, bf16[512,512]{1,0:T(8,128)(2,1)S(1)}, u32[]{:S(2)}, u32[]{:S(2)}) collective-permute-start(bf16[512,512]{1,0:T(8,128)(2,1)S(1)} %pad_maximum_fusion.2), channel_id=1, source_target_pairs={{0,16},{16,0},{1,17},{17,1},{2,18},{18,2},{3,19},{19,3},{4,20},{20... | collective-permute-start | bytes 1572872 | tf_op jit(solution)/shard_map/ppermute | solution.py:467
  68.2 14.1 %collective-permute-start.15 = (bf16[512,512]{1,0:T(8,128)(2,1)S(1)}, bf16[512,512]{1,0:T(8,128)(2,1)S(1)}, u32[]{:S(2)}, u32[]{:S(2)}) collective-permute-start(bf16[512,512]{1,0:T(8,128)(2,1)S(1)} %copy-done.4), channel_id=1, source_target_pairs={{0,2},{1,3},{2,0},{3,1},{4,6},{5,7},{6,4},{7,5},{8,10},{9,11},{10,... | collective-permute-start | bytes 1572872 | tf_op jit(solution)/shard_map/ppermute | solution.py:461
  82.4 13.3 %collective-permute-start.16 = (bf16[256,512]{1,0:T(8,128)(2,1)S(1)}, bf16[256,512]{1,0:T(8,128)(2,1)S(1)}, u32[]{:S(2)}, u32[]{:S(2)}) collective-permute-start(bf16[256,512]{1,0:T(8,128)(2,1)S(1)} %constant_dynamic-slice_fusion), channel_id=1, source_target_pairs={{0,8},{1,9},{2,10},{3,11},{4,12},{5,13},{6,14},{7,15},{8,0},{9,1},... | collective-permute-start | bytes 786440 | tf_op jit(solution)/shard_map/ppermute | solution.py:464
  82.4 14.8 %collective-permute-start.18 = (bf16[512,512]{1,0:T(8,128)(2,1)S(1)}, bf16[512,512]{1,0:T(8,128)(2,1)S(1)}, u32[]{:S(2)}, u32[]{:S(2)}) collective-permute-start(bf16[512,512]{1,0:T(8,128)(2,1)S(1)} %constant_dynamic-update-slice_fusion.17), channel_id=1, source_target_pairs={{0,2},{1,3},{2,0},{3,1},{4,6},{5,7},{6,4},{7,5},{8,10},{9,11},{10,... | collective-permute-start | bytes 1572872 | tf_op jit(solution)/shard_map/ppermute | solution.py:461
  82.9 14.8 %collective-permute-start.19 = (bf16[512,512]{1,0:T(8,128)(2,1)S(1)}, bf16[512,512]{1,0:T(8,128)(2,1)S(1)}, u32[]{:S(2)}, u32[]{:S(2)}) collective-permute-start(bf16[512,512]{1,0:T(8,128)(2,1)S(1)} %constant_dynamic-update-slice_fusion.17), channel_id=1, source_target_pairs={{0,16},{16,0},{1,17},{17,1},{2,18},{18,2},{3,19},{19,3},{4,20},{20... | collective-permute-start | bytes 1572872 | tf_op jit(solution)/shard_map/ppermute | solution.py:467
  84.5 32.7 %collective-permute-start.12 = (bf16[128,512]{1,0:T(8,128)(2,1)S(1)}, bf16[128,512]{1,0:T(8,128)(2,1)S(1)}, u32[]{:S(2)}, u32[]{:S(2)}) collective-permute-start(bf16[128,512]{1,0:T(8,128)(2,1)S(1)} %get-tuple-element.67), channel_id=1, source_target_pairs={{0,1},{1,0},{2,3},{3,2},{4,5},{5,4},{6,7},{7,6},{8,9},{9,8},{10,11... | collective-permute-start | bytes 393224 | tf_op jit(solution)/shard_map/ppermute | solution.py:461
  95.7 9.2 %collective-permute-start.17 = (bf16[256,512]{1,0:T(8,128)(2,1)S(1)}, bf16[256,512]{1,0:T(8,128)(2,1)S(1)}, u32[]{:S(2)}, u32[]{:S(2)}) collective-permute-start(bf16[256,512]{1,0:T(8,128)(2,1)S(1)} %collective-permute-done.16.refs_7_), channel_id=1, source_target_pairs={{0,16},{16,0},{1,17},{17,1},{2,18},{18,2},{3,19},{19,3},{4,20},{20... | collective-permute-start | bytes 786440 | tf_op jit(solution)/shard_map/ppermute | solution.py:467
  97.2 13.8 %collective-permute-start.22 = (bf16[256,512]{1,0:T(8,128)(2,1)S(1)}, bf16[256,512]{1,0:T(8,128)(2,1)S(1)}, u32[]{:S(2)}, u32[]{:S(2)}) collective-permute-start(bf16[256,512]{1,0:T(8,128)(2,1)S(1)} %collective-permute-done.16.refs_7_), channel_id=1, source_target_pairs={{0,2},{1,3},{2,0},{3,1},{4,6},{5,7},{6,4},{7,5},{8,10},{9,11},{10,... | collective-permute-start | bytes 786440 | tf_op jit(solution)/shard_map/ppermute | solution.py:461
  97.7 17.0 %collective-permute-start.20 = (bf16[512,512]{1,0:T(8,128)(2,1)S(1)}, bf16[512,512]{1,0:T(8,128)(2,1)S(1)}, u32[]{:S(2)}, u32[]{:S(2)}) collective-permute-start(bf16[512,512]{1,0:T(8,128)(2,1)S(1)} %collective-permute-done.18.refs_8_), channel_id=1, source_target_pairs={{0,16},{16,0},{1,17},{17,1},{2,18},{18,2},{3,19},{19,3},{4,20},{20... | collective-permute-start | bytes 1572872 | tf_op jit(solution)/shard_map/ppermute | solution.py:467
  104.9 9.8 %collective-permute-start.21 = (bf16[256,512]{1,0:T(8,128)(2,1)S(1)}, bf16[256,512]{1,0:T(8,128)(2,1)S(1)}, u32[]{:S(2)}, u32[]{:S(2)}) collective-permute-start(bf16[256,512]{1,0:T(8,128)(2,1)S(1)} %collective-permute-done.17.refs_3_), channel_id=1, source_target_pairs={{0,2},{1,3},{2,0},{3,1},{4,6},{5,7},{6,4},{7,5},{8,10},{9,11},{10,... | collective-permute-start | bytes 786440 | tf_op jit(solution)/shard_map/ppermute | solution.py:461
  110.2 0.8 copy-start.6
  111.0 25.3 %collective-permute-start.11 = (f32[256,512]{1,0:T(8,128)S(1)}, f32[256,512]{1,0:T(8,128)}, u32[]{:S(2)}, u32[]{:S(2)}) collective-permute-start(f32[256,512]{1,0:T(8,128)S(1)} %get-tuple-element.42), channel_id=1, source_target_pairs={{0,1},{1,0},{2,3},{3,2},{4,5},{5,4},{6,7},{7,6},{8,9},{9,8},{10,11... | collective-permute-start | bytes 1572872 | tf_op jit(solution)/shard_map/ppermute | solution.py:461
  114.7 2.4 %copy-start.8 = (bf16[512,256]{1,0:T(8,128)(2,1)S(1)}, bf16[512,256]{1,0:T(8,128)(2,1)}, u32[]{:S(2)}) copy-start(bf16[512,256]{1,0:T(8,128)(2,1)} %down_ref.1) | copy-start | bytes 786436
  116.5 15.6 %copy-start.7 = (bf16[16,16,512]{2,1,0:T(8,128)(2,1)S(1)}, bf16[16,16,512]{2,1,0:T(8,128)(2,1)}, u32[]{:S(2)}) copy-start(bf16[16,16,512]{2,1,0:T(8,128)(2,1)} %up_ref.1) | copy-start | bytes 786436
  116.5 15.6 %copy-start.15 = (s32[8]{0:T(128)S(1)}, s32[8]{0:T(128)}, u32[]{:S(2)}) copy-start(s32[8]{0:T(128)} %tenant_ref.3) | copy-start | bytes 100
  116.5 15.6 %copy-start.17 = (s32[16]{0:T(128)S(1)}, s32[16]{0:T(128)}, u32[]{:S(2)}) copy-start(s32[16]{0:T(128)} %page_ref.3) | copy-start | bytes 196
  116.5 22.3 %collective-permute-start.23 = (f32[256,512]{1,0:T(8,128)S(1)}, f32[256,512]{1,0:T(8,128)S(1)}, u32[]{:S(2)}, u32[]{:S(2)}) collective-permute-start(f32[256,512]{1,0:T(8,128)S(1)} %get-tuple-element.56), channel_id=1, source_target_pairs={{0,1},{1,0},{2,3},{3,2},{4,5},{5,4},{6,7},{7,6},{8,9},{9,8},{10,11... | collective-permute-start | bytes 1572872 | tf_op jit(solution)/shard_map/ppermute | solution.py:461
  117.1 19.2 %copy-start.5 = (bf16[256,512]{1,0:T(8,128)(2,1)}, bf16[256,512]{1,0:T(8,128)(2,1)S(1)}, u32[]{:S(2)}) copy-start(bf16[256,512]{1,0:T(8,128)(2,1)S(1)} %constant_dynamic-update-slice_fusion.8.extras_ref) | copy-start | bytes 786436
  118.6 13.5 %all-to-all-start = ((bf16[16,16,512]{2,1,0:T(8,128)(2,1)}), bf16[16,16,512]{2,1,0:T(8,128)(2,1)S(1)}, u32[]{:S(2)}, u32[]{:S(2)}) async-start(bf16[16,16,512]{2,1,0:T(8,128)(2,1)} %shard_map.124), calls=%async_computation | async-start | bytes 524288 | tf_op jit(solution)/shard_map/all_to_all | solution.py:537
  132.1 2.2 %copy-start.1 = (bf16[1,256,8192]{2,1,0:T(8,128)(2,1)S(1)}, bf16[1,256,8192]{2,1,0:T(8,128)(2,1)}, u32[]{:S(2)}) copy-start(bf16[1,256,8192]{2,1,0:T(8,128)(2,1)} %param.12) | copy-start | bytes 12582916
  136.3 2.5 %copy-start.13 = (s32[2]{0:T(128)S(1)}, s32[2]{0:T(128)}, u32[]{:S(2)}) copy-start(s32[2]{0:T(128)} %copy-done.12) | copy-start | bytes 28
  138.9 0.8 copy-start.9
  139.7 0.7 copy-start.10
  142.0 1.9 %collective-permute-start.24 = (f32[4,40,128]{2,1,0:T(8,128)S(1)}, f32[4,40,128]{2,1,0:T(8,128)S(1)}, u32[]{:S(2)}, u32[]{:S(2)}) collective-permute-start(f32[4,40,128]{2,1,0:T(8,128)S(1)} %get-tuple-element.60), channel_id=1, source_target_pairs={{0,1},{1,0},{2,3},{3,2},{4,5},{5,4},{6,7},{7,6},{8,9},{9,8},{10,11... | collective-permute-start | bytes 245768 | tf_op jit(solution)/shard_map/ppermute | solution.py:461
  142.1 5.3 %collective-permute-start.25 = (f32[4,40,128]{2,1,0:T(8,128)S(1)}, f32[4,40,128]{2,1,0:T(8,128)S(1)}, u32[]{:S(2)}, u32[]{:S(2)}) collective-permute-start(f32[4,40,128]{2,1,0:T(8,128)S(1)} %get-tuple-element.61), channel_id=1, source_target_pairs={{0,2},{1,3},{2,0},{3,1},{4,6},{5,7},{6,4},{7,5},{8,10},{9,11},{10,... | collective-permute-start | bytes 245768 | tf_op jit(solution)/shard_map/ppermute | solution.py:461
  142.6 5.7 %collective-permute-start.26 = (f32[4,40,128]{2,1,0:T(8,128)S(1)}, f32[4,40,128]{2,1,0:T(8,128)S(1)}, u32[]{:S(2)}, u32[]{:S(2)}) collective-permute-start(f32[4,40,128]{2,1,0:T(8,128)S(1)} %get-tuple-element.62), channel_id=1, source_target_pairs={{0,3},{1,2},{2,1},{3,0},{4,7},{5,6},{6,5},{7,4},{8,11},{9,10},{10,... | collective-permute-start | bytes 245768 | tf_op jit(solution)/shard_map/ppermute | solution.py:461
  148.9 5.6 %collective-permute-start.27 = (f32[40,128]{1,0:T(8,128)S(1)}, f32[40,128]{1,0:T(8,128)S(1)}, u32[]{:S(2)}, u32[]{:S(2)}) collective-permute-start(f32[40,128]{1,0:T(8,128)S(1)} %get-tuple-element.64), channel_id=1, source_target_pairs={{0,4},{1,5},{2,6},{3,7},{4,8},{5,9},{6,10},{7,11},{8,12},{9,13},{1... | collective-permute-start | bytes 61448 | tf_op jit(solution)/shard_map/ppermute | solution.py:464
  149.0 5.6 %collective-permute-start.28 = (f32[40,128]{1,0:T(8,128)S(1)}, f32[40,128]{1,0:T(8,128)S(1)}, u32[]{:S(2)}, u32[]{:S(2)}) collective-permute-start(f32[40,128]{1,0:T(8,128)S(1)} %get-tuple-element.65), channel_id=1, source_target_pairs={{0,8},{1,9},{2,10},{3,11},{4,12},{5,13},{6,14},{7,15},{8,0},{9,1},... | collective-permute-start | bytes 61448 | tf_op jit(solution)/shard_map/ppermute | solution.py:464
  150.4 4.8 %collective-permute-start.29 = (f32[40,128]{1,0:T(8,128)S(1)}, f32[40,128]{1,0:T(8,128)S(1)}, u32[]{:S(2)}, u32[]{:S(2)}) collective-permute-start(f32[40,128]{1,0:T(8,128)S(1)} %get-tuple-element.66), channel_id=1, source_target_pairs={{0,12},{1,13},{2,14},{3,15},{4,0},{5,1},{6,2},{7,3},{8,4},{9,5},{1... | collective-permute-start | bytes 61448 | tf_op jit(solution)/shard_map/ppermute | solution.py:464
  (3 other events, 2.0 us)

commit v2 on v1

--- a/solution.py
+++ b/solution.py
@@ -141,6 +141,7 @@
 EXTRA = 16
 WINDOW = 4
 MESSAGE = 40
+IMAGES = 4
 
 
 def after(value, *others):
@@ -165,104 +166,131 @@
     )
 
 
-def split_kernel(place_ref, vision_ref, out_ref):
-    out_ref[...] = vision_ref[...]
-
-
-def split_vision(vision, core, rows):
+def send_kernel(half, targets, vision_ref, *refs):
+    out_refs, sems = refs[:-1], refs[-1]
+    y, core = lax.axis_index("groups"), lax.rem(lax.axis_index("image"), CORES)
+    started = []
+    for t, (core_flip, half_flip) in enumerate(targets):
+        at_core = 1 - core if core_flip else core
+        at_half = 1 - y if half_flip else y
+        for p in range(out_refs[t].shape[1] // half):
+            at = pl.multiple_of(((p * CORES + at_core) * 2 + at_half) * half, half)
+            copy = pltpu.make_async_copy(
+                vision_ref.at[:, pl.ds(at, half)],
+                out_refs[t].at[:, p * half : (p + 1) * half],
+                sems.at[t, p],
+            )
+            copy.start()
+            started.append(copy)
+    for copy in started:
+        copy.wait()
+
+
+def send_columns(vision, half, targets):
     keys, depth = vision.shape
-    shards = depth // rows // CORES
+    pairs = depth // half // (2 * CORES)
+    one = jax.ShapeDtypeStruct((keys, pairs * half), vision.dtype)
+    count = len(targets)
     return pl.pallas_call(
-        split_kernel,
-        out_shape=jax.ShapeDtypeStruct((keys, shards * rows), vision.dtype),
-        grid_spec=pltpu.PrefetchScalarGridSpec(
-            num_scalar_prefetch=1,
-            grid=(shards,),
-            in_specs=[pl.BlockSpec((keys, rows), lambda i, place: (0, CORES * i + 1 - place[0]))],
-            out_specs=pl.BlockSpec((keys, rows), lambda i, place: (0, i)),
-        ),
-        cost_estimate=pl.CostEstimate(flops=0, bytes_accessed=keys * depth * 2, transcendentals=0),
-    )(core.reshape(1), vision)
-
-
-def prepare_kernel(half, place_ref, text_ref, image_ref, tenant_ref, page_ref, queries_ref, key_ref, out_ref):
-    start = pl.multiple_of(place_ref[0] * half, half)
-    out_ref[0:half, :] = key_ref[pl.ds(start, half), :]
+        functools.partial(send_kernel, half, targets),
+        out_shape=[one] * count,
+        in_specs=whole(1, pl.ANY),
+        out_specs=whole(count, pl.ANY),
+        scratch_shapes=[pltpu.SemaphoreType.DMA((count, pairs))],
+        cost_estimate=pl.CostEstimate(flops=0, bytes_accessed=count * keys * depth, transcendentals=0),
+    )(vision)
+
+
+def prepare_kernel(
+    half, text_ref, image_ref, tiles_ref, tenant_ref, page_ref, queries_ref, key_ref, value_ref,
+    key_out, value_out, text, image, tiles, tenant, pages, line, sems,
+):
+    start = pl.multiple_of(lax.axis_index("groups") * half, half)
+    copies = [
+        pltpu.make_async_copy(*pair, sems.at[i])
+        for i, pair in enumerate(
+            (
+                (text_ref, text), (image_ref, image), (tiles_ref, tiles), (tenant_ref, tenant),
+                (page_ref, pages), (queries_ref, line),
+                (key_ref.at[pl.ds(start, half), :], key_out.at[0:half, :]),
+                (value_ref.at[pl.ds(start, half), :], value_out),
+            )
+        )
+    ]
+    for copy in copies:
+        copy.start()
+    for copy in copies:
+        copy.wait()
     width = key_ref.shape[1]
-    owner = image_ref[0, 0]
-    page = page_ref[tenant_ref[owner]]
+    owner = image[0, 0]
+    page = pages[tenant[owner]]
     row = lax.broadcasted_iota(jnp.int32, (EXTRA, width), 0)
     lane = lax.broadcasted_iota(jnp.int32, (EXTRA, width), 1)
     block = jnp.zeros((EXTRA, width), jnp.float32)
     for r in range(queries_ref.shape[1] // width):
-        piece = queries_ref[0:1, r * width : (r + 1) * width].astype(jnp.float32)
+        piece = line[0:1, r * width : (r + 1) * width].astype(jnp.float32)
         block = jnp.where(row == r, piece, block)
-    for at, number in enumerate((text_ref[0], owner, page)):
+    for at, number in enumerate((text[0], owner, page, tiles[0])):
         block = jnp.where((row == 8) & (lane == at), number.astype(jnp.float32), block)
-    out_ref[half : half + EXTRA, :] = block.astype(out_ref.dtype)
-
-
-def project_kernel(pieces, arrays, half, adds, *refs):
-    cols_ref, vision_ref, other_ref = refs[:3]
-    weight_refs = refs[3 : 3 + arrays]
-    before = refs[3 + arrays : 3 + arrays + adds]
-    own_ref, send_ref, slots, sems = refs[3 + arrays + adds :]
-    keys = own_ref.shape[0]
-
-    def copies(p):
-        own_at = pl.multiple_of(cols_ref[0, p] * half, half)
-        other_at = pl.multiple_of(cols_ref[1, p] * half, half)
-        to = p * half
-        return (
+    key_out[half : half + EXTRA, :] = block.astype(key_out.dtype)
+
+
+def project_kernel(pieces, arrays, half, *refs):
+    cols_ref = refs[0]
+    vision_refs = refs[1 : 1 + IMAGES]
+    weight_refs = refs[1 + IMAGES : 1 + IMAGES + arrays]
+    out_ref, slots, weights, sems = refs[1 + IMAGES + arrays :]
+    keys = vision_refs[0].shape[0]
+    count = len(pieces)
+    weight_copies = []
+    image_copies = [[] for _ in range(IMAGES)]
+    for p, (which, row) in enumerate(pieces):
+        weight_copies.append(
             pltpu.make_async_copy(
-                vision_ref.at[:, pl.ds(own_at, half)], slots.at[0:keys, to : to + half], sems.at[0, p]
-            ),
-            pltpu.make_async_copy(
-                other_ref.at[:, pl.ds(other_at, half)],
-                slots.at[keys : 2 * keys, to : to + half],
-                sems.at[1, p],
-            ),
+                weight_refs[which].at[row : row + half, :],
+                weights.at[p * half : (p + 1) * half, :],
+                sems.at[IMAGES, p],
+            )
         )
-
-    for p in range(len(pieces)):
-        for one in copies(p):
-            one.start()
-    total = [None, None]
-    for p, (which, row) in enumerate(pieces):
-        for one in copies(p):
-            one.wait()
-        weight = weight_refs[which][row : row + half, :]
-        for i in range(2):
-            term = jnp.dot(
-                slots[i * keys : (i + 1) * keys, p * half : (p + 1) * half],
-                weight,
-                preferred_element_type=jnp.float32,
+    for i in range(IMAGES):
+        for p in range(count):
+            at = pl.multiple_of(cols_ref[0 if i == 0 else 1, p] * half, half)
+            image_copies[i].append(
+                pltpu.make_async_copy(
+                    vision_refs[i].at[:, pl.ds(at, half)],
+                    slots.at[i, :, p * half : (p + 1) * half],
+                    sems.at[i, p],
+                )
             )
-            if p == 0 and adds:
-                total[i] = before[i][...] + term
-            else:
-                total[i] = term if total[i] is None else total[i] + term
-    own_ref[...] = total[0]
-    send_ref[...] = total[1]
-
-
-def project(vision, other, arrays, pieces, cols, half, before=()):
-    keys = vision.shape[0]
+    order = [weight_copies] + image_copies
+    for group in order:
+        for copy in group:
+            copy.start()
+    for copy in weight_copies:
+        copy.wait()
+    for i in range(IMAGES):
+        for copy in image_copies[i]:
+            copy.wait()
+        out_ref[i] = jnp.dot(slots[i], weights[...], preferred_element_type=jnp.float32)
+
+
+def project(images, arrays, pieces, cols, half):
+    keys = images[0].shape[0]
     width = arrays[0].shape[1]
-    result = jax.ShapeDtypeStruct((keys, width), jnp.float32)
     count = len(pieces)
     return call(
-        functools.partial(project_kernel, pieces, len(arrays), half, len(before)),
-        [result, result],
-        whole(1, pltpu.SMEM) + whole(2, pl.ANY) + whole(len(arrays) + len(before)),
+        functools.partial(project_kernel, pieces, len(arrays), half),
+        jax.ShapeDtypeStruct((IMAGES, keys, width), jnp.float32),
+        whole(1, pltpu.SMEM) + whole(IMAGES + len(arrays), pl.ANY),
         scratch=[
-            pltpu.VMEM((2 * keys, count * half), vision.dtype),
-            pltpu.SemaphoreType.DMA((2, count)),
+            pltpu.VMEM((IMAGES, keys, count * half), images[0].dtype),
+            pltpu.VMEM((count * half, width), arrays[0].dtype),
+            pltpu.SemaphoreType.DMA((IMAGES + 1, count)),
         ],
         vmem=24,
-        flops=4 * keys * half * width * count,
-        moved=count * half * (2 * keys + width) * 2,
-    )(cols, vision, other, *arrays, *before)
+        flops=2 * IMAGES * keys * half * width * count,
+        moved=count * half * (IMAGES * keys + width) * 2,
+    )(cols, *images, *arrays)
 
 
 def slot_of(token, me, steps):
@@ -273,8 +301,8 @@
     return across * steps + d
 
 
-def pick_kernel(total, steps, rank, place_ref, extras_ref, down_ref, out_ref, flat):
-    me = place_ref[1]
+def pick_kernel(total, steps, rank, extras_ref, down_ref, out_ref, flat):
+    me = lax.axis_index("image")
     flat[...] = down_ref[...].T
     for dest in range(total):
         at = pl.multiple_of(slot_of(jnp.int32(dest), me, steps) * EXTRA, EXTRA)
@@ -283,7 +311,11 @@
         out_ref[dest] = flat[pl.ds(pl.multiple_of(page * rank, rank), rank), :]
 
 
-def lowrank_kernel(image_ref, tenant_ref, page_ref, vision_ref, down_ref, up_ref, out_ref):
+def own_fact(extras_ref, lane):
+    return extras_ref[0:EXTRA, 0:HEAD].astype(jnp.float32)[8, lane].astype(jnp.int32)
+
+
+def lowrank_kernel(extras_ref, vision_ref, down_ref, up_ref, out_ref):
     shards, rank, rows = down_ref.shape
     total = jnp.zeros((vision_ref.shape[0], rank), jnp.float32)
     for j in range(shards):
@@ -293,7 +325,7 @@
             (((1,), (1,)), ((), ())),
             preferred_element_type=jnp.float32,
         )
-    page = page_ref[tenant_ref[image_ref[0, 0]]]
+    page = own_fact(extras_ref, 2)
     out_ref[...] = jnp.dot(
         total.astype(jnp.bfloat16), up_ref[page], preferred_element_type=jnp.float32
     )
@@ -316,12 +348,9 @@
     return result
 
 
-def score_kernel(
-    total, steps, place_ref, image_ref, tiles_ref, mine_ref, got_ref, gain_ref, extras_ref,
-    weights_ref, stats_ref, state_ref,
-):
-    me, owner = place_ref[1], image_ref[0, 0]
-    keys = mine_ref.shape[0]
+def score_kernel(total, steps, mine_ref, core_ref, pair_ref, gain_ref, extras_ref, weights_ref, stats_ref):
+    me, owner = lax.axis_index("image"), own_fact(extras_ref, 1)
+    keys = mine_ref.shape[1]
     first = window_start(extras_ref, owner, total)
     tiles = []
     match = []
@@ -331,7 +360,7 @@
         tiles += [block[0:8, k * HEAD : (k + 1) * HEAD] for k in range(KV_HEADS)]
         match.append(block[8, 0].astype(jnp.int32) == owner)
     query = jnp.concatenate(tiles, axis=0).astype(jnp.bfloat16)
-    key_raw = mine_ref[...] + got_ref[...]
+    key_raw = mine_ref[0] + core_ref[0] + pair_ref[...]
     gain = gain_ref[...]
     parts = []
     for k in range(KV_HEADS):
@@ -345,7 +374,7 @@
     row = lax.broadcasted_iota(jnp.int32, scores.shape, 0) // (8 * KV_HEADS)
     lane = lax.broadcasted_iota(jnp.int32, scores.shape, 1)
     limit = jnp.zeros(scores.shape, jnp.int32)
-    slots = tiles_ref[0] * (keys // TILES)
+    slots = own_fact(extras_ref, 3) * (keys // TILES)
     for s in range(WINDOW):
         limit = jnp.where(row == s, jnp.where(match[s], slots, 0), limit)
     usable = lane < limit
@@ -361,17 +390,15 @@
         own = slice(s * rows, (s + 1) * rows)
         top_row = jnp.sum(jnp.where(eye, top[own], 0.0), axis=0, keepdims=True)
         sum_row = jnp.sum(jnp.where(eye, sums[own], 0.0), axis=0, keepdims=True)
-        stats_ref[s] = jnp.where(line == 0, top_row, jnp.where(line == 1, sum_row, 0.0))
-        state_ref[1 + s] = match[s].astype(jnp.int32)
-    state_ref[0] = first
-
-
-def value_kernel(
-    steps, place_ref, state_ref, mine_ref, got_ref, lowrank_ref, weights_ref, stats_ref, *refs
-):
+        block = jnp.where(line == 0, top_row, jnp.where(line == 1, sum_row, 0.0))
+        block = jnp.where(line == 2, first.astype(jnp.float32), block)
+        stats_ref[s] = jnp.where(line == 3, jnp.where(match[s], 1.0, 0.0), block)
+
+
+def value_kernel(steps, mine_ref, core_ref, pair_ref, lowrank_ref, weights_ref, stats_ref, *refs):
     out_refs, numerators = refs[:-1], refs[-1]
-    me, first = place_ref[1], state_ref[0]
-    value = (mine_ref[...] + got_ref[...] + lowrank_ref[...]).astype(jnp.bfloat16)
+    me, first = lax.axis_index("image"), stats_ref[0][2, 0].astype(jnp.int32)
+    value = (mine_ref[0] + core_ref[0] + pair_ref[...] + lowrank_ref[...]).astype(jnp.bfloat16)
     weights = weights_ref[...]
     parts = [
         jnp.dot(weights, value[:, k * HEAD : (k + 1) * HEAD], preferred_element_type=jnp.float32)
@@ -382,6 +409,7 @@
     for s in range(WINDOW):
         numerators[s, 0:rows, :] = result[s * rows : (s + 1) * rows]
         numerators[s, rows:MESSAGE, :] = stats_ref[s]
+    match = [stats_ref[s][3, 0] for s in range(WINDOW)]
     line = lax.broadcasted_iota(jnp.int32, (MESSAGE, HEAD), 0)
     empty = jnp.where(line == rows, masked_score, 0.0)
     group = lax.rem(me, PLANE)
@@ -392,7 +420,10 @@
             s = z * PLANE + to - first
             inside = (s >= 0) & (s < WINDOW)
             s = jnp.clip(s, 0, WINDOW - 1)
-            good = inside & (state_ref[1 + s] == 1)
+            good = match[0] > 0.5
+            for j in range(1, WINDOW):
+                good = jnp.where(s == j, match[j], jnp.where(good, 1.0, 0.0)) > 0.5
+            good = inside & good
             out_ref[z] = jnp.where(good, numerators[s], empty)
 
 
@@ -410,7 +441,7 @@
     return numerator, top, total, eye
 
 
-def plane_kernel(steps, place_ref, *refs):
+def plane_kernel(steps, *refs):
     in_refs, out_refs, merged = refs[:PLANE], refs[PLANE : PLANE + steps], refs[-1]
     rows = 8 * KV_HEADS
     line = lax.broadcasted_iota(jnp.int32, (8, HEAD), 0)
@@ -419,7 +450,7 @@
         merged[z, 0:rows, :] = numerator
         merged[z, rows:MESSAGE, :] = jnp.where(line == 0, top, jnp.where(line == 1, total, 0.0))
     for d, out_ref in enumerate(out_refs):
-        out_ref[...] = merged[lax.rem(place_ref[1] // PLANE + d, steps)]
+        out_ref[...] = merged[lax.rem(lax.axis_index("image") // PLANE + d, steps)]
 
 
 def final_kernel(*refs):
@@ -428,7 +459,9 @@
     column = jnp.sum(jnp.where(eye, total, 0.0), axis=1, keepdims=True)
     out = numerator / column
     for k in range(KV_HEADS):
-        out_ref[:, k * HEAD : (k + 1) * HEAD] = out[8 * k : 8 * k + 8].astype(out_ref.dtype)
+        for r in range(8):
+            at = (r * KV_HEADS + k) * HEAD
+            out_ref[:, at : at + HEAD] = out[8 * k + r : 8 * k + r + 1].astype(out_ref.dtype)
 
 
 def local(
@@ -454,7 +487,6 @@
     rows, width = key_weight.shape
     half = rows // 2
     rank = up_pages.shape[1]
-    place = jnp.stack([y, me])
     everyone = range(devices)
 
     def across(value, bits):
@@ -463,131 +495,116 @@
     def along(value, d):
         return lax.ppermute(value, "image", [(i, (i - PLANE * d) % devices) for i in everyone])
 
-    def swap(value):
-        return lax.ppermute(value, "groups", [(0, 1), (1, 0)])
+    def swap(value, bits=0):
+        pairs = [(g * devices + i, (1 - g) * devices + (i ^ bits)) for g in range(2) for i in everyone]
+        return lax.ppermute(value, ("groups", "image"), pairs)
 
     def join(*arrays):
         return jnp.concatenate(arrays, axis=0)
 
-    key_half = call(
+    step = half + EXTRA
+    key_half, value_half = pl.pallas_call(
         functools.partial(prepare_kernel, half),
-        jax.ShapeDtypeStruct((half + EXTRA, width), key_weight.dtype),
-        whole(5, pltpu.SMEM) + whole(2),
-    )(place, text_request, image_request, request_tenant, tenant_page, queries, key_weight)
-    value_half = lax.dynamic_slice_in_dim(value_weight, y * half, half, 0)
-    extra = key_half[half:]
-
-    k_own = across(key_weight, CORES)
+        out_shape=[
+            jax.ShapeDtypeStruct((step, width), key_weight.dtype),
+            jax.ShapeDtypeStruct((half, width), value_weight.dtype),
+        ],
+        in_specs=whole(8, pl.ANY),
+        out_specs=whole(2),
+        scratch_shapes=[
+            pltpu.SMEM(text_request.shape, jnp.int32),
+            pltpu.SMEM(image_request.shape, jnp.int32),
+            pltpu.SMEM(image_tiles.shape, jnp.int32),
+            pltpu.SMEM(request_tenant.shape, jnp.int32),
+            pltpu.SMEM(tenant_page.shape, jnp.int32),
+            pltpu.VMEM(queries.shape, queries.dtype),
+            pltpu.SemaphoreType.DMA((8,)),
+        ],
+    )(text_request, image_request, image_tiles, request_tenant, tenant_page, queries, key_weight, value_weight)
+
+    to_pair, to_diagonal = send_columns(tokens, half, ((False, True), (True, True)))
+    (to_core,) = send_columns(tokens, half, ((True, False),))
+    from_pair = swap(to_pair)
+    from_diagonal = swap(after(to_diagonal, from_pair), 1)
+    from_core = across(to_core, 1)
+
     k1, k3 = along(key_half, 1), along(key_half, 3)
+    k_own = across(key_half, CORES)
     k2 = along(after(key_half, k1, k3, k_own), 2)
-    other = across(split_vision(tokens, core, rows), 1)
-    kx = across(after(join(k1, k3, extra), k_own), CORES)
-    ky = swap(after(join(k1[:half], k3[:half]), k_own))
-    kx2 = across(k2, CORES)
-    ky2 = swap(k2)
-    v1, v3 = along(after(value_half, k2), 1), along(after(value_half, k2), 3)
-    v_own = across(after(value_weight, kx, ky), CORES)
-    kd = swap(after(join(kx[:half], kx[half + EXTRA : 2 * half + EXTRA]), ky))
-    kd2 = swap(after(kx2, ky2))
-    v2 = along(after(value_half, v1, v3, v_own, kd), 2)
-    v_pair = join(v1, v3)
-    vx = across(after(v_pair, kx2, v_own), CORES)
-    vy = swap(after(v_pair, kd))
-    vx2 = across(after(v2, v_own), CORES)
-    vy2 = swap(after(v2, kd2))
-    vd = swap(after(vx, vy))
-    vd2 = across(after(vy2, vx), CORES)
-
-    def columns(spots):
-        own, other_at = [], []
-        for d, mirrored, part in spots:
-            pair = lax.rem(z + d, steps) * COLUMNS + (1 - x if mirrored else x)
-            at = part if isinstance(part, int) else jnp.where(part == "near", y, 1 - y)
-            at = {"near": y, "far": 1 - y}.get(part, part)
-            own.append((pair * CORES + core) * 2 + at)
-            other_at.append(pair * 2 + at)
-        return jnp.stack([jnp.stack([jnp.int32(0) + v for v in own]), jnp.stack([jnp.int32(0) + v for v in other_at])])
-
-    step = half + EXTRA
-    spots = [
-        (0, False, 0), (0, False, 1), (0, True, 0), (0, True, 1),
-        (1, False, "near"), (3, False, "near"), (2, False, "near"),
-        (1, True, "near"), (3, True, "near"), (2, True, "near"),
-        (1, False, "far"), (3, False, "far"), (2, False, "far"),
-        (1, True, "far"), (3, True, "far"), (2, True, "far"),
-    ]
-    cols = columns(spots)
-    key_arrays = [key_weight, k_own, k1, k3, k2, kx, kx2, ky, ky2, kd, kd2]
-    key_pieces = [
-        (0, 0), (0, half), (1, 0), (1, half), (2, 0), (3, 0), (4, 0),
-        (5, 0), (5, step), (6, 0), (7, 0), (7, half), (8, 0), (9, 0), (9, half), (10, 0),
-    ]
-    key_mine, key_send = project(tokens, other, key_arrays, tuple(key_pieces), cols, half)
-    key_got = across(key_send, 1)
-
-    near = join(extra, k1[half:], k2[half:], k3[half:], kx[2 * step :], kx[half:step], kx2[half:], kx[step + half : 2 * step])
+    kx = across(after(join(k1, k3), k_own), CORES)
+    v_own = across(after(value_half, k_own), CORES)
+    v1, v3 = along(after(value_half, k2, kx), 1), along(after(value_half, k2, kx), 3)
+    kx2 = across(after(k2, kx), CORES)
+    v2 = along(after(value_half, v1, v3), 2)
+    vx = across(after(join(v1, v3), kx2), CORES)
+    vx2 = across(v2, CORES)
+
+    spots = [(d, mirrored) for mirrored in (False, True) for d in (0, 1, 3, 2)]
+    pairs = [lax.rem(z + d, steps) * COLUMNS + (1 - x if mirrored else x) for d, mirrored in spots]
+    cols = jnp.stack([jnp.stack([(p * CORES + core) * 2 + y for p in pairs]), jnp.stack(pairs)])
+
+    near = join(key_half[half:], k1[half:], k2[half:], k3[half:], k_own[half:], kx[half:step], kx2[half:], kx[step + half :])
     extras = join(near, across(near, 1))
-
     picked = call(
         functools.partial(pick_kernel, devices, steps, rank),
         jax.ShapeDtypeStruct((devices, rank, rows), down_pages.dtype),
-        whole(1, pltpu.SMEM) + whole(2),
+        whole(2),
         scratch=[pltpu.VMEM(down_pages.shape[::-1], down_pages.dtype)],
-    )(place, extras, down_pages)
+    )(extras, down_pages)
     picked = lax.all_to_all(picked, "image", 0, 0, tiled=True)
     lowrank = call(
         lowrank_kernel,
         jax.ShapeDtypeStruct((tokens.shape[0], width), jnp.float32),
-        whole(3, pltpu.SMEM) + whole(3),
+        whole(4),
         vmem=16,
         moved=tokens.size * 2,
-    )(image_request, request_tenant, tenant_page, tokens, picked, up_pages)
+    )(extras, tokens, picked, up_pages)
+
+    images = [tokens, from_core, from_pair, from_diagonal]
+    pieces = ((0, 0), (2, 0), (3, 0), (4, 0), (1, 0), (5, 0), (5, step), (6, 0))
+    keys_part = project(images, [key_half, k_own, k1, k3, k2, kx, kx2], pieces, after(cols, lowrank), half)
+    pieces = ((0, 0), (2, 0), (3, 0), (4, 0), (1, 0), (5, 0), (5, half), (6, 0))
+    values_part = project(
+        images, [value_half, v_own, v1, v3, v2, vx, vx2], pieces, after(cols, keys_part), half
+    )
+
+    keys_core = across(jnp.stack([keys_part[1], keys_part[3]]), 1)
+    keys_pair = swap(keys_part[2] + keys_core[1])
+    values_core = across(jnp.stack([values_part[1], values_part[3]]), 1)
+    values_pair = swap(after(values_part[2] + values_core[1], keys_pair))
 
     heads = WINDOW * 8 * KV_HEADS
-    weights, stats, state = pl.pallas_call(
+    weights, stats = call(
         functools.partial(score_kernel, devices, steps),
-        out_shape=[
+        [
             jax.ShapeDtypeStruct((heads, tokens.shape[0]), jnp.bfloat16),
             jax.ShapeDtypeStruct((WINDOW, 8, HEAD), jnp.float32),
-            jax.ShapeDtypeStruct((WINDOW + 1,), jnp.int32),
         ],
-        in_specs=whole(3, pltpu.SMEM) + whole(4),
-        out_specs=whole(2) + whole(1, pltpu.SMEM),
-    )(place, image_request, image_tiles, key_mine, key_got, key_gain.reshape(1, HEAD), extras)
-
-    value_arrays = [value_weight, v_own, v1, v3, v2, vx, vx2, vy]
-    value_pieces = [
-        (0, 0), (0, half), (1, 0), (1, half), (2, 0), (3, 0), (4, 0),
-        (5, 0), (5, half), (6, 0), (7, 0), (7, half),
-    ]
-    early = project(tokens, other, value_arrays, tuple(value_pieces), cols[:, :12], half)
-    value_mine, value_send = project(
-        tokens, other, [vy2, vd, vd2], ((0, 0), (1, 0), (1, half), (2, 0)), cols[:, 12:], half, early
-    )
-    value_got = across(value_send, 1)
+        whole(5),
+    )(keys_part, keys_core, keys_pair, key_gain.reshape(1, HEAD), extras)
 
     message = jax.ShapeDtypeStruct((steps, MESSAGE, HEAD), jnp.float32)
     messages = call(
         functools.partial(value_kernel, steps),
         [message] * PLANE,
-        whole(2, pltpu.SMEM) + whole(5),
+        whole(6),
         scratch=[pltpu.VMEM((WINDOW, MESSAGE, HEAD), jnp.float32)],
-    )(place, state, value_mine, value_got, lowrank, weights, stats)
+    )(values_part, values_core, values_pair, lowrank, weights, stats)
     arrived = [messages[0]] + [across(messages[k], k) for k in range(1, PLANE)]
     one = jax.ShapeDtypeStruct((MESSAGE, HEAD), jnp.float32)
     merged = call(
         functools.partial(plane_kernel, steps),
         [one] * steps,
-        whole(1, pltpu.SMEM) + whole(PLANE),
+        whole(PLANE),
         scratch=[pltpu.VMEM((steps, MESSAGE, HEAD), jnp.float32)],
-    )(place, *arrived)
+    )(*arrived)
     arrived = [merged[0]] + [along(merged[d], steps - d) for d in range(1, steps)]
     out = call(
         final_kernel,
-        jax.ShapeDtypeStruct((8, KV_HEADS * HEAD), jnp.bfloat16),
+        jax.ShapeDtypeStruct(queries.shape, jnp.bfloat16),
         whole(steps),
     )(*arrived)
-    return out.reshape(queries.shape)
+    return out
 
 
 def fits(mesh, vision, queries, key_weight):

time: 157 us -> 227 us (1.45)
  Pallas kernels: 24 us -> 114 us
  waiting for transfers between devices: 88.4 us -> 64.6 us
    pallas_call x9, Pallas kernels: 20.6 us -> 112 us  [the longest x2 97.7 us: send_columns(): pl.pallas_call(functools.partial(send_kernel, half, targets), out_shape=[...]
    ppermute x9, waiting for transfers between devices: 41.9 us -> 30.5 us  [along(): lax.ppermute(value, 'image', [(i, (i - PLANE * d) % devices) for i in eve...]
    all_to_all x1, waiting for transfers between devices: 9.36 us -> 0.01 us  [local(): picked = lax.all_to_all(picked, 'image', 0, 0, tiled=True)]
    ppermute x7 -> x4, waiting for transfers between devices: 32.9 us -> 24.1 us  [swap(): return lax.ppermute(value, ('groups', 'image'), pairs)]
    ppermute x7 -> x4, starting transfers between devices: 8.68 us -> 2.74 us  [swap(): return lax.ppermute(value, ('groups', 'image'), pairs)]
    ppermute x14 -> x13, waiting for transfers between devices: 4.33 us -> 9.96 us  [across(): return lax.ppermute(value, 'image', [(i, i ^ bits) for i in everyone])]
    ppermute x9, starting transfers between devices: 10.5 us -> 14.6 us  [along(): lax.ppermute(value, 'image', [(i, (i - PLANE * d) % devices) for i in eve...]
    unnamed x52 -> x47, local copies, waits for them, and re-layouts: 9.01 us -> 10.6 us
  transfers between devices with their start and end apart: 31 -> 27, of which waited for: 13 -> 10; matrix products, arithmetic and copies ran while one was open for 0% -> 1% of each run, Pallas kernels for 14% -> 49%
where the time goes in v2:
time: 227 us; the launch traced here: 226 us
  Pallas kernels  114 us (50%)
  waiting for transfers between devices  64.6 us (28%)
  starting transfers between devices  31.7 us (14%)
  local copies, waits for them, and re-layouts  10.9 us (5%)
  between operations  2.4 us (1%)
    pallas_call x2, Pallas kernels, send_columns(): pl.pallas_call(functools.partial(send_kernel, half, targets), out_shape=[...  97.7 us
    ppermute x9, waiting for transfers between devices, along(): lax.ppermute(value, 'image', [(i, (i - PLANE * d) % devices) for i in eve...  30.5 us
    ppermute x4, waiting for transfers between devices, swap(): return lax.ppermute(value, ('groups', 'image'), pairs)  24.1 us
    ppermute x9, starting transfers between devices, along(): lax.ppermute(value, 'image', [(i, (i - PLANE * d) % devices) for i in eve...  14.6 us
    unnamed x47, local copies, waits for them, and re-layouts  10.6 us
    pallas_call x2, Pallas kernels, project(): call(functools.partial(project_kernel, pieces, len(arrays), half), jax.Sh...  10 us
    ppermute x13, waiting for transfers between devices, across(): return lax.ppermute(value, 'image', [(i, i ^ bits) for i in everyone])  9.96 us
    ppermute x13, starting transfers between devices, across(): return lax.ppermute(value, 'image', [(i, i ^ bits) for i in everyone])  9.9 us
  transfers between devices with their start and end apart: 27, of which 10 were waited for; matrix products, arithmetic and copies ran while one was open for 1% of the time, Pallas kernels for 49%

profile of v2, /device:TPU:0, one launch (start us, length us, event | category | flops | bytes accessed | tf_op | source)
XLA Modules:
  0.0 226.3 jit_solution(6464886290561939267)
XLA Ops:
  1.9 1.9 shard_map.118
  3.9 3.0 %collective-permute-start.2 = (bf16[272,512]{1,0:T(8,128)(2,1)}, bf16[272,512]{1,0:T(8,128)(2,1)}, u32[]{:S(2)}, u32[]{:S(2)}) collective-permute-start(bf16[272,512]{1,0:T(8,128)(2,1)} %get-tuple-element.31.refs_5_), channel_id=1, source_target_pairs={{0,2},{1,3},{2,0},{3,1},{4,6},{5,7},{6,4},{7,5},{8,10},{9,11},{10,... | collective-permute-start | bytes 835592 | tf_op jit(solution)/shard_map/ppermute | solution.py:493
  6.9 3.6 %collective-permute-start = (bf16[272,512]{1,0:T(8,128)(2,1)}, bf16[272,512]{1,0:T(8,128)(2,1)S(1)}, u32[]{:S(2)}, u32[]{:S(2)}) collective-permute-start(bf16[272,512]{1,0:T(8,128)(2,1)} %get-tuple-element.31.refs_5_), channel_id=1, source_target_pairs={{0,12},{1,13},{2,14},{3,15},{4,0},{5,1},{6,2},{7,3},{8,4},{9,5},{1... | collective-permute-start | bytes 835592 | tf_op jit(solution)/shard_map/ppermute | solution.py:496
  10.5 64.8 %shard_map.122 = (bf16[256,2048]{1,0:T(8,128)(2,1)}, bf16[256,2048]{1,0:T(8,128)(2,1)}) custom-call(bf16[256,8192]{1,0:T(8,128)(2,1)} %bitcast.24), custom_call_target="tpu_custom_call" | custom-call | bytes 4194304 | tf_op jit(solution)/shard_map/pallas_call | solution.py:194
  75.3 1.6 collective-permute-start.8
  76.9 32.9 %shard_map.121 = bf16[256,2048]{1,0:T(8,128)(2,1)} custom-call(bf16[256,8192]{1,0:T(8,128)(2,1)} %bitcast.25), custom_call_target="tpu_custom_call" | custom-call | bytes 2097152 | tf_op jit(solution)/shard_map/pallas_call | solution.py:194
  110.0 1.1 collective-permute-start.3
  111.1 0.6 collective-permute-start.4
  111.7 14.3 %collective-permute-done.3.refs_9_ = bf16[272,512]{1,0:T(8,128)(2,1)S(1)} collective-permute-done((bf16[272,512]{1,0:T(8,128)(2,1)S(1)}, bf16[272,512]{1,0:T(8,128)(2,1)S(1)}, u32[]{:S(2)}, u32[]{:S(2)}) %collective-permute-start.3) | collective-permute-done | bytes 278560 | tf_op jit(solution)/shard_map/ppermute | solution.py:496
  126.0 0.6 collective-permute-start.5
  126.6 0.7 constant_dynamic-update-slice_fusion.3
  127.3 3.0 %collective-permute-start.11 = (bf16[256,512]{1,0:T(8,128)(2,1)}, bf16[256,512]{1,0:T(8,128)(2,1)}, u32[]{:S(2)}, u32[]{:S(2)}) collective-permute-start(bf16[256,512]{1,0:T(8,128)(2,1)} %get-tuple-element.42.refs_5_), channel_id=1, source_target_pairs={{0,12},{1,13},{2,14},{3,15},{4,0},{5,1},{6,2},{7,3},{8,4},{9,5},{1... | collective-permute-start | bytes 786440 | tf_op jit(solution)/shard_map/ppermute | solution.py:496
  130.6 3.7 %collective-permute-done.5.refs_11_ = bf16[272,512]{1,0:T(8,128)(2,1)S(1)} collective-permute-done((bf16[272,512]{1,0:T(8,128)(2,1)S(1)}, bf16[272,512]{1,0:T(8,128)(2,1)S(1)}, u32[]{:S(2)}, u32[]{:S(2)}) %collective-permute-start.5) | collective-permute-done | bytes 278560 | tf_op jit(solution)/shard_map/ppermute | solution.py:493
  134.3 0.7 copy-done.9
  135.0 0.8 copy-done.7
  135.9 0.9 copy-done.15
  137.0 0.7 copy-done.6
  137.7 4.5 %all-to-all-start = ((bf16[16,16,512]{2,1,0:T(8,128)(2,1)}), bf16[16,16,512]{2,1,0:T(8,128)(2,1)}, u32[]{:S(2)}, u32[]{:S(2)}) async-start(bf16[16,16,512]{2,1,0:T(8,128)(2,1)} %copy-done.6), calls=%async_computation | async-start | bytes 524288 | tf_op jit(solution)/shard_map/all_to_all | solution.py:554
  142.2 2.8 %collective-permute-start.13 = (bf16[256,512]{1,0:T(8,128)(2,1)}, bf16[256,512]{1,0:T(8,128)(2,1)}, u32[]{:S(2)}, u32[]{:S(2)}) collective-permute-start(bf16[256,512]{1,0:T(8,128)(2,1)} %get-tuple-element.42.refs_5_), channel_id=1, source_target_pairs={{0,8},{1,9},{2,10},{3,11},{4,12},{5,13},{6,14},{7,15},{8,0},{9,1},... | collective-permute-start | bytes 786440 | tf_op jit(solution)/shard_map/ppermute | solution.py:496
  145.2 1.5 collective-permute-start.10
  146.8 1.8 pad_maximum_fusion.3
  148.6 0.6 collective-permute-start.14
  149.2 14.0 %collective-permute-done.13.refs_9_ = bf16[256,512]{1,0:T(8,128)(2,1)} collective-permute-done((bf16[256,512]{1,0:T(8,128)(2,1)}, bf16[256,512]{1,0:T(8,128)(2,1)}, u32[]{:S(2)}, u32[]{:S(2)}) %collective-permute-start.13) | collective-permute-done | bytes 262176 | tf_op jit(solution)/shard_map/ppermute | solution.py:496
  163.1 1.5 collective-permute-start.15
  164.6 2.2 copy-done
  166.8 0.9 copy-done.17
  167.8 2.6 %shard_map.120.lowrank_ref = f32[256,512]{1,0:T(8,128)S(1)} custom-call(bf16[256,512]{1,0:T(8,128)(2,1)S(1)} %constant_dynamic-update-slice_fusion.8.extras_ref, bf16[256,8192]{1,0:T(8,128)(2,1)S(1)} %bitcast.26, bf16[16,16,512]{2,1,0:T(8,128)(2,1)} %all-to-all-done.down_ref, bf16[16,16,512]{2,1,0:T(8,128)(2,1)S(1)} %copy-done.17), custom_call_target="tpu_custom_call" | custom-call | bytes 4194304 | tf_op jit(solution)/shard_map/pallas_call | solution.py:555
  170.4 0.9 copy-done.10
  171.3 1.0 copy-done.12
  172.3 1.0 copy-done.14
  173.3 4.8 %shard_map.123.mine_ref = f32[4,256,512]{2,1,0:T(8,128)S(1)} custom-call(s32[2,8]{1,0:T(2,128)S(1)} %pad_add_fusion.refs_0_, bf16[256,8192]{1,0:T(8,128)(2,1)S(1)} %bitcast.27, bf16[256,2048]{1,0:T(8,128)(2,1)S(1)} %collective-permute-done.7.refs_2_, bf16[256,2048]{1,0:T(8,128)(2,1)S(1)} %collective-permute-done.8.refs_3_, ...), custom_call_target="tpu_custom_call" | custom-call | flops 2147483648 | bytes 6291456 | tf_op jit(solution)/shard_map/pallas_call | solution.py:281
  178.4 0.7 copy-done.16
  179.0 5.2 %shard_map.124.mine_ref = f32[4,256,512]{2,1,0:T(8,128)S(1)} custom-call(s32[2,8]{1,0:T(2,128)S(1)} %pad_add_fusion.refs_0_, bf16[256,8192]{1,0:T(8,128)(2,1)S(1)} %bitcast.28, bf16[256,2048]{1,0:T(8,128)(2,1)S(1)} %collective-permute-done.7.refs_2_, bf16[256,2048]{1,0:T(8,128)(2,1)S(1)} %collective-permute-done.8.refs_3_, ...), custom_call_target="tpu_custom_call" | custom-call | flops 2147483648 | bytes 6291456 | tf_op jit(solution)/shard_map/pallas_call | solution.py:281
  184.6 0.6 collective-permute-start.18
  185.2 2.0 collective-permute-done.16.core_ref
  187.2 11.7 %collective-permute-done.18.pair_ref = f32[256,512]{1,0:T(8,128)S(1)} collective-permute-done((f32[256,512]{1,0:T(8,128)S(1)}, f32[256,512]{1,0:T(8,128)S(1)}, u32[]{:S(2)}, u32[]{:S(2)}) %collective-permute-start.18) | collective-permute-done | bytes 524320 | tf_op jit(solution)/shard_map/ppermute | solution.py:500
  199.0 0.5 collective-permute-start.19
  199.5 0.7 shard_map.125
  200.2 12.3 %collective-permute-done.19.pair_ref = f32[256,512]{1,0:T(8,128)S(1)} collective-permute-done((f32[256,512]{1,0:T(8,128)S(1)}, f32[256,512]{1,0:T(8,128)S(1)}, u32[]{:S(2)}, u32[]{:S(2)}) %collective-permute-start.19) | collective-permute-done | bytes 524320 | tf_op jit(solution)/shard_map/ppermute | solution.py:500
  213.0 0.6 collective-permute-start.21
  213.6 1.2 collective-permute-start.22
  214.9 3.4 %collective-permute-done.21.refs_2_ = f32[4,40,128]{2,1,0:T(8,128)S(1)} collective-permute-done((f32[4,40,128]{2,1,0:T(8,128)S(1)}, f32[4,40,128]{2,1,0:T(8,128)S(1)}, u32[]{:S(2)}, u32[]{:S(2)}) %collective-permute-start.21) | collective-permute-done | bytes 81952 | tf_op jit(solution)/shard_map/ppermute | solution.py:493
  218.3 0.8 collective-permute-done.22.refs_3_
  219.4 2.0 collective-permute-start.24
  221.4 1.8 collective-permute-start.25
  223.2 1.8 collective-permute-done.23.refs_1_
  225.0 0.6 collective-permute-done.25.refs_3_
  225.5 0.7 shard_map.128
  (77 shorter events, 2.2 us)
Async XLA Ops:
  3.9 106.0 %collective-permute-start.2 = (bf16[272,512]{1,0:T(8,128)(2,1)}, bf16[272,512]{1,0:T(8,128)(2,1)}, u32[]{:S(2)}, u32[]{:S(2)}) collective-permute-start(bf16[272,512]{1,0:T(8,128)(2,1)} %get-tuple-element.31.refs_5_), channel_id=1, source_target_pairs={{0,2},{1,3},{2,0},{3,1},{4,6},{5,7},{6,4},{7,5},{8,10},{9,11},{10,... | collective-permute-start | bytes 835592 | tf_op jit(solution)/shard_map/ppermute | solution.py:493
  6.9 103.0 %collective-permute-start = (bf16[272,512]{1,0:T(8,128)(2,1)}, bf16[272,512]{1,0:T(8,128)(2,1)S(1)}, u32[]{:S(2)}, u32[]{:S(2)}) collective-permute-start(bf16[272,512]{1,0:T(8,128)(2,1)} %get-tuple-element.31.refs_5_), channel_id=1, source_target_pairs={{0,12},{1,13},{2,14},{3,15},{4,0},{5,1},{6,2},{7,3},{8,4},{9,5},{1... | collective-permute-start | bytes 835592 | tf_op jit(solution)/shard_map/ppermute | solution.py:496
  10.5 99.5 %collective-permute-start.1 = (bf16[272,512]{1,0:T(8,128)(2,1)}, bf16[272,512]{1,0:T(8,128)(2,1)S(1)}, u32[]{:S(2)}, u32[]{:S(2)}) collective-permute-start(bf16[272,512]{1,0:T(8,128)(2,1)} %get-tuple-element.31.refs_5_), channel_id=1, source_target_pairs={{0,4},{1,5},{2,6},{3,7},{4,8},{5,9},{6,10},{7,11},{8,12},{9,13},{1... | collective-permute-start | bytes 835592 | tf_op jit(solution)/shard_map/ppermute | solution.py:496
  75.3 34.6 %copy-start.11 = (bf16[272,512]{1,0:T(8,128)(2,1)S(1)}, bf16[272,512]{1,0:T(8,128)(2,1)}, u32[]{:S(2)}) copy-start(bf16[272,512]{1,0:T(8,128)(2,1)} %get-tuple-element.31.refs_5_) | copy-start | bytes 835588
  75.3 55.2 %collective-permute-start.8 = (bf16[256,2048]{1,0:T(8,128)(2,1)}, bf16[256,2048]{1,0:T(8,128)(2,1)S(1)}, u32[]{:S(2)}, u32[]{:S(2)}) collective-permute-start(bf16[256,2048]{1,0:T(8,128)(2,1)} %get-tuple-element.35), channel_id=1, source_target_pairs={{0,16},{1,17},{2,18},{3,19},{4,20},{5,21},{6,22},{7,23},{8,24},{9,... | collective-permute-start | bytes 3145736 | tf_op jit(solution)/shard_map/ppermute | solution.py:500
  109.8 60.5 %collective-permute-start.7 = (bf16[256,2048]{1,0:T(8,128)(2,1)}, bf16[256,2048]{1,0:T(8,128)(2,1)S(1)}, u32[]{:S(2)}, u32[]{:S(2)}) collective-permute-start(bf16[256,2048]{1,0:T(8,128)(2,1)} %shard_map.121), channel_id=1, source_target_pairs={{0,1},{1,0},{2,3},{3,2},{4,5},{5,4},{6,7},{7,6},{8,9},{9,8},{10,11... | collective-permute-start | bytes 3145736 | tf_op jit(solution)/shard_map/ppermute | solution.py:493
  109.9 20.6 %copy-start.2 = (bf16[272,512]{1,0:T(8,128)(2,1)}, bf16[272,512]{1,0:T(8,128)(2,1)S(1)}, u32[]{:S(2)}) copy-start(bf16[272,512]{1,0:T(8,128)(2,1)S(1)} %collective-permute-done.refs_7_) | copy-start | bytes 835588
  110.0 20.6 %copy-start.4 = (bf16[272,512]{1,0:T(8,128)(2,1)}, bf16[272,512]{1,0:T(8,128)(2,1)S(1)}, u32[]{:S(2)}) copy-start(bf16[272,512]{1,0:T(8,128)(2,1)S(1)} %collective-permute-done.1.refs_8_) | copy-start | bytes 835588
  110.0 16.0 %collective-permute-start.3 = (bf16[272,512]{1,0:T(8,128)(2,1)S(1)}, bf16[272,512]{1,0:T(8,128)(2,1)S(1)}, u32[]{:S(2)}, u32[]{:S(2)}) collective-permute-start(bf16[272,512]{1,0:T(8,128)(2,1)S(1)} %copy-done.11), channel_id=1, source_target_pairs={{0,8},{1,9},{2,10},{3,11},{4,12},{5,13},{6,14},{7,15},{8,0},{9,1},... | collective-permute-start | bytes 835592 | tf_op jit(solution)/shard_map/ppermute | solution.py:496
  111.1 14.9 %collective-permute-start.4 = (bf16[544,512]{1,0:T(8,128)(2,1)S(1)}, bf16[544,512]{1,0:T(8,128)(2,1)S(1)}, u32[]{:S(2)}, u32[]{:S(2)}) collective-permute-start(bf16[544,512]{1,0:T(8,128)(2,1)S(1)} %pad_maximum_fusion.2), channel_id=1, source_target_pairs={{0,2},{1,3},{2,0},{3,1},{4,6},{5,7},{6,4},{7,5},{8,10},{9,11},{10,... | collective-permute-start | bytes 1671176 | tf_op jit(solution)/shard_map/ppermute | solution.py:493
  125.9 9.9 %copy-start.13 = (bf16[272,512]{1,0:T(8,128)(2,1)}, bf16[272,512]{1,0:T(8,128)(2,1)S(1)}, u32[]{:S(2)}) copy-start(bf16[272,512]{1,0:T(8,128)(2,1)S(1)} %collective-permute-done.3.refs_9_) | copy-start | bytes 835588
  126.0 8.3 %collective-permute-start.5 = (bf16[272,512]{1,0:T(8,128)(2,1)S(1)}, bf16[272,512]{1,0:T(8,128)(2,1)S(1)}, u32[]{:S(2)}, u32[]{:S(2)}) collective-permute-start(bf16[272,512]{1,0:T(8,128)(2,1)S(1)} %collective-permute-done.3.refs_9_), channel_id=1, source_target_pairs={{0,2},{1,3},{2,0},{3,1},{4,6},{5,7},{6,4},{7,5},{8,10},{9,11},{10,... | collective-permute-start | bytes 835592 | tf_op jit(solution)/shard_map/ppermute | solution.py:493
  127.3 14.9 %collective-permute-start.11 = (bf16[256,512]{1,0:T(8,128)(2,1)}, bf16[256,512]{1,0:T(8,128)(2,1)}, u32[]{:S(2)}, u32[]{:S(2)}) collective-permute-start(bf16[256,512]{1,0:T(8,128)(2,1)} %get-tuple-element.42.refs_5_), channel_id=1, source_target_pairs={{0,12},{1,13},{2,14},{3,15},{4,0},{5,1},{6,2},{7,3},{8,4},{9,5},{1... | collective-permute-start | bytes 786440 | tf_op jit(solution)/shard_map/ppermute | solution.py:496
  130.2 12.0 %collective-permute-start.12 = (bf16[256,512]{1,0:T(8,128)(2,1)}, bf16[256,512]{1,0:T(8,128)(2,1)}, u32[]{:S(2)}, u32[]{:S(2)}) collective-permute-start(bf16[256,512]{1,0:T(8,128)(2,1)} %get-tuple-element.42.refs_5_), channel_id=1, source_target_pairs={{0,4},{1,5},{2,6},{3,7},{4,8},{5,9},{6,10},{7,11},{8,12},{9,13},{1... | collective-permute-start | bytes 786440 | tf_op jit(solution)/shard_map/ppermute | solution.py:496
  130.5 39.8 %collective-permute-start.9 = (bf16[256,2048]{1,0:T(8,128)(2,1)}, bf16[256,2048]{1,0:T(8,128)(2,1)S(1)}, u32[]{:S(2)}, u32[]{:S(2)}) collective-permute-start(bf16[256,2048]{1,0:T(8,128)(2,1)} %get-tuple-element.37), channel_id=1, source_target_pairs={{0,17},{1,16},{2,19},{3,18},{4,21},{5,20},{6,23},{7,22},{8,25},{9,... | collective-permute-start | bytes 3145736 | tf_op jit(solution)/shard_map/ppermute | solution.py:500
  134.3 1.6 collective-permute-start.6
  134.3 0.7 copy-start.9
  135.0 0.8 copy-start.7
  135.9 1.0 copy-start.15
  137.0 0.7 copy-start.6
  137.7 26.9 %all-to-all-start = ((bf16[16,16,512]{2,1,0:T(8,128)(2,1)}), bf16[16,16,512]{2,1,0:T(8,128)(2,1)}, u32[]{:S(2)}, u32[]{:S(2)}) async-start(bf16[16,16,512]{2,1,0:T(8,128)(2,1)} %copy-done.6), calls=%async_computation | async-start | bytes 524288 | tf_op jit(solution)/shard_map/all_to_all | solution.py:554
  142.2 20.9 %collective-permute-start.13 = (bf16[256,512]{1,0:T(8,128)(2,1)}, bf16[256,512]{1,0:T(8,128)(2,1)}, u32[]{:S(2)}, u32[]{:S(2)}) collective-permute-start(bf16[256,512]{1,0:T(8,128)(2,1)} %get-tuple-element.42.refs_5_), channel_id=1, source_target_pairs={{0,8},{1,9},{2,10},{3,11},{4,12},{5,13},{6,14},{7,15},{8,0},{9,1},... | collective-permute-start | bytes 786440 | tf_op jit(solution)/shard_map/ppermute | solution.py:496
  145.2 33.1 %collective-permute-start.10 = (bf16[256,512]{1,0:T(8,128)(2,1)}, bf16[256,512]{1,0:T(8,128)(2,1)}, u32[]{:S(2)}, u32[]{:S(2)}) collective-permute-start(bf16[256,512]{1,0:T(8,128)(2,1)} %get-tuple-element.42.refs_5_), channel_id=1, source_target_pairs={{0,2},{1,3},{2,0},{3,1},{4,6},{5,7},{6,4},{7,5},{8,10},{9,11},{10,... | collective-permute-start | bytes 786440 | tf_op jit(solution)/shard_map/ppermute | solution.py:493
  148.6 29.7 %collective-permute-start.14 = (bf16[512,512]{1,0:T(8,128)(2,1)}, bf16[512,512]{1,0:T(8,128)(2,1)}, u32[]{:S(2)}, u32[]{:S(2)}) collective-permute-start(bf16[512,512]{1,0:T(8,128)(2,1)} %pad_maximum_fusion.3), channel_id=1, source_target_pairs={{0,2},{1,3},{2,0},{3,1},{4,6},{5,7},{6,4},{7,5},{8,10},{9,11},{10,... | collective-permute-start | bytes 1572872 | tf_op jit(solution)/shard_map/ppermute | solution.py:493
  163.1 15.2 %collective-permute-start.15 = (bf16[256,512]{1,0:T(8,128)(2,1)}, bf16[256,512]{1,0:T(8,128)(2,1)}, u32[]{:S(2)}, u32[]{:S(2)}) collective-permute-start(bf16[256,512]{1,0:T(8,128)(2,1)} %collective-permute-done.13.refs_9_), channel_id=1, source_target_pairs={{0,2},{1,3},{2,0},{3,1},{4,6},{5,7},{6,4},{7,5},{8,10},{9,11},{10,... | collective-permute-start | bytes 786440 | tf_op jit(solution)/shard_map/ppermute | solution.py:493
  164.6 2.2 copy-start
  166.8 0.9 copy-start.17
  167.7 2.6 %copy-start.1 = (bf16[1,256,8192]{2,1,0:T(8,128)(2,1)S(1)}, bf16[1,256,8192]{2,1,0:T(8,128)(2,1)}, u32[]{:S(2)}) copy-start(bf16[1,256,8192]{2,1,0:T(8,128)(2,1)} %param.12) | copy-start | bytes 12582916
  167.7 2.6 %copy-start.3 = (bf16[272,512]{1,0:T(8,128)(2,1)S(1)}, bf16[272,512]{1,0:T(8,128)(2,1)}, u32[]{:S(2)}) copy-start(bf16[272,512]{1,0:T(8,128)(2,1)} %copy-done.2) | copy-start | bytes 835588
  167.7 2.6 %copy-start.5 = (bf16[272,512]{1,0:T(8,128)(2,1)S(1)}, bf16[272,512]{1,0:T(8,128)(2,1)}, u32[]{:S(2)}) copy-start(bf16[272,512]{1,0:T(8,128)(2,1)} %copy-done.4) | copy-start | bytes 835588
  167.7 2.6 %copy-start.8 = (bf16[544,512]{1,0:T(8,128)(2,1)S(1)}, bf16[544,512]{1,0:T(8,128)(2,1)}, u32[]{:S(2)}) copy-start(bf16[544,512]{1,0:T(8,128)(2,1)} %copy-done.7) | copy-start | bytes 1671172
  170.4 1.0 copy-start.10
  171.3 1.0 copy-start.12
  172.3 1.0 copy-start.14
  178.1 1.0 copy-start.16
  178.2 6.3 %collective-permute-start.17 = (f32[2,256,512]{2,1,0:T(8,128)S(1)}, f32[2,256,512]{2,1,0:T(8,128)S(1)}, u32[]{:S(2)}, u32[]{:S(2)}) collective-permute-start(f32[2,256,512]{2,1,0:T(8,128)S(1)} %pad_maximum_fusion.1), channel_id=1, source_target_pairs={{0,1},{1,0},{2,3},{3,2},{4,5},{5,4},{6,7},{7,6},{8,9},{9,8},{10,11... | collective-permute-start | bytes 3145736 | tf_op jit(solution)/shard_map/ppermute | solution.py:493
  184.4 15.1 %copy-start.18 = (f32[128]{0:T(128)S(1)}, f32[128]{0:T(128)}, u32[]{:S(2)}) copy-start(f32[128]{0:T(128)} %param.17) | copy-start | bytes 1540
  184.4 2.7 %collective-permute-start.16 = (f32[2,256,512]{2,1,0:T(8,128)S(1)}, f32[2,256,512]{2,1,0:T(8,128)S(1)}, u32[]{:S(2)}, u32[]{:S(2)}) collective-permute-start(f32[2,256,512]{2,1,0:T(8,128)S(1)} %pad_maximum_fusion), channel_id=1, source_target_pairs={{0,1},{1,0},{2,3},{3,2},{4,5},{5,4},{6,7},{7,6},{8,9},{9,8},{10,11... | collective-permute-start | bytes 3145736 | tf_op jit(solution)/shard_map/ppermute | solution.py:493
  184.6 14.4 %collective-permute-start.18 = (f32[256,512]{1,0:T(8,128)S(1)}, f32[256,512]{1,0:T(8,128)S(1)}, u32[]{:S(2)}, u32[]{:S(2)}) collective-permute-start(f32[256,512]{1,0:T(8,128)S(1)} %fusion), channel_id=1, source_target_pairs={{0,16},{1,17},{2,18},{3,19},{4,20},{5,21},{6,22},{7,23},{8,24},{9,... | collective-permute-start | bytes 1572872 | tf_op jit(solution)/shard_map/ppermute | solution.py:500
  199.0 13.5 %collective-permute-start.19 = (f32[256,512]{1,0:T(8,128)S(1)}, f32[256,512]{1,0:T(8,128)S(1)}, u32[]{:S(2)}, u32[]{:S(2)}) collective-permute-start(f32[256,512]{1,0:T(8,128)S(1)} %fusion.1), channel_id=1, source_target_pairs={{0,16},{1,17},{2,18},{3,19},{4,20},{5,21},{6,22},{7,23},{8,24},{9,... | collective-permute-start | bytes 1572872 | tf_op jit(solution)/shard_map/ppermute | solution.py:500
  212.9 1.9 collective-permute-start.20
  213.0 5.3 %collective-permute-start.21 = (f32[4,40,128]{2,1,0:T(8,128)S(1)}, f32[4,40,128]{2,1,0:T(8,128)S(1)}, u32[]{:S(2)}, u32[]{:S(2)}) collective-permute-start(f32[4,40,128]{2,1,0:T(8,128)S(1)} %get-tuple-element.49), channel_id=1, source_target_pairs={{0,2},{1,3},{2,0},{3,1},{4,6},{5,7},{6,4},{7,5},{8,10},{9,11},{10,... | collective-permute-start | bytes 245768 | tf_op jit(solution)/shard_map/ppermute | solution.py:493
  213.6 5.5 %collective-permute-start.22 = (f32[4,40,128]{2,1,0:T(8,128)S(1)}, f32[4,40,128]{2,1,0:T(8,128)S(1)}, u32[]{:S(2)}, u32[]{:S(2)}) collective-permute-start(f32[4,40,128]{2,1,0:T(8,128)S(1)} %get-tuple-element.50), channel_id=1, source_target_pairs={{0,3},{1,2},{2,1},{3,0},{4,7},{5,6},{6,5},{7,4},{8,11},{9,10},{10,... | collective-permute-start | bytes 245768 | tf_op jit(solution)/shard_map/ppermute | solution.py:493
  219.3 5.6 %collective-permute-start.23 = (f32[40,128]{1,0:T(8,128)S(1)}, f32[40,128]{1,0:T(8,128)S(1)}, u32[]{:S(2)}, u32[]{:S(2)}) collective-permute-start(f32[40,128]{1,0:T(8,128)S(1)} %get-tuple-element.52), channel_id=1, source_target_pairs={{0,4},{1,5},{2,6},{3,7},{4,8},{5,9},{6,10},{7,11},{8,12},{9,13},{1... | collective-permute-start | bytes 61448 | tf_op jit(solution)/shard_map/ppermute | solution.py:496
  219.4 5.6 %collective-permute-start.24 = (f32[40,128]{1,0:T(8,128)S(1)}, f32[40,128]{1,0:T(8,128)S(1)}, u32[]{:S(2)}, u32[]{:S(2)}) collective-permute-start(f32[40,128]{1,0:T(8,128)S(1)} %get-tuple-element.53), channel_id=1, source_target_pairs={{0,8},{1,9},{2,10},{3,11},{4,12},{5,13},{6,14},{7,15},{8,0},{9,1},... | collective-permute-start | bytes 61448 | tf_op jit(solution)/shard_map/ppermute | solution.py:496
  221.4 4.1 %collective-permute-start.25 = (f32[40,128]{1,0:T(8,128)S(1)}, f32[40,128]{1,0:T(8,128)S(1)}, u32[]{:S(2)}, u32[]{:S(2)}) collective-permute-start(f32[40,128]{1,0:T(8,128)S(1)} %get-tuple-element.54), channel_id=1, source_target_pairs={{0,12},{1,13},{2,14},{3,15},{4,0},{5,1},{6,2},{7,3},{8,4},{9,5},{1... | collective-permute-start | bytes 61448 | tf_op jit(solution)/shard_map/ppermute | solution.py:496

commit v3 on v2

--- a/solution.py
+++ b/solution.py
@@ -166,23 +166,29 @@
     )
 
 
-def send_kernel(half, targets, vision_ref, *refs):
-    out_refs, sems = refs[:-1], refs[-1]
+def column_copies(half, targets, vision_ref, out_refs, sems):
     y, core = lax.axis_index("groups"), lax.rem(lax.axis_index("image"), CORES)
-    started = []
+    copies = []
     for t, (core_flip, half_flip) in enumerate(targets):
         at_core = 1 - core if core_flip else core
         at_half = 1 - y if half_flip else y
         for p in range(out_refs[t].shape[1] // half):
             at = pl.multiple_of(((p * CORES + at_core) * 2 + at_half) * half, half)
-            copy = pltpu.make_async_copy(
-                vision_ref.at[:, pl.ds(at, half)],
-                out_refs[t].at[:, p * half : (p + 1) * half],
-                sems.at[t, p],
+            copies.append(
+                pltpu.make_async_copy(
+                    vision_ref.at[:, pl.ds(at, half)],
+                    out_refs[t].at[:, p * half : (p + 1) * half],
+                    sems.at[t, p],
+                )
             )
-            copy.start()
-            started.append(copy)
-    for copy in started:
+    return copies
+
+
+def send_kernel(half, targets, vision_ref, *refs):
+    copies = column_copies(half, targets, vision_ref, refs[:-1], refs[-1])
+    for copy in copies:
+        copy.start()
+    for copy in copies:
         copy.wait()
 
 
@@ -195,15 +201,15 @@
         functools.partial(send_kernel, half, targets),
         out_shape=[one] * count,
         in_specs=whole(1, pl.ANY),
-        out_specs=whole(count, pl.ANY),
+        out_specs=whole(count),
         scratch_shapes=[pltpu.SemaphoreType.DMA((count, pairs))],
         cost_estimate=pl.CostEstimate(flops=0, bytes_accessed=count * keys * depth, transcendentals=0),
     )(vision)
 
 
 def prepare_kernel(
-    half, text_ref, image_ref, tiles_ref, tenant_ref, page_ref, queries_ref, key_ref, value_ref,
-    key_out, value_out, text, image, tiles, tenant, pages, line, sems,
+    half, text_ref, image_ref, tiles_ref, tenant_ref, page_ref, queries_ref, key_ref, value_ref, vision_ref,
+    key_out, value_out, pair_out, diagonal_out, text, image, tiles, tenant, pages, line, sems, column_sems,
 ):
     start = pl.multiple_of(lax.axis_index("groups") * half, half)
     copies = [
@@ -217,7 +223,10 @@
             )
         )
     ]
-    for copy in copies:
+    columns = column_copies(
+        half, ((False, True), (True, True)), vision_ref, (pair_out, diagonal_out), column_sems
+    )
+    for copy in copies + columns:
         copy.start()
     for copy in copies:
         copy.wait()
@@ -233,28 +242,33 @@
     for at, number in enumerate((text[0], owner, page, tiles[0])):
         block = jnp.where((row == 8) & (lane == at), number.astype(jnp.float32), block)
     key_out[half : half + EXTRA, :] = block.astype(key_out.dtype)
-
-
-def project_kernel(pieces, arrays, half, *refs):
-    cols_ref = refs[0]
-    vision_refs = refs[1 : 1 + IMAGES]
-    weight_refs = refs[1 + IMAGES : 1 + IMAGES + arrays]
-    out_ref, slots, weights, sems = refs[1 + IMAGES + arrays :]
-    keys = vision_refs[0].shape[0]
+    for copy in columns:
+        copy.wait()
+
+
+def project_kernel(pieces, spots, images, own, arrays, adds, half, steps, *refs):
+    vision_refs = refs[:images]
+    weight_refs = refs[images : images + arrays]
+    before = refs[images + arrays : images + arrays + adds]
+    out_ref, slots, weights, sems = refs[images + arrays + adds :]
+    me, y = lax.axis_index("image"), lax.axis_index("groups")
+    z, x, core = me // PLANE, me // CORES % COLUMNS, me % CORES
     count = len(pieces)
     weight_copies = []
-    image_copies = [[] for _ in range(IMAGES)]
+    image_copies = [[] for _ in range(images)]
     for p, (which, row) in enumerate(pieces):
         weight_copies.append(
             pltpu.make_async_copy(
                 weight_refs[which].at[row : row + half, :],
                 weights.at[p * half : (p + 1) * half, :],
-                sems.at[IMAGES, p],
+                sems.at[images, p],
             )
         )
-    for i in range(IMAGES):
+    for i in range(images):
         for p in range(count):
-            at = pl.multiple_of(cols_ref[0 if i == 0 else 1, p] * half, half)
+            d, mirrored = spots[p]
+            pair = lax.rem(z + d, steps) * COLUMNS + (1 - x if mirrored else x)
+            at = pl.multiple_of(((pair * CORES + core) * 2 + y if i == own else pair) * half, half)
             image_copies[i].append(
                 pltpu.make_async_copy(
                     vision_refs[i].at[:, pl.ds(at, half)],
@@ -268,29 +282,31 @@
             copy.start()
     for copy in weight_copies:
         copy.wait()
-    for i in range(IMAGES):
+    for i in range(images):
         for copy in image_copies[i]:
             copy.wait()
-        out_ref[i] = jnp.dot(slots[i], weights[...], preferred_element_type=jnp.float32)
-
-
-def project(images, arrays, pieces, cols, half):
-    keys = images[0].shape[0]
+        product = jnp.dot(slots[i], weights[...], preferred_element_type=jnp.float32)
+        out_ref[i] = before[0][i] + product if adds else product
+
+
+def project(images, own, arrays, pieces, spots, half, steps, *before):
+    keys = images[-1].shape[0]
     width = arrays[0].shape[1]
     count = len(pieces)
+    number = len(images)
     return call(
-        functools.partial(project_kernel, pieces, len(arrays), half),
-        jax.ShapeDtypeStruct((IMAGES, keys, width), jnp.float32),
-        whole(1, pltpu.SMEM) + whole(IMAGES + len(arrays), pl.ANY),
+        functools.partial(project_kernel, pieces, spots, number, own, len(arrays), len(before), half, steps),
+        jax.ShapeDtypeStruct((number, keys, width), jnp.float32),
+        whole(number + len(arrays), pl.ANY) + whole(len(before)),
         scratch=[
-            pltpu.VMEM((IMAGES, keys, count * half), images[0].dtype),
+            pltpu.VMEM((number, keys, count * half), images[0].dtype),
             pltpu.VMEM((count * half, width), arrays[0].dtype),
-            pltpu.SemaphoreType.DMA((IMAGES + 1, count)),
+            pltpu.SemaphoreType.DMA((number + 1, count)),
         ],
-        vmem=24,
-        flops=2 * IMAGES * keys * half * width * count,
-        moved=count * half * (IMAGES * keys + width) * 2,
-    )(cols, *images, *arrays)
+        vmem=16,
+        flops=2 * number * keys * half * width * count,
+        moved=count * half * (number * keys + width) * 2,
+    )(*images, *arrays, *before)
 
 
 def slot_of(token, me, steps):
@@ -304,23 +320,24 @@
 def pick_kernel(total, steps, rank, extras_ref, down_ref, out_ref, flat):
     me = lax.axis_index("image")
     flat[...] = down_ref[...].T
-    for dest in range(total):
-        at = pl.multiple_of(slot_of(jnp.int32(dest), me, steps) * EXTRA, EXTRA)
+    for k in range(total):
+        at = pl.multiple_of(slot_of(jnp.bitwise_xor(me, k), me, steps) * EXTRA, EXTRA)
         tile = extras_ref[pl.ds(at, EXTRA), 0:HEAD].astype(jnp.float32)
         page = tile[8, 2].astype(jnp.int32)
-        out_ref[dest] = flat[pl.ds(pl.multiple_of(page * rank, rank), rank), :]
+        out_ref[k] = flat[pl.ds(pl.multiple_of(page * rank, rank), rank), :]
 
 
 def own_fact(extras_ref, lane):
     return extras_ref[0:EXTRA, 0:HEAD].astype(jnp.float32)[8, lane].astype(jnp.int32)
 
 
-def lowrank_kernel(extras_ref, vision_ref, down_ref, up_ref, out_ref):
+def lowrank_kernel(order, extras_ref, vision_ref, down_ref, up_ref, out_ref):
     shards, rank, rows = down_ref.shape
     total = jnp.zeros((vision_ref.shape[0], rank), jnp.float32)
     for j in range(shards):
+        shard = jnp.bitwise_xor(lax.axis_index("image"), order[j])
         total = total + lax.dot_general(
-            vision_ref[:, j * rows : (j + 1) * rows],
+            vision_ref[:, pl.ds(pl.multiple_of(shard * rows, rows), rows)],
             down_ref[j],
             (((1,), (1,)), ((), ())),
             preferred_element_type=jnp.float32,
@@ -348,7 +365,9 @@
     return result
 
 
-def score_kernel(total, steps, mine_ref, core_ref, pair_ref, gain_ref, extras_ref, weights_ref, stats_ref):
+def score_kernel(
+    total, steps, mine_ref, core_ref, low_ref, high_ref, gain_ref, extras_ref, weights_ref, stats_ref
+):
     me, owner = lax.axis_index("image"), own_fact(extras_ref, 1)
     keys = mine_ref.shape[1]
     first = window_start(extras_ref, owner, total)
@@ -360,7 +379,7 @@
         tiles += [block[0:8, k * HEAD : (k + 1) * HEAD] for k in range(KV_HEADS)]
         match.append(block[8, 0].astype(jnp.int32) == owner)
     query = jnp.concatenate(tiles, axis=0).astype(jnp.bfloat16)
-    key_raw = mine_ref[0] + core_ref[0] + pair_ref[...]
+    key_raw = mine_ref[0] + core_ref[...] + jnp.concatenate([low_ref[...], high_ref[...]], axis=1)
     gain = gain_ref[...]
     parts = []
     for k in range(KV_HEADS):
@@ -503,14 +522,17 @@
         return jnp.concatenate(arrays, axis=0)
 
     step = half + EXTRA
-    key_half, value_half = pl.pallas_call(
+    sent = jax.ShapeDtypeStruct((tokens.shape[0], tokens.shape[1] // 4), tokens.dtype)
+    key_half, value_half, to_pair, to_diagonal = pl.pallas_call(
         functools.partial(prepare_kernel, half),
         out_shape=[
             jax.ShapeDtypeStruct((step, width), key_weight.dtype),
             jax.ShapeDtypeStruct((half, width), value_weight.dtype),
+            sent,
+            sent,
         ],
-        in_specs=whole(8, pl.ANY),
-        out_specs=whole(2),
+        in_specs=whole(9, pl.ANY),
+        out_specs=whole(4),
         scratch_shapes=[
             pltpu.SMEM(text_request.shape, jnp.int32),
             pltpu.SMEM(image_request.shape, jnp.int32),
@@ -519,10 +541,13 @@
             pltpu.SMEM(tenant_page.shape, jnp.int32),
             pltpu.VMEM(queries.shape, queries.dtype),
             pltpu.SemaphoreType.DMA((8,)),
+            pltpu.SemaphoreType.DMA((2, sent.shape[1] // half)),
         ],
-    )(text_request, image_request, image_tiles, request_tenant, tenant_page, queries, key_weight, value_weight)
-
-    to_pair, to_diagonal = send_columns(tokens, half, ((False, True), (True, True)))
+    )(
+        text_request, image_request, image_tiles, request_tenant, tenant_page, queries, key_weight,
+        value_weight, tokens,
+    )
+
     (to_core,) = send_columns(tokens, half, ((True, False),))
     from_pair = swap(to_pair)
     from_diagonal = swap(after(to_diagonal, from_pair), 1)
@@ -540,38 +565,46 @@
     vx2 = across(v2, CORES)
 
     spots = [(d, mirrored) for mirrored in (False, True) for d in (0, 1, 3, 2)]
-    pairs = [lax.rem(z + d, steps) * COLUMNS + (1 - x if mirrored else x) for d, mirrored in spots]
-    cols = jnp.stack([jnp.stack([(p * CORES + core) * 2 + y for p in pairs]), jnp.stack(pairs)])
-
     near = join(key_half[half:], k1[half:], k2[half:], k3[half:], k_own[half:], kx[half:step], kx2[half:], kx[step + half :])
     extras = join(near, across(near, 1))
+    images = [tokens, from_core, from_pair]
+    arrays = [key_half, k_own, k1, k3, k2, kx, kx2]
+    pieces = ((0, 0), (2, 0), (3, 0), (4, 0), (1, 0), (5, 0), (5, step), (6, 0))
+    keys_part = project(images, 0, arrays, pieces, spots, half, steps)
+    keys_core = across(keys_part[1], 1)
+    late = project([from_diagonal], -1, [after(key_half, keys_part)] + arrays[1:], pieces, spots, half, steps)
+    keys_sum = keys_part[2] + across(late[0], 1)
+    middle = width // KV_HEADS
+    keys_pair = [swap(keys_sum[:, :middle]), swap(keys_sum[:, middle:])]
     picked = call(
         functools.partial(pick_kernel, devices, steps, rank),
         jax.ShapeDtypeStruct((devices, rank, rows), down_pages.dtype),
         whole(2),
         scratch=[pltpu.VMEM(down_pages.shape[::-1], down_pages.dtype)],
-    )(extras, down_pages)
-    picked = lax.all_to_all(picked, "image", 0, 0, tiled=True)
+    )(after(extras, keys_sum), down_pages)
+    picked = picked.reshape(devices, 1, rank, rows)
+    order = [0]
+    while picked.shape[0] > 1:
+        bit = picked.shape[0] // 2
+        picked = jnp.concatenate([picked[:bit], across(picked[bit:], bit)], axis=1)
+        order = order + [k ^ bit for k in order]
+    picked = picked.reshape(devices, rank, rows)
     lowrank = call(
-        lowrank_kernel,
+        functools.partial(lowrank_kernel, tuple(order)),
         jax.ShapeDtypeStruct((tokens.shape[0], width), jnp.float32),
         whole(4),
         vmem=16,
         moved=tokens.size * 2,
     )(extras, tokens, picked, up_pages)
 
-    images = [tokens, from_core, from_pair, from_diagonal]
-    pieces = ((0, 0), (2, 0), (3, 0), (4, 0), (1, 0), (5, 0), (5, step), (6, 0))
-    keys_part = project(images, [key_half, k_own, k1, k3, k2, kx, kx2], pieces, after(cols, lowrank), half)
     pieces = ((0, 0), (2, 0), (3, 0), (4, 0), (1, 0), (5, 0), (5, half), (6, 0))
-    values_part = project(
-        images, [value_half, v_own, v1, v3, v2, vx, vx2], pieces, after(cols, keys_part), half
-    )
-
-    keys_core = across(jnp.stack([keys_part[1], keys_part[3]]), 1)
-    keys_pair = swap(keys_part[2] + keys_core[1])
+    near_values = after(value_half, keys_pair[0])
+    images = images + [from_diagonal]
+    values_part = project(images, 0, [near_values, v_own, v1, v3, v2, vx], pieces[:-1], spots, half, steps)
+    values_part = project(images, 0, [after(vx2, keys_pair[1])], ((0, 0),), spots[-1:], half, steps, values_part)
     values_core = across(jnp.stack([values_part[1], values_part[3]]), 1)
-    values_pair = swap(after(values_part[2] + values_core[1], keys_pair))
+    values_sum = (values_part[2] + values_core[1]).astype(jnp.bfloat16)
+    values_pair = swap(values_sum)
 
     heads = WINDOW * 8 * KV_HEADS
     weights, stats = call(
@@ -580,8 +613,8 @@
             jax.ShapeDtypeStruct((heads, tokens.shape[0]), jnp.bfloat16),
             jax.ShapeDtypeStruct((WINDOW, 8, HEAD), jnp.float32),
         ],
-        whole(5),
-    )(keys_part, keys_core, keys_pair, key_gain.reshape(1, HEAD), extras)
+        whole(6),
+    )(keys_part, keys_core, *keys_pair, key_gain.reshape(1, HEAD), extras)
 
     message = jax.ShapeDtypeStruct((steps, MESSAGE, HEAD), jnp.float32)
     messages = call(

time: 227 us -> 123 us (0.54)
  Pallas kernels: 114 us -> 18.9 us
  local copies, waits for them, and re-layouts: 10.9 us -> 2.74 us
  waiting for transfers between devices: 64.6 us -> 72 us
  starting transfers between devices: 31.7 us -> 26.4 us
    pallas_call x2 -> x1, Pallas kernels: 97.7 us -> 2.33 us  [send_columns(): pl.pallas_call(functools.partial(send_kernel, half, targets), out_shape=[...]
    ppermute x13 -> x18, waiting for transfers between devices: 9.96 us -> 23 us  [across(): return lax.ppermute(value, 'image', [(i, i ^ bits) for i in everyone])]
    ppermute x4 -> x5, waiting for transfers between devices: 24.1 us -> 15 us  [swap(): return lax.ppermute(value, ('groups', 'image'), pairs)]
    unnamed x47 -> x23, local copies, waits for them, and re-layouts: 10.6 us -> 2.54 us
    all_to_all x1 -> x0, starting transfers between devices: 4.49 us -> none  [local(): picked = lax.all_to_all(picked, 'image', 0, 0, tiled=True)]
    ppermute x9, waiting for transfers between devices: 30.5 us -> 34 us  [along(): lax.ppermute(value, 'image', [(i, (i - PLANE * d) % devices) for i in eve...]
    ppermute x9, starting transfers between devices: 14.6 us -> 11.2 us  [along(): lax.ppermute(value, 'image', [(i, (i - PLANE * d) % devices) for i in eve...]
    ppermute x4 -> x5, starting transfers between devices: 2.74 us -> 6 us  [swap(): return lax.ppermute(value, ('groups', 'image'), pairs)]
  transfers between devices with their start and end apart: 27 -> 32, of which waited for: 10 -> 18; matrix products, arithmetic and copies ran while one was open for 1% -> 1% of each run, Pallas kernels for 49% -> 11%
where the time goes in v3:
time: 123 us
  waiting for transfers between devices  72 us (59%)
  starting transfers between devices  26.4 us (21%)
  Pallas kernels  18.9 us (15%)
  local copies, waits for them, and re-layouts  2.74 us (2%)
  between operations  2.3 us (2%)
    ppermute x9, waiting for transfers between devices, along(): lax.ppermute(value, 'image', [(i, (i - PLANE * d) % devices) for i in eve...  34 us
    ppermute x18, waiting for transfers between devices, across(): return lax.ppermute(value, 'image', [(i, i ^ bits) for i in everyone])  23 us
    ppermute x5, waiting for transfers between devices, swap(): return lax.ppermute(value, ('groups', 'image'), pairs)  15 us
    ppermute x9, starting transfers between devices, along(): lax.ppermute(value, 'image', [(i, (i - PLANE * d) % devices) for i in eve...  11.2 us
    pallas_call x4, Pallas kernels, project(): call(functools.partial(project_kernel, pieces, spots, number, own, len(ar...  9.17 us
    ppermute x18, starting transfers between devices, across(): return lax.ppermute(value, 'image', [(i, i ^ bits) for i in everyone])  9.12 us
    ppermute x5, starting transfers between devices, swap(): return lax.ppermute(value, ('groups', 'image'), pairs)  6 us
    pallas_call x1, Pallas kernels, local(): pl.pallas_call(functools.partial(prepare_kernel, half), out_shape=[jax.Sh...  3.57 us
  transfers between devices with their start and end apart: 32, of which 18 were waited for; matrix products, arithmetic and copies ran while one was open for 1% of the time, Pallas kernels for 11%

profile of v3, /device:TPU:0, one launch (start us, length us, event | category | flops | bytes accessed | tf_op | source)
XLA Modules:
  0.0 122.7 jit_solution(4889276503729822610)
XLA Ops:
  1.9 3.6 %shard_map.119 = (bf16[272,512]{1,0:T(8,128)(2,1)}, bf16[256,512]{1,0:T(8,128)(2,1)}, bf16[256,2048]{1,0:T(8,128)(2,1)}, bf16[256,2048]{1,0:T(8,128)(2,1)}) custom-call(s32[1]{0:T(128)S(6)} %copy.28.text_ref, s32[1,1]{1,0:T(1,128)S(6)} %copy.29.image_ref, s32[1]{0:T(128)S(6)} %copy.30.tiles_ref, s32[8]{0:T(128)} %tenant_ref.1, s32[16]{0:T(128)} %page_ref.1, ...), custom_call_target="tpu_custom_call" | custom-call | tf_op jit(solution)/shard_map/pallas_call | solution.py:526
  5.5 3.0 %collective-permute-start.1 = (bf16[256,2048]{1,0:T(8,128)(2,1)}, bf16[256,2048]{1,0:T(8,128)(2,1)S(1)}, u32[]{:S(2)}, u32[]{:S(2)}) collective-permute-start(bf16[256,2048]{1,0:T(8,128)(2,1)} %get-tuple-element.31), channel_id=1, source_target_pairs={{0,16},{1,17},{2,18},{3,19},{4,20},{5,21},{6,22},{7,23},{8,24},{9,... | collective-permute-start | bytes 3145736 | tf_op jit(solution)/shard_map/ppermute | solution.py:519
  8.6 1.5 %collective-permute-start.5 = (bf16[272,512]{1,0:T(8,128)(2,1)}, bf16[272,512]{1,0:T(8,128)(2,1)S(1)}, u32[]{:S(2)}, u32[]{:S(2)}) collective-permute-start(bf16[272,512]{1,0:T(8,128)(2,1)} %get-tuple-element.41.refs_3_.refs_1_), channel_id=1, source_target_pairs={{0,2},{1,3},{2,0},{3,1},{4,6},{5,7},{6,4},{7,5},{8,10},{9,11},{10,... | collective-permute-start | bytes 835592 | tf_op jit(solution)/shard_map/ppermute | solution.py:512
  10.1 3.6 %collective-permute-start.3 = (bf16[272,512]{1,0:T(8,128)(2,1)}, bf16[272,512]{1,0:T(8,128)(2,1)S(1)}, u32[]{:S(2)}, u32[]{:S(2)}) collective-permute-start(bf16[272,512]{1,0:T(8,128)(2,1)} %get-tuple-element.41.refs_3_.refs_1_), channel_id=1, source_target_pairs={{0,12},{1,13},{2,14},{3,15},{4,0},{5,1},{6,2},{7,3},{8,4},{9,5},{1... | collective-permute-start | bytes 835592 | tf_op jit(solution)/shard_map/ppermute | solution.py:515
  13.7 2.3 %shard_map.118 = bf16[256,2048]{1,0:T(8,128)(2,1)} custom-call(bf16[256,8192]{1,0:T(8,128)(2,1)} %bitcast.18), custom_call_target="tpu_custom_call" | custom-call | bytes 2097152 | tf_op jit(solution)/shard_map/pallas_call | solution.py:200
  16.1 0.8 collective-permute-done.5.refs_4_.refs_2_
  16.9 4.2 %collective-permute-done.3.refs_5_.refs_3_ = bf16[272,512]{1,0:T(8,128)(2,1)S(1)} collective-permute-done((bf16[272,512]{1,0:T(8,128)(2,1)}, bf16[272,512]{1,0:T(8,128)(2,1)S(1)}, u32[]{:S(2)}, u32[]{:S(2)}) %collective-permute-start.3) | collective-permute-done | bytes 278560 | tf_op jit(solution)/shard_map/ppermute | solution.py:515
  21.1 5.0 %collective-permute-done.4.refs_6_.refs_4_ = bf16[272,512]{1,0:T(8,128)(2,1)S(1)} collective-permute-done((bf16[272,512]{1,0:T(8,128)(2,1)}, bf16[272,512]{1,0:T(8,128)(2,1)S(1)}, u32[]{:S(2)}, u32[]{:S(2)}) %collective-permute-start.4) | collective-permute-done | bytes 278560 | tf_op jit(solution)/shard_map/ppermute | solution.py:515
  26.1 0.7 collective-permute-start.6
  26.9 0.6 collective-permute-start.7
  27.5 4.5 %collective-permute-done.1.refs_2_ = bf16[256,2048]{1,0:T(8,128)(2,1)S(1)} collective-permute-done((bf16[256,2048]{1,0:T(8,128)(2,1)}, bf16[256,2048]{1,0:T(8,128)(2,1)S(1)}, u32[]{:S(2)}, u32[]{:S(2)}) %collective-permute-start.1) | collective-permute-done | bytes 1048608 | tf_op jit(solution)/shard_map/ppermute | solution.py:519
  32.2 7.6 %collective-permute-done.6.refs_7_.refs_5_ = bf16[272,512]{1,0:T(8,128)(2,1)S(1)} collective-permute-done((bf16[272,512]{1,0:T(8,128)(2,1)S(1)}, bf16[272,512]{1,0:T(8,128)(2,1)S(1)}, u32[]{:S(2)}, u32[]{:S(2)}) %collective-permute-start.6) | collective-permute-done | bytes 278560 | tf_op jit(solution)/shard_map/ppermute | solution.py:515
  39.9 2.9 %collective-permute-start.8 = (bf16[256,512]{1,0:T(8,128)(2,1)S(1)}, bf16[256,512]{1,0:T(8,128)(2,1)S(1)}, u32[]{:S(2)}, u32[]{:S(2)}) collective-permute-start(bf16[256,512]{1,0:T(8,128)(2,1)S(1)} %copy-done.4), channel_id=1, source_target_pairs={{0,12},{1,13},{2,14},{3,15},{4,0},{5,1},{6,2},{7,3},{8,4},{9,5},{1... | collective-permute-start | bytes 786440 | tf_op jit(solution)/shard_map/ppermute | solution.py:515
  42.8 0.5 collective-permute-start.12
  43.4 6.2 %collective-permute-done.8.refs_6_ = bf16[256,512]{1,0:T(8,128)(2,1)S(1)} collective-permute-done((bf16[256,512]{1,0:T(8,128)(2,1)S(1)}, bf16[256,512]{1,0:T(8,128)(2,1)S(1)}, u32[]{:S(2)}, u32[]{:S(2)}) %collective-permute-start.8) | collective-permute-done | bytes 262176 | tf_op jit(solution)/shard_map/ppermute | solution.py:515
  49.6 0.5 collective-permute-start.16
  50.1 3.9 %collective-permute-done.9.refs_7_ = bf16[256,512]{1,0:T(8,128)(2,1)S(1)} collective-permute-done((bf16[256,512]{1,0:T(8,128)(2,1)S(1)}, bf16[256,512]{1,0:T(8,128)(2,1)S(1)}, u32[]{:S(2)}, u32[]{:S(2)}) %collective-permute-start.9) | collective-permute-done | bytes 262176 | tf_op jit(solution)/shard_map/ppermute | solution.py:515
  54.1 2.2 %copy-done = bf16[1,256,8192]{2,1,0:T(8,128)(2,1)S(1)} copy-done((bf16[1,256,8192]{2,1,0:T(8,128)(2,1)S(1)}, bf16[1,256,8192]{2,1,0:T(8,128)(2,1)}, u32[]{:S(2)}) %copy-start) | copy-done | bytes 4194328
  56.3 3.1 %shard_map.120.mine_ref = f32[3,256,512]{2,1,0:T(8,128)S(1)} custom-call(bf16[256,8192]{1,0:T(8,128)(2,1)S(1)} %bitcast.19, bf16[256,2048]{1,0:T(8,128)(2,1)S(1)} %collective-permute-done.refs_1_, bf16[256,2048]{1,0:T(8,128)(2,1)S(1)} %collective-permute-done.1.refs_2_, bf16[272,512]{1,0:T(8,128)(2,1)S(1)} %copy-done.2, ...), custom_call_target="tpu_custom_call" | custom-call | flops 1610612736 | bytes 5242880 | tf_op jit(solution)/shard_map/pallas_call | solution.py:297
  59.5 1.2 shard_map.121
  60.8 0.6 collective-permute-start.17
  61.4 4.7 %collective-permute-done.10.refs_8_ = bf16[256,512]{1,0:T(8,128)(2,1)S(1)} collective-permute-done((bf16[256,512]{1,0:T(8,128)(2,1)S(1)}, bf16[256,512]{1,0:T(8,128)(2,1)S(1)}, u32[]{:S(2)}, u32[]{:S(2)}) %collective-permute-start.10) | collective-permute-done | bytes 262176 | tf_op jit(solution)/shard_map/ppermute | solution.py:515
  66.1 0.5 collective-permute-start.11
  66.8 0.6 collective-permute-start.14
  67.4 1.5 %collective-permute-start.15 = (f32[256,128]{1,0:T(8,128)S(1)}, f32[256,128]{1,0:T(8,128)S(1)}, u32[]{:S(2)}, u32[]{:S(2)}) collective-permute-start(f32[256,128]{1,0:T(8,128)S(1)} %slice.106), channel_id=1, source_target_pairs={{0,16},{1,17},{2,18},{3,19},{4,20},{5,21},{6,22},{7,23},{8,24},{9,... | collective-permute-start | bytes 393224 | tf_op jit(solution)/shard_map/ppermute | solution.py:519
  68.9 10.2 %collective-permute-done.15.low_ref = f32[256,128]{1,0:T(8,128)S(1)} collective-permute-done((f32[256,128]{1,0:T(8,128)S(1)}, f32[256,128]{1,0:T(8,128)S(1)}, u32[]{:S(2)}, u32[]{:S(2)}) %collective-permute-start.15) | collective-permute-done | bytes 131104 | tf_op jit(solution)/shard_map/ppermute | solution.py:519
  79.1 3.7 %shard_map.122.refs_5_ = f32[4,256,512]{2,1,0:T(8,128)S(1)} custom-call(bf16[256,8192]{1,0:T(8,128)(2,1)S(1)} %bitcast.20, bf16[256,2048]{1,0:T(8,128)(2,1)S(1)} %collective-permute-done.refs_1_, bf16[256,2048]{1,0:T(8,128)(2,1)S(1)} %collective-permute-done.1.refs_2_, bf16[256,2048]{1,0:T(8,128)(2,1)S(1)} %collective-permute-done.2.refs_0_.refs_3_, ...), custom_call_target="tpu_custom_call" | custom-call | flops 1879048192 | bytes 5505024 | tf_op jit(solution)/shard_map/pallas_call | solution.py:297
  82.8 1.1 shard_map.123.mine_ref
  84.1 0.5 collective-permute-start.18
  85.4 0.9 collective-permute-start.21
  86.3 8.8 %collective-permute-done.21 = bf16[8,1,16,512]{3,2,1,0:T(8,128)(2,1)S(1)} collective-permute-done((bf16[8,1,16,512]{3,2,1,0:T(8,128)(2,1)S(1)}, bf16[8,1,16,512]{3,2,1,0:T(8,128)(2,1)S(1)}, u32[]{:S(2)}, u32[]{:S(2)}) %collective-permute-start.21) | collective-permute-done | bytes 131104 | tf_op jit(solution)/shard_map/ppermute | solution.py:512
  95.3 5.2 %collective-permute-done.22 = bf16[4,2,16,512]{3,2,1,0:T(8,128)(2,1)S(1)} collective-permute-done((bf16[4,2,16,512]{3,2,1,0:T(8,128)(2,1)S(1)}, bf16[4,2,16,512]{3,2,1,0:T(8,128)(2,1)S(1)}, u32[]{:S(2)}, u32[]{:S(2)}) %collective-permute-start.22) | collective-permute-done | bytes 131104 | tf_op jit(solution)/shard_map/ppermute | solution.py:512
  100.5 1.1 collective-permute-start.23
  101.7 0.6 collective-permute-start.19
  102.3 3.3 %collective-permute-done.23 = bf16[2,4,16,512]{3,2,1,0:T(8,128)(2,1)S(1)} collective-permute-done((bf16[2,4,16,512]{3,2,1,0:T(8,128)(2,1)S(1)}, bf16[2,4,16,512]{3,2,1,0:T(8,128)(2,1)S(1)}, u32[]{:S(2)}, u32[]{:S(2)}) %collective-permute-start.23) | collective-permute-done | bytes 131104 | tf_op jit(solution)/shard_map/ppermute | solution.py:512
  105.7 0.7 shard_map.126
  106.4 0.6 collective-permute-done.24
  107.0 1.5 %shard_map.125.lowrank_ref = f32[256,512]{1,0:T(8,128)S(1)} custom-call(bf16[256,512]{1,0:T(8,128)(2,1)S(1)} %constant_dynamic-update-slice_fusion.8.extras_ref, bf16[256,8192]{1,0:T(8,128)(2,1)S(1)} %bitcast.22, bf16[16,16,512]{2,1,0:T(8,128)(2,1)S(1)} %maximum_bitcast_fusion.down_ref, bf16[16,16,512]{2,1,0:T(8,128)(2,1)S(1)} %copy-done.5), custom_call_target="tpu_custom_call" | custom-call | bytes 4194304 | tf_op jit(solution)/shard_map/pallas_call | solution.py:592
  109.4 0.9 collective-permute-start.27
  110.3 1.0 collective-permute-start.28
  111.3 3.4 %collective-permute-done.27.refs_2_ = f32[4,40,128]{2,1,0:T(8,128)S(1)} collective-permute-done((f32[4,40,128]{2,1,0:T(8,128)S(1)}, f32[4,40,128]{2,1,0:T(8,128)S(1)}, u32[]{:S(2)}, u32[]{:S(2)}) %collective-permute-start.27) | collective-permute-done | bytes 81952 | tf_op jit(solution)/shard_map/ppermute | solution.py:512
  114.7 0.8 collective-permute-done.28.refs_3_
  115.7 0.7 collective-permute-start.29
  116.4 1.8 %collective-permute-start.30 = (f32[40,128]{1,0:T(8,128)S(1)}, f32[40,128]{1,0:T(8,128)S(1)}, u32[]{:S(2)}, u32[]{:S(2)}) collective-permute-start(f32[40,128]{1,0:T(8,128)S(1)} %get-tuple-element.55), channel_id=1, source_target_pairs={{0,8},{1,9},{2,10},{3,11},{4,12},{5,13},{6,14},{7,15},{8,0},{9,1},... | collective-permute-start | bytes 61448 | tf_op jit(solution)/shard_map/ppermute | solution.py:515
  118.1 1.5 %collective-permute-start.31 = (f32[40,128]{1,0:T(8,128)S(1)}, f32[40,128]{1,0:T(8,128)S(1)}, u32[]{:S(2)}, u32[]{:S(2)}) collective-permute-start(f32[40,128]{1,0:T(8,128)S(1)} %get-tuple-element.56), channel_id=1, source_target_pairs={{0,12},{1,13},{2,14},{3,15},{4,0},{5,1},{6,2},{7,3},{8,4},{9,5},{1... | collective-permute-start | bytes 61448 | tf_op jit(solution)/shard_map/ppermute | solution.py:515
  119.6 1.9 %collective-permute-done.29.refs_1_ = f32[40,128]{1,0:T(8,128)S(1)} collective-permute-done((f32[40,128]{1,0:T(8,128)S(1)}, f32[40,128]{1,0:T(8,128)S(1)}, u32[]{:S(2)}, u32[]{:S(2)}) %collective-permute-start.29) | collective-permute-done | bytes 20512 | tf_op jit(solution)/shard_map/ppermute | solution.py:515
  121.5 0.4 collective-permute-done.31.refs_3_
  121.9 0.7 shard_map.129
  (67 shorter events, 3.2 us)
Async XLA Ops:
  5.5 26.4 %collective-permute-start.1 = (bf16[256,2048]{1,0:T(8,128)(2,1)}, bf16[256,2048]{1,0:T(8,128)(2,1)S(1)}, u32[]{:S(2)}, u32[]{:S(2)}) collective-permute-start(bf16[256,2048]{1,0:T(8,128)(2,1)} %get-tuple-element.31), channel_id=1, source_target_pairs={{0,16},{1,17},{2,18},{3,19},{4,20},{5,21},{6,22},{7,23},{8,24},{9,... | collective-permute-start | bytes 3145736 | tf_op jit(solution)/shard_map/ppermute | solution.py:519
  8.6 7.5 %copy-start.2 = (bf16[272,512]{1,0:T(8,128)(2,1)S(1)}, bf16[272,512]{1,0:T(8,128)(2,1)}, u32[]{:S(2)}) copy-start(bf16[272,512]{1,0:T(8,128)(2,1)} %get-tuple-element.41.refs_3_.refs_1_) | copy-start | bytes 835588
  8.6 31.3 %copy-start.4 = (bf16[256,512]{1,0:T(8,128)(2,1)S(1)}, bf16[256,512]{1,0:T(8,128)(2,1)}, u32[]{:S(2)}) copy-start(bf16[256,512]{1,0:T(8,128)(2,1)} %get-tuple-element.44.refs_4_) | copy-start | bytes 786436
  8.6 8.3 %collective-permute-start.5 = (bf16[272,512]{1,0:T(8,128)(2,1)}, bf16[272,512]{1,0:T(8,128)(2,1)S(1)}, u32[]{:S(2)}, u32[]{:S(2)}) collective-permute-start(bf16[272,512]{1,0:T(8,128)(2,1)} %get-tuple-element.41.refs_3_.refs_1_), channel_id=1, source_target_pairs={{0,2},{1,3},{2,0},{3,1},{4,6},{5,7},{6,4},{7,5},{8,10},{9,11},{10,... | collective-permute-start | bytes 835592 | tf_op jit(solution)/shard_map/ppermute | solution.py:512
  10.1 11.0 %collective-permute-start.3 = (bf16[272,512]{1,0:T(8,128)(2,1)}, bf16[272,512]{1,0:T(8,128)(2,1)S(1)}, u32[]{:S(2)}, u32[]{:S(2)}) collective-permute-start(bf16[272,512]{1,0:T(8,128)(2,1)} %get-tuple-element.41.refs_3_.refs_1_), channel_id=1, source_target_pairs={{0,12},{1,13},{2,14},{3,15},{4,0},{5,1},{6,2},{7,3},{8,4},{9,5},{1... | collective-permute-start | bytes 835592 | tf_op jit(solution)/shard_map/ppermute | solution.py:515
  13.7 12.4 %collective-permute-start.4 = (bf16[272,512]{1,0:T(8,128)(2,1)}, bf16[272,512]{1,0:T(8,128)(2,1)S(1)}, u32[]{:S(2)}, u32[]{:S(2)}) collective-permute-start(bf16[272,512]{1,0:T(8,128)(2,1)} %get-tuple-element.41.refs_3_.refs_1_), channel_id=1, source_target_pairs={{0,4},{1,5},{2,6},{3,7},{4,8},{5,9},{6,10},{7,11},{8,12},{9,13},{1... | collective-permute-start | bytes 835592 | tf_op jit(solution)/shard_map/ppermute | solution.py:515
  16.0 38.1 %collective-permute-start = (bf16[256,2048]{1,0:T(8,128)(2,1)}, bf16[256,2048]{1,0:T(8,128)(2,1)S(1)}, u32[]{:S(2)}, u32[]{:S(2)}) collective-permute-start(bf16[256,2048]{1,0:T(8,128)(2,1)} %shard_map.118), channel_id=1, source_target_pairs={{0,1},{1,0},{2,3},{3,2},{4,5},{5,4},{6,7},{7,6},{8,9},{9,8},{10,11... | collective-permute-start | bytes 3145736 | tf_op jit(solution)/shard_map/ppermute | solution.py:512
  26.1 13.8 %collective-permute-start.6 = (bf16[272,512]{1,0:T(8,128)(2,1)S(1)}, bf16[272,512]{1,0:T(8,128)(2,1)S(1)}, u32[]{:S(2)}, u32[]{:S(2)}) collective-permute-start(bf16[272,512]{1,0:T(8,128)(2,1)S(1)} %copy-done.2), channel_id=1, source_target_pairs={{0,8},{1,9},{2,10},{3,11},{4,12},{5,13},{6,14},{7,15},{8,0},{9,1},... | collective-permute-start | bytes 835592 | tf_op jit(solution)/shard_map/ppermute | solution.py:515
  26.9 13.0 %collective-permute-start.7 = (bf16[544,512]{1,0:T(8,128)(2,1)S(1)}, bf16[544,512]{1,0:T(8,128)(2,1)S(1)}, u32[]{:S(2)}, u32[]{:S(2)}) collective-permute-start(bf16[544,512]{1,0:T(8,128)(2,1)S(1)} %pad_maximum_fusion.1), channel_id=1, source_target_pairs={{0,2},{1,3},{2,0},{3,1},{4,6},{5,7},{6,4},{7,5},{8,10},{9,11},{10,... | collective-permute-start | bytes 1671176 | tf_op jit(solution)/shard_map/ppermute | solution.py:512
  31.9 27.5 %collective-permute-start.2 = (bf16[256,2048]{1,0:T(8,128)(2,1)}, bf16[256,2048]{1,0:T(8,128)(2,1)S(1)}, u32[]{:S(2)}, u32[]{:S(2)}) collective-permute-start(bf16[256,2048]{1,0:T(8,128)(2,1)} %get-tuple-element.33), channel_id=1, source_target_pairs={{0,17},{1,16},{2,19},{3,18},{4,21},{5,20},{6,23},{7,22},{8,25},{9,... | collective-permute-start | bytes 3145736 | tf_op jit(solution)/shard_map/ppermute | solution.py:519
  39.9 9.7 %collective-permute-start.8 = (bf16[256,512]{1,0:T(8,128)(2,1)S(1)}, bf16[256,512]{1,0:T(8,128)(2,1)S(1)}, u32[]{:S(2)}, u32[]{:S(2)}) collective-permute-start(bf16[256,512]{1,0:T(8,128)(2,1)S(1)} %copy-done.4), channel_id=1, source_target_pairs={{0,12},{1,13},{2,14},{3,15},{4,0},{5,1},{6,2},{7,3},{8,4},{9,5},{1... | collective-permute-start | bytes 786440 | tf_op jit(solution)/shard_map/ppermute | solution.py:515
  42.8 11.2 %collective-permute-start.9 = (bf16[256,512]{1,0:T(8,128)(2,1)S(1)}, bf16[256,512]{1,0:T(8,128)(2,1)S(1)}, u32[]{:S(2)}, u32[]{:S(2)}) collective-permute-start(bf16[256,512]{1,0:T(8,128)(2,1)S(1)} %copy-done.4), channel_id=1, source_target_pairs={{0,4},{1,5},{2,6},{3,7},{4,8},{5,9},{6,10},{7,11},{8,12},{9,13},{1... | collective-permute-start | bytes 786440 | tf_op jit(solution)/shard_map/ppermute | solution.py:515
  42.8 11.3 %collective-permute-start.12 = (bf16[272,512]{1,0:T(8,128)(2,1)S(1)}, bf16[272,512]{1,0:T(8,128)(2,1)S(1)}, u32[]{:S(2)}, u32[]{:S(2)}) collective-permute-start(bf16[272,512]{1,0:T(8,128)(2,1)S(1)} %collective-permute-done.6.refs_7_.refs_5_), channel_id=1, source_target_pairs={{0,2},{1,3},{2,0},{3,1},{4,6},{5,7},{6,4},{7,5},{8,10},{9,11},{10,... | collective-permute-start | bytes 835592 | tf_op jit(solution)/shard_map/ppermute | solution.py:512
  49.6 29.4 %collective-permute-start.16 = (bf16[256,512]{1,0:T(8,128)(2,1)S(1)}, bf16[256,512]{1,0:T(8,128)(2,1)S(1)}, u32[]{:S(2)}, u32[]{:S(2)}) collective-permute-start(bf16[256,512]{1,0:T(8,128)(2,1)S(1)} %copy-done.4), channel_id=1, source_target_pairs={{0,2},{1,3},{2,0},{3,1},{4,6},{5,7},{6,4},{7,5},{8,10},{9,11},{10,... | collective-permute-start | bytes 786440 | tf_op jit(solution)/shard_map/ppermute | solution.py:512
  54.0 12.1 %collective-permute-start.10 = (bf16[256,512]{1,0:T(8,128)(2,1)S(1)}, bf16[256,512]{1,0:T(8,128)(2,1)S(1)}, u32[]{:S(2)}, u32[]{:S(2)}) collective-permute-start(bf16[256,512]{1,0:T(8,128)(2,1)S(1)} %copy-done.4), channel_id=1, source_target_pairs={{0,8},{1,9},{2,10},{3,11},{4,12},{5,13},{6,14},{7,15},{8,0},{9,1},... | collective-permute-start | bytes 786440 | tf_op jit(solution)/shard_map/ppermute | solution.py:515
  54.1 2.2 %copy-start = (bf16[1,256,8192]{2,1,0:T(8,128)(2,1)S(1)}, bf16[1,256,8192]{2,1,0:T(8,128)(2,1)}, u32[]{:S(2)}) copy-start(bf16[1,256,8192]{2,1,0:T(8,128)(2,1)} %param.12) | copy-start | bytes 12582916
  59.4 19.6 %copy-start.1 = (bf16[1,256,8192]{2,1,0:T(8,128)(2,1)S(1)}, bf16[1,256,8192]{2,1,0:T(8,128)(2,1)}, u32[]{:S(2)}) copy-start(bf16[1,256,8192]{2,1,0:T(8,128)(2,1)} %param.12) | copy-start | bytes 12582916
  60.7 6.0 %collective-permute-start.13 = (f32[256,512]{1,0:T(8,128)S(1)}, f32[256,512]{1,0:T(8,128)S(1)}, u32[]{:S(2)}, u32[]{:S(2)}) collective-permute-start(f32[256,512]{1,0:T(8,128)S(1)} %bitcast.23), channel_id=1, source_target_pairs={{0,1},{1,0},{2,3},{3,2},{4,5},{5,4},{6,7},{7,6},{8,9},{9,8},{10,11... | collective-permute-start | bytes 1572872 | tf_op jit(solution)/shard_map/ppermute | solution.py:512
  60.8 18.3 %collective-permute-start.17 = (bf16[512,512]{1,0:T(8,128)(2,1)S(1)}, bf16[512,512]{1,0:T(8,128)(2,1)S(1)}, u32[]{:S(2)}, u32[]{:S(2)}) collective-permute-start(bf16[512,512]{1,0:T(8,128)(2,1)S(1)} %pad_maximum_fusion.2), channel_id=1, source_target_pairs={{0,2},{1,3},{2,0},{3,1},{4,6},{5,7},{6,4},{7,5},{8,10},{9,11},{10,... | collective-permute-start | bytes 1572872 | tf_op jit(solution)/shard_map/ppermute | solution.py:512
  66.1 16.7 %collective-permute-start.11 = (bf16[256,512]{1,0:T(8,128)(2,1)S(1)}, bf16[256,512]{1,0:T(8,128)(2,1)S(1)}, u32[]{:S(2)}, u32[]{:S(2)}) collective-permute-start(bf16[256,512]{1,0:T(8,128)(2,1)S(1)} %collective-permute-done.10.refs_8_), channel_id=1, source_target_pairs={{0,2},{1,3},{2,0},{3,1},{4,6},{5,7},{6,4},{7,5},{8,10},{9,11},{10,... | collective-permute-start | bytes 786440 | tf_op jit(solution)/shard_map/ppermute | solution.py:512
  66.8 16.0 %collective-permute-start.14 = (f32[256,384]{1,0:T(8,128)S(1)}, f32[256,384]{1,0:T(8,128)S(1)}, u32[]{:S(2)}, u32[]{:S(2)}) collective-permute-start(f32[256,384]{1,0:T(8,128)S(1)} %slice.105), channel_id=1, source_target_pairs={{0,16},{1,17},{2,18},{3,19},{4,20},{5,21},{6,22},{7,23},{8,24},{9,... | collective-permute-start | bytes 1179656 | tf_op jit(solution)/shard_map/ppermute | solution.py:519
  67.4 11.7 %collective-permute-start.15 = (f32[256,128]{1,0:T(8,128)S(1)}, f32[256,128]{1,0:T(8,128)S(1)}, u32[]{:S(2)}, u32[]{:S(2)}) collective-permute-start(f32[256,128]{1,0:T(8,128)S(1)} %slice.106), channel_id=1, source_target_pairs={{0,16},{1,17},{2,18},{3,19},{4,20},{5,21},{6,22},{7,23},{8,24},{9,... | collective-permute-start | bytes 393224 | tf_op jit(solution)/shard_map/ppermute | solution.py:519
  79.0 5.6 %collective-permute-start.20 = (bf16[128,512]{1,0:T(8,128)(2,1)S(1)}, bf16[128,512]{1,0:T(8,128)(2,1)S(1)}, u32[]{:S(2)}, u32[]{:S(2)}) collective-permute-start(bf16[128,512]{1,0:T(8,128)(2,1)S(1)} %get-tuple-element.59), channel_id=1, source_target_pairs={{0,1},{1,0},{2,3},{3,2},{4,5},{5,4},{6,7},{7,6},{8,9},{9,8},{10,11... | collective-permute-start | bytes 393224 | tf_op jit(solution)/shard_map/ppermute | solution.py:512
  84.0 1.0 copy-start.3
  84.1 17.5 %collective-permute-start.18 = (f32[2,256,512]{2,1,0:T(8,128)S(1)}, f32[2,256,512]{2,1,0:T(8,128)S(1)}, u32[]{:S(2)}, u32[]{:S(2)}) collective-permute-start(f32[2,256,512]{2,1,0:T(8,128)S(1)} %pad_maximum_fusion), channel_id=1, source_target_pairs={{0,1},{1,0},{2,3},{3,2},{4,5},{5,4},{6,7},{7,6},{8,9},{9,8},{10,11... | collective-permute-start | bytes 3145736 | tf_op jit(solution)/shard_map/ppermute | solution.py:512
  85.4 9.7 %collective-permute-start.21 = (bf16[8,1,16,512]{3,2,1,0:T(8,128)(2,1)S(1)}, bf16[8,1,16,512]{3,2,1,0:T(8,128)(2,1)S(1)}, u32[]{:S(2)}, u32[]{:S(2)}) collective-permute-start(bf16[8,1,16,512]{3,2,1,0:T(8,128)(2,1)S(1)} %get-tuple-element.78), channel_id=1, source_target_pairs={{0,8},{1,9},{2,10},{3,11},{4,12},{5,13},{6,14},{7,15},{8,0},{9,1},... | collective-permute-start | bytes 393224 | tf_op jit(solution)/shard_map/ppermute | solution.py:512
  95.1 10.6 %copy-start.6 = (f32[128]{0:T(128)S(1)}, f32[128]{0:T(128)}, u32[]{:S(2)}) copy-start(f32[128]{0:T(128)} %param.17) | copy-start | bytes 1540
  95.1 5.4 %collective-permute-start.22 = (bf16[4,2,16,512]{3,2,1,0:T(8,128)(2,1)S(1)}, bf16[4,2,16,512]{3,2,1,0:T(8,128)(2,1)S(1)}, u32[]{:S(2)}, u32[]{:S(2)}) collective-permute-start(bf16[4,2,16,512]{3,2,1,0:T(8,128)(2,1)S(1)} %get-tuple-element.76), channel_id=1, source_target_pairs={{0,4},{1,5},{2,6},{3,7},{4,0},{5,1},{6,2},{7,3},{8,12},{9,13},{10,... | collective-permute-start | bytes 393224 | tf_op jit(solution)/shard_map/ppermute | solution.py:512
  95.2 10.5 %collective-permute-start.25 = (f32[256,512]{1,0:T(8,128)S(1)}, f32[256,512]{1,0:T(8,128)S(1)}, u32[]{:S(2)}, u32[]{:S(2)}) collective-permute-start(f32[256,512]{1,0:T(8,128)S(1)} %slice_bitcast_fusion), channel_id=1, source_target_pairs={{0,1},{1,0},{2,3},{3,2},{4,5},{5,4},{6,7},{7,6},{8,9},{9,8},{10,11... | collective-permute-start | bytes 1572872 | tf_op jit(solution)/shard_map/ppermute | solution.py:512
  100.5 5.0 %collective-permute-start.23 = (bf16[2,4,16,512]{3,2,1,0:T(8,128)(2,1)S(1)}, bf16[2,4,16,512]{3,2,1,0:T(8,128)(2,1)S(1)}, u32[]{:S(2)}, u32[]{:S(2)}) collective-permute-start(bf16[2,4,16,512]{3,2,1,0:T(8,128)(2,1)S(1)} %get-tuple-element.74), channel_id=1, source_target_pairs={{0,2},{1,3},{2,0},{3,1},{4,6},{5,7},{6,4},{7,5},{8,10},{9,11},{10,... | collective-permute-start | bytes 393224 | tf_op jit(solution)/shard_map/ppermute | solution.py:512
  101.7 7.2 %collective-permute-start.19 = (bf16[256,512]{1,0:T(8,128)(2,1)S(1)}, bf16[256,512]{1,0:T(8,128)(2,1)S(1)}, u32[]{:S(2)}, u32[]{:S(2)}) collective-permute-start(bf16[256,512]{1,0:T(8,128)(2,1)S(1)} %fusion.2), channel_id=1, source_target_pairs={{0,16},{1,17},{2,18},{3,19},{4,20},{5,21},{6,22},{7,23},{8,24},{9,... | collective-permute-start | bytes 786440 | tf_op jit(solution)/shard_map/ppermute | solution.py:519
  105.6 1.4 %collective-permute-start.24 = (bf16[1,8,16,512]{3,2,1,0:T(8,128)(2,1)S(1)}, bf16[1,8,16,512]{3,2,1,0:T(8,128)(2,1)S(1)}, u32[]{:S(2)}, u32[]{:S(2)}) collective-permute-start(bf16[1,8,16,512]{3,2,1,0:T(8,128)(2,1)S(1)} %get-tuple-element.72), channel_id=1, source_target_pairs={{0,1},{1,0},{2,3},{3,2},{4,5},{5,4},{6,7},{7,6},{8,9},{9,8},{10,11... | collective-permute-start | bytes 393224 | tf_op jit(solution)/shard_map/ppermute | solution.py:512
  105.7 1.3 %copy-start.5 = (bf16[16,16,512]{2,1,0:T(8,128)(2,1)S(1)}, bf16[16,16,512]{2,1,0:T(8,128)(2,1)}, u32[]{:S(2)}) copy-start(bf16[16,16,512]{2,1,0:T(8,128)(2,1)} %up_ref.1) | copy-start | bytes 786436
  109.3 1.9 %collective-permute-start.26 = (f32[4,40,128]{2,1,0:T(8,128)S(1)}, f32[4,40,128]{2,1,0:T(8,128)S(1)}, u32[]{:S(2)}, u32[]{:S(2)}) collective-permute-start(f32[4,40,128]{2,1,0:T(8,128)S(1)} %get-tuple-element.50), channel_id=1, source_target_pairs={{0,1},{1,0},{2,3},{3,2},{4,5},{5,4},{6,7},{7,6},{8,9},{9,8},{10,11... | collective-permute-start | bytes 245768 | tf_op jit(solution)/shard_map/ppermute | solution.py:512
  109.4 5.3 %collective-permute-start.27 = (f32[4,40,128]{2,1,0:T(8,128)S(1)}, f32[4,40,128]{2,1,0:T(8,128)S(1)}, u32[]{:S(2)}, u32[]{:S(2)}) collective-permute-start(f32[4,40,128]{2,1,0:T(8,128)S(1)} %get-tuple-element.51), channel_id=1, source_target_pairs={{0,2},{1,3},{2,0},{3,1},{4,6},{5,7},{6,4},{7,5},{8,10},{9,11},{10,... | collective-permute-start | bytes 245768 | tf_op jit(solution)/shard_map/ppermute | solution.py:512
  110.3 5.2 %collective-permute-start.28 = (f32[4,40,128]{2,1,0:T(8,128)S(1)}, f32[4,40,128]{2,1,0:T(8,128)S(1)}, u32[]{:S(2)}, u32[]{:S(2)}) collective-permute-start(f32[4,40,128]{2,1,0:T(8,128)S(1)} %get-tuple-element.52), channel_id=1, source_target_pairs={{0,3},{1,2},{2,1},{3,0},{4,7},{5,6},{6,5},{7,4},{8,11},{9,10},{10,... | collective-permute-start | bytes 245768 | tf_op jit(solution)/shard_map/ppermute | solution.py:512
  115.7 5.8 %collective-permute-start.29 = (f32[40,128]{1,0:T(8,128)S(1)}, f32[40,128]{1,0:T(8,128)S(1)}, u32[]{:S(2)}, u32[]{:S(2)}) collective-permute-start(f32[40,128]{1,0:T(8,128)S(1)} %get-tuple-element.54), channel_id=1, source_target_pairs={{0,4},{1,5},{2,6},{3,7},{4,8},{5,9},{6,10},{7,11},{8,12},{9,13},{1... | collective-permute-start | bytes 61448 | tf_op jit(solution)/shard_map/ppermute | solution.py:515
  116.4 5.1 %collective-permute-start.30 = (f32[40,128]{1,0:T(8,128)S(1)}, f32[40,128]{1,0:T(8,128)S(1)}, u32[]{:S(2)}, u32[]{:S(2)}) collective-permute-start(f32[40,128]{1,0:T(8,128)S(1)} %get-tuple-element.55), channel_id=1, source_target_pairs={{0,8},{1,9},{2,10},{3,11},{4,12},{5,13},{6,14},{7,15},{8,0},{9,1},... | collective-permute-start | bytes 61448 | tf_op jit(solution)/shard_map/ppermute | solution.py:515
  118.1 3.8 %collective-permute-start.31 = (f32[40,128]{1,0:T(8,128)S(1)}, f32[40,128]{1,0:T(8,128)S(1)}, u32[]{:S(2)}, u32[]{:S(2)}) collective-permute-start(f32[40,128]{1,0:T(8,128)S(1)} %get-tuple-element.56), channel_id=1, source_target_pairs={{0,12},{1,13},{2,14},{3,15},{4,0},{5,1},{6,2},{7,3},{8,4},{9,5},{1... | collective-permute-start | bytes 61448 | tf_op jit(solution)/shard_map/ppermute | solution.py:515

commit v4 on v3

--- a/solution.py
+++ b/solution.py
@@ -366,7 +366,7 @@
 
 
 def score_kernel(
-    total, steps, mine_ref, core_ref, low_ref, high_ref, gain_ref, extras_ref, weights_ref, stats_ref
+    total, steps, mine_ref, core_ref, pair_ref, gain_ref, extras_ref, weights_ref, stats_ref
 ):
     me, owner = lax.axis_index("image"), own_fact(extras_ref, 1)
     keys = mine_ref.shape[1]
@@ -379,7 +379,7 @@
         tiles += [block[0:8, k * HEAD : (k + 1) * HEAD] for k in range(KV_HEADS)]
         match.append(block[8, 0].astype(jnp.int32) == owner)
     query = jnp.concatenate(tiles, axis=0).astype(jnp.bfloat16)
-    key_raw = mine_ref[0] + core_ref[...] + jnp.concatenate([low_ref[...], high_ref[...]], axis=1)
+    key_raw = mine_ref[0] + core_ref[...] + pair_ref[...]
     gain = gain_ref[...]
     parts = []
     for k in range(KV_HEADS):
@@ -550,7 +550,7 @@
 
     (to_core,) = send_columns(tokens, half, ((True, False),))
     from_pair = swap(to_pair)
-    from_diagonal = swap(after(to_diagonal, from_pair), 1)
+    from_diagonal = swap(to_diagonal, 1)
     from_core = across(to_core, 1)
 
     k1, k3 = along(key_half, 1), along(key_half, 3)
@@ -562,7 +562,6 @@
     kx2 = across(after(k2, kx), CORES)
     v2 = along(after(value_half, v1, v3), 2)
     vx = across(after(join(v1, v3), kx2), CORES)
-    vx2 = across(v2, CORES)
 
     spots = [(d, mirrored) for mirrored in (False, True) for d in (0, 1, 3, 2)]
     near = join(key_half[half:], k1[half:], k2[half:], k3[half:], k_own[half:], kx[half:step], kx2[half:], kx[step + half :])
@@ -574,8 +573,8 @@
     keys_core = across(keys_part[1], 1)
     late = project([from_diagonal], -1, [after(key_half, keys_part)] + arrays[1:], pieces, spots, half, steps)
     keys_sum = keys_part[2] + across(late[0], 1)
-    middle = width // KV_HEADS
-    keys_pair = [swap(keys_sum[:, :middle]), swap(keys_sum[:, middle:])]
+    vx2 = across(after(v2, keys_sum), CORES)
+    keys_pair = [swap(keys_sum)]
     picked = call(
         functools.partial(pick_kernel, devices, steps, rank),
         jax.ShapeDtypeStruct((devices, rank, rows), down_pages.dtype),
@@ -584,9 +583,11 @@
     )(after(extras, keys_sum), down_pages)
     picked = picked.reshape(devices, 1, rank, rows)
     order = [0]
+    pages = []
     while picked.shape[0] > 1:
         bit = picked.shape[0] // 2
-        picked = jnp.concatenate([picked[:bit], across(picked[bit:], bit)], axis=1)
+        pages.append(across(picked[bit:], bit))
+        picked = jnp.concatenate([picked[:bit], pages[-1]], axis=1)
         order = order + [k ^ bit for k in order]
     picked = picked.reshape(devices, rank, rows)
     lowrank = call(
@@ -598,10 +599,10 @@
     )(extras, tokens, picked, up_pages)
 
     pieces = ((0, 0), (2, 0), (3, 0), (4, 0), (1, 0), (5, 0), (5, half), (6, 0))
-    near_values = after(value_half, keys_pair[0])
+    near_values = after(value_half, keys_sum, pages[0])
     images = images + [from_diagonal]
     values_part = project(images, 0, [near_values, v_own, v1, v3, v2, vx], pieces[:-1], spots, half, steps)
-    values_part = project(images, 0, [after(vx2, keys_pair[1])], ((0, 0),), spots[-1:], half, steps, values_part)
+    values_part = project(images, 0, [after(vx2, keys_pair[0], pages[1])], ((0, 0),), spots[-1:], half, steps, values_part)
     values_core = across(jnp.stack([values_part[1], values_part[3]]), 1)
     values_sum = (values_part[2] + values_core[1]).astype(jnp.bfloat16)
     values_pair = swap(values_sum)
@@ -613,7 +614,7 @@
             jax.ShapeDtypeStruct((heads, tokens.shape[0]), jnp.bfloat16),
             jax.ShapeDtypeStruct((WINDOW, 8, HEAD), jnp.float32),
         ],
-        whole(6),
+        whole(5),
     )(keys_part, keys_core, *keys_pair, key_gain.reshape(1, HEAD), extras)
 
     message = jax.ShapeDtypeStruct((steps, MESSAGE, HEAD), jnp.float32)

time: 123 us -> 113 us (0.919)
  waiting for transfers between devices: 72 us -> 58.2 us
  starting transfers between devices: 26.4 us -> 30.3 us
    ppermute x5 -> x4, waiting for transfers between devices: 15 us -> 2.04 us  [swap(): return lax.ppermute(value, ('groups', 'image'), pairs)]
    ppermute x18, starting transfers between devices: 9.12 us -> 11.8 us  [across(): return lax.ppermute(value, 'image', [(i, i ^ bits) for i in everyone])]
    ppermute x9, starting transfers between devices: 11.2 us -> 13.2 us  [along(): lax.ppermute(value, 'image', [(i, (i - PLANE * d) % devices) for i in eve...]
    ppermute x5 -> x4, starting transfers between devices: 6 us -> 5.31 us  [swap(): return lax.ppermute(value, ('groups', 'image'), pairs)]
  transfers between devices with their start and end apart: 32 -> 31, of which waited for: 18 -> 18; matrix products, arithmetic and copies ran while one was open for 1% -> 0% of each run, Pallas kernels for 11% -> 11%
where the time goes in v4:
time: 113 us; the launch traced here: 112 us
  waiting for transfers between devices  58.2 us (52%)
  starting transfers between devices  30.3 us (27%)
  Pallas kernels  18.8 us (17%)
  local copies, waits for them, and re-layouts  2.4 us (2%)
  between operations  2.28 us (2%)
    ppermute x9, waiting for transfers between devices, along(): lax.ppermute(value, 'image', [(i, (i - PLANE * d) % devices) for i in eve...  32.9 us
    ppermute x18, waiting for transfers between devices, across(): return lax.ppermute(value, 'image', [(i, i ^ bits) for i in everyone])  23.2 us
    ppermute x9, starting transfers between devices, along(): lax.ppermute(value, 'image', [(i, (i - PLANE * d) % devices) for i in eve...  13.2 us
    ppermute x18, starting transfers between devices, across(): return lax.ppermute(value, 'image', [(i, i ^ bits) for i in everyone])  11.8 us
    pallas_call x4, Pallas kernels, project(): call(functools.partial(project_kernel, pieces, spots, number, own, len(ar...  9.07 us
    ppermute x4, starting transfers between devices, swap(): return lax.ppermute(value, ('groups', 'image'), pairs)  5.31 us
    pallas_call x1, Pallas kernels, local(): pl.pallas_call(functools.partial(prepare_kernel, half), out_shape=[jax.Sh...  3.58 us
    pallas_call x1, Pallas kernels, send_columns(): pl.pallas_call(functools.partial(send_kernel, half, targets), out_shape=[...  2.32 us
  transfers between devices with their start and end apart: 31, of which 18 were waited for; matrix products, arithmetic and copies ran while one was open for 0% of the time, Pallas kernels for 11%

profile of v4, /device:TPU:0, one launch (start us, length us, event | category | flops | bytes accessed | tf_op | source)
XLA Modules:
  0.0 112.4 jit_solution(895950546824383876)
XLA Ops:
  1.9 3.6 %shard_map.119 = (bf16[272,512]{1,0:T(8,128)(2,1)}, bf16[256,512]{1,0:T(8,128)(2,1)}, bf16[256,2048]{1,0:T(8,128)(2,1)}, bf16[256,2048]{1,0:T(8,128)(2,1)}) custom-call(s32[1]{0:T(128)S(6)} %copy.28.text_ref, s32[1,1]{1,0:T(1,128)S(6)} %copy.29.image_ref, s32[1]{0:T(128)S(6)} %copy.30.tiles_ref, s32[8]{0:T(128)} %tenant_ref.1, s32[16]{0:T(128)} %page_ref.1, ...), custom_call_target="tpu_custom_call" | custom-call | tf_op jit(solution)/shard_map/pallas_call | solution.py:526
  5.5 3.0 %collective-permute-start.5 = (bf16[272,512]{1,0:T(8,128)(2,1)}, bf16[272,512]{1,0:T(8,128)(2,1)S(1)}, u32[]{:S(2)}, u32[]{:S(2)}) collective-permute-start(bf16[272,512]{1,0:T(8,128)(2,1)} %get-tuple-element.40.refs_3_.refs_1_), channel_id=1, source_target_pairs={{0,2},{1,3},{2,0},{3,1},{4,6},{5,7},{6,4},{7,5},{8,10},{9,11},{10,... | collective-permute-start | bytes 835592 | tf_op jit(solution)/shard_map/ppermute | solution.py:512
  8.5 3.6 %collective-permute-start.3 = (bf16[272,512]{1,0:T(8,128)(2,1)}, bf16[272,512]{1,0:T(8,128)(2,1)S(1)}, u32[]{:S(2)}, u32[]{:S(2)}) collective-permute-start(bf16[272,512]{1,0:T(8,128)(2,1)} %get-tuple-element.40.refs_3_.refs_1_), channel_id=1, source_target_pairs={{0,12},{1,13},{2,14},{3,15},{4,0},{5,1},{6,2},{7,3},{8,4},{9,5},{1... | collective-permute-start | bytes 835592 | tf_op jit(solution)/shard_map/ppermute | solution.py:515
  12.1 1.5 %collective-permute-start.1 = (bf16[256,2048]{1,0:T(8,128)(2,1)}, bf16[256,2048]{1,0:T(8,128)(2,1)S(1)}, u32[]{:S(2)}, u32[]{:S(2)}) collective-permute-start(bf16[256,2048]{1,0:T(8,128)(2,1)} %get-tuple-element.31), channel_id=1, source_target_pairs={{0,16},{1,17},{2,18},{3,19},{4,20},{5,21},{6,22},{7,23},{8,24},{9,... | collective-permute-start | bytes 3145736 | tf_op jit(solution)/shard_map/ppermute | solution.py:519
  13.7 2.3 %shard_map.118 = bf16[256,2048]{1,0:T(8,128)(2,1)} custom-call(bf16[256,8192]{1,0:T(8,128)(2,1)} %bitcast.18), custom_call_target="tpu_custom_call" | custom-call | bytes 2097152 | tf_op jit(solution)/shard_map/pallas_call | solution.py:200
  16.1 0.6 collective-permute-start.2
  16.7 2.9 %collective-permute-done.3.refs_5_.refs_3_ = bf16[272,512]{1,0:T(8,128)(2,1)S(1)} collective-permute-done((bf16[272,512]{1,0:T(8,128)(2,1)}, bf16[272,512]{1,0:T(8,128)(2,1)S(1)}, u32[]{:S(2)}, u32[]{:S(2)}) %collective-permute-start.3) | collective-permute-done | bytes 278560 | tf_op jit(solution)/shard_map/ppermute | solution.py:515
  19.6 5.3 %collective-permute-done.4.refs_6_.refs_4_ = bf16[272,512]{1,0:T(8,128)(2,1)S(1)} collective-permute-done((bf16[272,512]{1,0:T(8,128)(2,1)}, bf16[272,512]{1,0:T(8,128)(2,1)S(1)}, u32[]{:S(2)}, u32[]{:S(2)}) %collective-permute-start.4) | collective-permute-done | bytes 278560 | tf_op jit(solution)/shard_map/ppermute | solution.py:515
  24.9 0.7 collective-permute-start.6
  25.6 0.6 collective-permute-start.7
  26.2 12.7 %collective-permute-done.6.refs_7_.refs_5_ = bf16[272,512]{1,0:T(8,128)(2,1)S(1)} collective-permute-done((bf16[272,512]{1,0:T(8,128)(2,1)S(1)}, bf16[272,512]{1,0:T(8,128)(2,1)S(1)}, u32[]{:S(2)}, u32[]{:S(2)}) %collective-permute-start.6) | collective-permute-done | bytes 278560 | tf_op jit(solution)/shard_map/ppermute | solution.py:515
  39.0 2.9 %collective-permute-start.8 = (bf16[256,512]{1,0:T(8,128)(2,1)S(1)}, bf16[256,512]{1,0:T(8,128)(2,1)S(1)}, u32[]{:S(2)}, u32[]{:S(2)}) collective-permute-start(bf16[256,512]{1,0:T(8,128)(2,1)S(1)} %copy-done.4), channel_id=1, source_target_pairs={{0,12},{1,13},{2,14},{3,15},{4,0},{5,1},{6,2},{7,3},{8,4},{9,5},{1... | collective-permute-start | bytes 786440 | tf_op jit(solution)/shard_map/ppermute | solution.py:515
  41.9 6.8 %collective-permute-done.8.refs_6_ = bf16[256,512]{1,0:T(8,128)(2,1)S(1)} collective-permute-done((bf16[256,512]{1,0:T(8,128)(2,1)S(1)}, bf16[256,512]{1,0:T(8,128)(2,1)S(1)}, u32[]{:S(2)}, u32[]{:S(2)}) %collective-permute-start.8) | collective-permute-done | bytes 262176 | tf_op jit(solution)/shard_map/ppermute | solution.py:515
  48.7 0.5 collective-permute-start.11
  49.2 3.3 %collective-permute-done.9.refs_7_ = bf16[256,512]{1,0:T(8,128)(2,1)S(1)} collective-permute-done((bf16[256,512]{1,0:T(8,128)(2,1)S(1)}, bf16[256,512]{1,0:T(8,128)(2,1)S(1)}, u32[]{:S(2)}, u32[]{:S(2)}) %collective-permute-start.9) | collective-permute-done | bytes 262176 | tf_op jit(solution)/shard_map/ppermute | solution.py:515
  53.0 4.7 %collective-permute-done.11.refs_9_.refs_7_ = bf16[272,512]{1,0:T(8,128)(2,1)S(1)} collective-permute-done((bf16[272,512]{1,0:T(8,128)(2,1)S(1)}, bf16[272,512]{1,0:T(8,128)(2,1)S(1)}, u32[]{:S(2)}, u32[]{:S(2)}) %collective-permute-start.11) | collective-permute-done | bytes 278560 | tf_op jit(solution)/shard_map/ppermute | solution.py:512
  57.7 0.8 collective-permute-start.10
  58.7 2.2 %copy-done = bf16[1,256,8192]{2,1,0:T(8,128)(2,1)S(1)} copy-done((bf16[1,256,8192]{2,1,0:T(8,128)(2,1)S(1)}, bf16[1,256,8192]{2,1,0:T(8,128)(2,1)}, u32[]{:S(2)}) %copy-start) | copy-done | bytes 4194328
  60.8 3.1 %shard_map.120.mine_ref = f32[3,256,512]{2,1,0:T(8,128)S(1)} custom-call(bf16[256,8192]{1,0:T(8,128)(2,1)S(1)} %bitcast.19, bf16[256,2048]{1,0:T(8,128)(2,1)S(1)} %collective-permute-done.refs_1_, bf16[256,2048]{1,0:T(8,128)(2,1)S(1)} %collective-permute-done.1.refs_2_, bf16[272,512]{1,0:T(8,128)(2,1)S(1)} %copy-done.2, ...), custom_call_target="tpu_custom_call" | custom-call | flops 1610612736 | bytes 5242880 | tf_op jit(solution)/shard_map/pallas_call | solution.py:297
  64.0 1.2 %shard_map.121 = f32[1,256,512]{2,1,0:T(8,128)S(1)} custom-call(bf16[256,2048]{1,0:T(8,128)(2,1)S(1)} %collective-permute-done.2.refs_0_.refs_3_, bf16[272,512]{1,0:T(8,128)(2,1)S(1)} %copy-done.2, bf16[272,512]{1,0:T(8,128)(2,1)S(1)} %collective-permute-done.5.refs_4_.refs_2_, bf16[272,512]{1,0:T(8,128)(2,1)S(1)} %collective-permute-done.3.refs_5_.refs_3_, ...), custom_call_target="tpu_custom_call" | custom-call | flops 536870912 | bytes 3145728 | tf_op jit(solution)/shard_map/pallas_call | solution.py:297
  65.2 0.6 collective-permute-start.12
  65.8 0.5 collective-permute-start.19
  66.4 1.0 collective-permute-done.12
  67.4 1.6 %collective-permute-start.14 = (f32[256,512]{1,0:T(8,128)S(1)}, f32[256,512]{1,0:T(8,128)S(1)}, u32[]{:S(2)}, u32[]{:S(2)}) collective-permute-start(f32[256,512]{1,0:T(8,128)S(1)} %fusion.1), channel_id=1, source_target_pairs={{0,16},{1,17},{2,18},{3,19},{4,20},{5,21},{6,22},{7,23},{8,24},{9,... | collective-permute-start | bytes 1572872 | tf_op jit(solution)/shard_map/ppermute | solution.py:519
  69.5 2.2 %collective-permute-start.16 = (bf16[8,1,16,512]{3,2,1,0:T(8,128)(2,1)S(1)}, bf16[8,1,16,512]{3,2,1,0:T(8,128)(2,1)S(1)}, u32[]{:S(2)}, u32[]{:S(2)}) collective-permute-start(bf16[8,1,16,512]{3,2,1,0:T(8,128)(2,1)S(1)} %get-tuple-element.75), channel_id=1, source_target_pairs={{0,8},{1,9},{2,10},{3,11},{4,12},{5,13},{6,14},{7,15},{8,0},{9,1},... | collective-permute-start | bytes 393224 | tf_op jit(solution)/shard_map/ppermute | solution.py:512
  72.2 6.5 %collective-permute-done.16 = bf16[8,1,16,512]{3,2,1,0:T(8,128)(2,1)S(1)} collective-permute-done((bf16[8,1,16,512]{3,2,1,0:T(8,128)(2,1)S(1)}, bf16[8,1,16,512]{3,2,1,0:T(8,128)(2,1)S(1)}, u32[]{:S(2)}, u32[]{:S(2)}) %collective-permute-start.16) | collective-permute-done | bytes 131104 | tf_op jit(solution)/shard_map/ppermute | solution.py:512
  78.8 1.8 %collective-permute-done.19.refs_9_ = bf16[512,512]{1,0:T(8,128)(2,1)S(1)} collective-permute-done((bf16[512,512]{1,0:T(8,128)(2,1)S(1)}, bf16[512,512]{1,0:T(8,128)(2,1)S(1)}, u32[]{:S(2)}, u32[]{:S(2)}) %collective-permute-start.19) | collective-permute-done | bytes 524320 | tf_op jit(solution)/shard_map/ppermute | solution.py:512
  80.6 3.7 %shard_map.123.refs_5_ = f32[4,256,512]{2,1,0:T(8,128)S(1)} custom-call(bf16[256,8192]{1,0:T(8,128)(2,1)S(1)} %bitcast.20, bf16[256,2048]{1,0:T(8,128)(2,1)S(1)} %collective-permute-done.refs_1_, bf16[256,2048]{1,0:T(8,128)(2,1)S(1)} %collective-permute-done.1.refs_2_, bf16[256,2048]{1,0:T(8,128)(2,1)S(1)} %collective-permute-done.2.refs_0_.refs_3_, ...), custom_call_target="tpu_custom_call" | custom-call | flops 1879048192 | bytes 5505024 | tf_op jit(solution)/shard_map/pallas_call | solution.py:297
  84.3 1.1 collective-permute-done.13.refs_4_
  85.3 1.1 shard_map.124.mine_ref
  86.7 0.6 collective-permute-start.24
  87.3 0.6 collective-permute-start.22
  87.9 1.4 %collective-permute-done.20.core_ref = f32[2,256,512]{2,1,0:T(8,128)S(1)} collective-permute-done((f32[2,256,512]{2,1,0:T(8,128)S(1)}, f32[2,256,512]{2,1,0:T(8,128)S(1)}, u32[]{:S(2)}, u32[]{:S(2)}) %collective-permute-start.20) | collective-permute-done | bytes 1048608 | tf_op jit(solution)/shard_map/ppermute | solution.py:512
  89.4 1.6 %collective-permute-start.21 = (bf16[256,512]{1,0:T(8,128)(2,1)S(1)}, bf16[256,512]{1,0:T(8,128)(2,1)S(1)}, u32[]{:S(2)}, u32[]{:S(2)}) collective-permute-start(bf16[256,512]{1,0:T(8,128)(2,1)S(1)} %fusion.2), channel_id=1, source_target_pairs={{0,16},{1,17},{2,18},{3,19},{4,20},{5,21},{6,22},{7,23},{8,24},{9,... | collective-permute-start | bytes 786440 | tf_op jit(solution)/shard_map/ppermute | solution.py:519
  91.0 1.8 %collective-permute-done.22 = bf16[2,4,16,512]{3,2,1,0:T(8,128)(2,1)S(1)} collective-permute-done((bf16[2,4,16,512]{3,2,1,0:T(8,128)(2,1)S(1)}, bf16[2,4,16,512]{3,2,1,0:T(8,128)(2,1)S(1)}, u32[]{:S(2)}, u32[]{:S(2)}) %collective-permute-start.22) | collective-permute-done | bytes 131104 | tf_op jit(solution)/shard_map/ppermute | solution.py:512
  92.9 0.7 shard_map.126
  93.6 0.6 collective-permute-done.23
  94.3 1.5 %shard_map.125.lowrank_ref = f32[256,512]{1,0:T(8,128)S(1)} custom-call(bf16[256,512]{1,0:T(8,128)(2,1)S(1)} %constant_dynamic-update-slice_fusion.8.extras_ref, bf16[256,8192]{1,0:T(8,128)(2,1)S(1)} %bitcast.22, bf16[16,16,512]{2,1,0:T(8,128)(2,1)S(1)} %maximum_bitcast_fusion.down_ref, bf16[16,16,512]{2,1,0:T(8,128)(2,1)S(1)} %copy-done.5), custom_call_target="tpu_custom_call" | custom-call | bytes 4194304 | tf_op jit(solution)/shard_map/pallas_call | solution.py:593
  95.8 2.0 %collective-permute-done.21.pair_ref = bf16[256,512]{1,0:T(8,128)(2,1)S(1)} collective-permute-done((bf16[256,512]{1,0:T(8,128)(2,1)S(1)}, bf16[256,512]{1,0:T(8,128)(2,1)S(1)}, u32[]{:S(2)}, u32[]{:S(2)}) %collective-permute-start.21) | collective-permute-done | bytes 262176 | tf_op jit(solution)/shard_map/ppermute | solution.py:519
  98.3 0.6 collective-permute-start.26
  98.9 1.3 %collective-permute-start.27 = (f32[4,40,128]{2,1,0:T(8,128)S(1)}, f32[4,40,128]{2,1,0:T(8,128)S(1)}, u32[]{:S(2)}, u32[]{:S(2)}) collective-permute-start(f32[4,40,128]{2,1,0:T(8,128)S(1)} %get-tuple-element.52), channel_id=1, source_target_pairs={{0,3},{1,2},{2,1},{3,0},{4,7},{5,6},{6,5},{7,4},{8,11},{9,10},{10,... | collective-permute-start | bytes 245768 | tf_op jit(solution)/shard_map/ppermute | solution.py:512
  100.1 3.4 %collective-permute-done.26.refs_2_ = f32[4,40,128]{2,1,0:T(8,128)S(1)} collective-permute-done((f32[4,40,128]{2,1,0:T(8,128)S(1)}, f32[4,40,128]{2,1,0:T(8,128)S(1)}, u32[]{:S(2)}, u32[]{:S(2)}) %collective-permute-start.26) | collective-permute-done | bytes 81952 | tf_op jit(solution)/shard_map/ppermute | solution.py:512
  103.6 0.8 collective-permute-done.27.refs_3_
  104.6 2.3 %collective-permute-start.28 = (f32[40,128]{1,0:T(8,128)S(1)}, f32[40,128]{1,0:T(8,128)S(1)}, u32[]{:S(2)}, u32[]{:S(2)}) collective-permute-start(f32[40,128]{1,0:T(8,128)S(1)} %get-tuple-element.54), channel_id=1, source_target_pairs={{0,4},{1,5},{2,6},{3,7},{4,8},{5,9},{6,10},{7,11},{8,12},{9,13},{1... | collective-permute-start | bytes 61448 | tf_op jit(solution)/shard_map/ppermute | solution.py:515
  106.9 2.8 %collective-permute-start.30 = (f32[40,128]{1,0:T(8,128)S(1)}, f32[40,128]{1,0:T(8,128)S(1)}, u32[]{:S(2)}, u32[]{:S(2)}) collective-permute-start(f32[40,128]{1,0:T(8,128)S(1)} %get-tuple-element.56), channel_id=1, source_target_pairs={{0,12},{1,13},{2,14},{3,15},{4,0},{5,1},{6,2},{7,3},{8,4},{9,5},{1... | collective-permute-start | bytes 61448 | tf_op jit(solution)/shard_map/ppermute | solution.py:515
  109.7 0.5 collective-permute-done.28.refs_1_
  110.2 1.4 %collective-permute-done.29.refs_2_ = f32[40,128]{1,0:T(8,128)S(1)} collective-permute-done((f32[40,128]{1,0:T(8,128)S(1)}, f32[40,128]{1,0:T(8,128)S(1)}, u32[]{:S(2)}, u32[]{:S(2)}) %collective-permute-start.29) | collective-permute-done | bytes 20512 | tf_op jit(solution)/shard_map/ppermute | solution.py:515
  111.7 0.7 shard_map.129
  (64 shorter events, 3.0 us)
Async XLA Ops:
  5.5 10.5 %collective-permute-start.5 = (bf16[272,512]{1,0:T(8,128)(2,1)}, bf16[272,512]{1,0:T(8,128)(2,1)S(1)}, u32[]{:S(2)}, u32[]{:S(2)}) collective-permute-start(bf16[272,512]{1,0:T(8,128)(2,1)} %get-tuple-element.40.refs_3_.refs_1_), channel_id=1, source_target_pairs={{0,2},{1,3},{2,0},{3,1},{4,6},{5,7},{6,4},{7,5},{8,10},{9,11},{10,... | collective-permute-start | bytes 835592 | tf_op jit(solution)/shard_map/ppermute | solution.py:512
  8.5 11.0 %collective-permute-start.3 = (bf16[272,512]{1,0:T(8,128)(2,1)}, bf16[272,512]{1,0:T(8,128)(2,1)S(1)}, u32[]{:S(2)}, u32[]{:S(2)}) collective-permute-start(bf16[272,512]{1,0:T(8,128)(2,1)} %get-tuple-element.40.refs_3_.refs_1_), channel_id=1, source_target_pairs={{0,12},{1,13},{2,14},{3,15},{4,0},{5,1},{6,2},{7,3},{8,4},{9,5},{1... | collective-permute-start | bytes 835592 | tf_op jit(solution)/shard_map/ppermute | solution.py:515
  12.1 12.7 %collective-permute-start.4 = (bf16[272,512]{1,0:T(8,128)(2,1)}, bf16[272,512]{1,0:T(8,128)(2,1)S(1)}, u32[]{:S(2)}, u32[]{:S(2)}) collective-permute-start(bf16[272,512]{1,0:T(8,128)(2,1)} %get-tuple-element.40.refs_3_.refs_1_), channel_id=1, source_target_pairs={{0,4},{1,5},{2,6},{3,7},{4,8},{5,9},{6,10},{7,11},{8,12},{9,13},{1... | collective-permute-start | bytes 835592 | tf_op jit(solution)/shard_map/ppermute | solution.py:515
  12.1 12.7 %copy-start.2 = (bf16[272,512]{1,0:T(8,128)(2,1)S(1)}, bf16[272,512]{1,0:T(8,128)(2,1)}, u32[]{:S(2)}) copy-start(bf16[272,512]{1,0:T(8,128)(2,1)} %get-tuple-element.40.refs_3_.refs_1_) | copy-start | bytes 835588
  12.1 26.8 %copy-start.4 = (bf16[256,512]{1,0:T(8,128)(2,1)S(1)}, bf16[256,512]{1,0:T(8,128)(2,1)}, u32[]{:S(2)}) copy-start(bf16[256,512]{1,0:T(8,128)(2,1)} %get-tuple-element.45.refs_4_) | copy-start | bytes 786436
  12.1 46.4 %collective-permute-start.1 = (bf16[256,2048]{1,0:T(8,128)(2,1)}, bf16[256,2048]{1,0:T(8,128)(2,1)S(1)}, u32[]{:S(2)}, u32[]{:S(2)}) collective-permute-start(bf16[256,2048]{1,0:T(8,128)(2,1)} %get-tuple-element.31), channel_id=1, source_target_pairs={{0,16},{1,17},{2,18},{3,19},{4,20},{5,21},{6,22},{7,23},{8,24},{9,... | collective-permute-start | bytes 3145736 | tf_op jit(solution)/shard_map/ppermute | solution.py:519
  16.0 42.7 %collective-permute-start = (bf16[256,2048]{1,0:T(8,128)(2,1)}, bf16[256,2048]{1,0:T(8,128)(2,1)S(1)}, u32[]{:S(2)}, u32[]{:S(2)}) collective-permute-start(bf16[256,2048]{1,0:T(8,128)(2,1)} %shard_map.118), channel_id=1, source_target_pairs={{0,1},{1,0},{2,3},{3,2},{4,5},{5,4},{6,7},{7,6},{8,9},{9,8},{10,11... | collective-permute-start | bytes 3145736 | tf_op jit(solution)/shard_map/ppermute | solution.py:512
  16.1 47.9 %collective-permute-start.2 = (bf16[256,2048]{1,0:T(8,128)(2,1)}, bf16[256,2048]{1,0:T(8,128)(2,1)S(1)}, u32[]{:S(2)}, u32[]{:S(2)}) collective-permute-start(bf16[256,2048]{1,0:T(8,128)(2,1)} %get-tuple-element.32), channel_id=1, source_target_pairs={{0,17},{1,16},{2,19},{3,18},{4,21},{5,20},{6,23},{7,22},{8,25},{9,... | collective-permute-start | bytes 3145736 | tf_op jit(solution)/shard_map/ppermute | solution.py:519
  24.9 14.1 %collective-permute-start.6 = (bf16[272,512]{1,0:T(8,128)(2,1)S(1)}, bf16[272,512]{1,0:T(8,128)(2,1)S(1)}, u32[]{:S(2)}, u32[]{:S(2)}) collective-permute-start(bf16[272,512]{1,0:T(8,128)(2,1)S(1)} %copy-done.2), channel_id=1, source_target_pairs={{0,8},{1,9},{2,10},{3,11},{4,12},{5,13},{6,14},{7,15},{8,0},{9,1},... | collective-permute-start | bytes 835592 | tf_op jit(solution)/shard_map/ppermute | solution.py:515
  25.6 13.3 %collective-permute-start.7 = (bf16[544,512]{1,0:T(8,128)(2,1)S(1)}, bf16[544,512]{1,0:T(8,128)(2,1)S(1)}, u32[]{:S(2)}, u32[]{:S(2)}) collective-permute-start(bf16[544,512]{1,0:T(8,128)(2,1)S(1)} %pad_maximum_fusion.1), channel_id=1, source_target_pairs={{0,2},{1,3},{2,0},{3,1},{4,6},{5,7},{6,4},{7,5},{8,10},{9,11},{10,... | collective-permute-start | bytes 1671176 | tf_op jit(solution)/shard_map/ppermute | solution.py:512
  39.0 9.7 %collective-permute-start.8 = (bf16[256,512]{1,0:T(8,128)(2,1)S(1)}, bf16[256,512]{1,0:T(8,128)(2,1)S(1)}, u32[]{:S(2)}, u32[]{:S(2)}) collective-permute-start(bf16[256,512]{1,0:T(8,128)(2,1)S(1)} %copy-done.4), channel_id=1, source_target_pairs={{0,12},{1,13},{2,14},{3,15},{4,0},{5,1},{6,2},{7,3},{8,4},{9,5},{1... | collective-permute-start | bytes 786440 | tf_op jit(solution)/shard_map/ppermute | solution.py:515
  41.9 10.6 %collective-permute-start.9 = (bf16[256,512]{1,0:T(8,128)(2,1)S(1)}, bf16[256,512]{1,0:T(8,128)(2,1)S(1)}, u32[]{:S(2)}, u32[]{:S(2)}) collective-permute-start(bf16[256,512]{1,0:T(8,128)(2,1)S(1)} %copy-done.4), channel_id=1, source_target_pairs={{0,4},{1,5},{2,6},{3,7},{4,8},{5,9},{6,10},{7,11},{8,12},{9,13},{1... | collective-permute-start | bytes 786440 | tf_op jit(solution)/shard_map/ppermute | solution.py:515
  48.7 9.1 %collective-permute-start.11 = (bf16[272,512]{1,0:T(8,128)(2,1)S(1)}, bf16[272,512]{1,0:T(8,128)(2,1)S(1)}, u32[]{:S(2)}, u32[]{:S(2)}) collective-permute-start(bf16[272,512]{1,0:T(8,128)(2,1)S(1)} %collective-permute-done.6.refs_7_.refs_5_), channel_id=1, source_target_pairs={{0,2},{1,3},{2,0},{3,1},{4,6},{5,7},{6,4},{7,5},{8,10},{9,11},{10,... | collective-permute-start | bytes 835592 | tf_op jit(solution)/shard_map/ppermute | solution.py:512
  52.5 26.3 %collective-permute-start.18 = (bf16[256,512]{1,0:T(8,128)(2,1)S(1)}, bf16[256,512]{1,0:T(8,128)(2,1)S(1)}, u32[]{:S(2)}, u32[]{:S(2)}) collective-permute-start(bf16[256,512]{1,0:T(8,128)(2,1)S(1)} %copy-done.4), channel_id=1, source_target_pairs={{0,2},{1,3},{2,0},{3,1},{4,6},{5,7},{6,4},{7,5},{8,10},{9,11},{10,... | collective-permute-start | bytes 786440 | tf_op jit(solution)/shard_map/ppermute | solution.py:512
  57.7 13.9 %collective-permute-start.10 = (bf16[256,512]{1,0:T(8,128)(2,1)S(1)}, bf16[256,512]{1,0:T(8,128)(2,1)S(1)}, u32[]{:S(2)}, u32[]{:S(2)}) collective-permute-start(bf16[256,512]{1,0:T(8,128)(2,1)S(1)} %copy-done.4), channel_id=1, source_target_pairs={{0,8},{1,9},{2,10},{3,11},{4,12},{5,13},{6,14},{7,15},{8,0},{9,1},... | collective-permute-start | bytes 786440 | tf_op jit(solution)/shard_map/ppermute | solution.py:515
  58.6 7.8 %collective-permute-start.15 = (bf16[128,512]{1,0:T(8,128)(2,1)S(1)}, bf16[128,512]{1,0:T(8,128)(2,1)S(1)}, u32[]{:S(2)}, u32[]{:S(2)}) collective-permute-start(bf16[128,512]{1,0:T(8,128)(2,1)S(1)} %get-tuple-element.59), channel_id=1, source_target_pairs={{0,1},{1,0},{2,3},{3,2},{4,5},{5,4},{6,7},{7,6},{8,9},{9,8},{10,11... | collective-permute-start | bytes 393224 | tf_op jit(solution)/shard_map/ppermute | solution.py:512
  58.7 2.2 %copy-start = (bf16[1,256,8192]{2,1,0:T(8,128)(2,1)S(1)}, bf16[1,256,8192]{2,1,0:T(8,128)(2,1)}, u32[]{:S(2)}) copy-start(bf16[1,256,8192]{2,1,0:T(8,128)(2,1)} %param.12) | copy-start | bytes 12582916
  64.0 16.6 %copy-start.1 = (bf16[1,256,8192]{2,1,0:T(8,128)(2,1)S(1)}, bf16[1,256,8192]{2,1,0:T(8,128)(2,1)}, u32[]{:S(2)}) copy-start(bf16[1,256,8192]{2,1,0:T(8,128)(2,1)} %param.12) | copy-start | bytes 12582916
  65.2 3.8 %copy-start.3 = (bf16[512,256]{1,0:T(8,128)(2,1)S(1)}, bf16[512,256]{1,0:T(8,128)(2,1)}, u32[]{:S(2)}) copy-start(bf16[512,256]{1,0:T(8,128)(2,1)} %down_ref.1) | copy-start | bytes 786436
  65.2 2.1 %collective-permute-start.12 = (f32[256,512]{1,0:T(8,128)S(1)}, f32[256,512]{1,0:T(8,128)S(1)}, u32[]{:S(2)}, u32[]{:S(2)}) collective-permute-start(f32[256,512]{1,0:T(8,128)S(1)} %bitcast.23), channel_id=1, source_target_pairs={{0,1},{1,0},{2,3},{3,2},{4,5},{5,4},{6,7},{7,6},{8,9},{9,8},{10,11... | collective-permute-start | bytes 1572872 | tf_op jit(solution)/shard_map/ppermute | solution.py:512
  65.8 14.8 %collective-permute-start.19 = (bf16[512,512]{1,0:T(8,128)(2,1)S(1)}, bf16[512,512]{1,0:T(8,128)(2,1)S(1)}, u32[]{:S(2)}, u32[]{:S(2)}) collective-permute-start(bf16[512,512]{1,0:T(8,128)(2,1)S(1)} %pad_maximum_fusion.2), channel_id=1, source_target_pairs={{0,2},{1,3},{2,0},{3,1},{4,6},{5,7},{6,4},{7,5},{8,10},{9,11},{10,... | collective-permute-start | bytes 1572872 | tf_op jit(solution)/shard_map/ppermute | solution.py:512
  67.4 17.9 %collective-permute-start.14 = (f32[256,512]{1,0:T(8,128)S(1)}, f32[256,512]{1,0:T(8,128)S(1)}, u32[]{:S(2)}, u32[]{:S(2)}) collective-permute-start(f32[256,512]{1,0:T(8,128)S(1)} %fusion.1), channel_id=1, source_target_pairs={{0,16},{1,17},{2,18},{3,19},{4,20},{5,21},{6,22},{7,23},{8,24},{9,... | collective-permute-start | bytes 1572872 | tf_op jit(solution)/shard_map/ppermute | solution.py:519
  69.5 9.3 %collective-permute-start.16 = (bf16[8,1,16,512]{3,2,1,0:T(8,128)(2,1)S(1)}, bf16[8,1,16,512]{3,2,1,0:T(8,128)(2,1)S(1)}, u32[]{:S(2)}, u32[]{:S(2)}) collective-permute-start(bf16[8,1,16,512]{3,2,1,0:T(8,128)(2,1)S(1)} %get-tuple-element.75), channel_id=1, source_target_pairs={{0,8},{1,9},{2,10},{3,11},{4,12},{5,13},{6,14},{7,15},{8,0},{9,1},... | collective-permute-start | bytes 393224 | tf_op jit(solution)/shard_map/ppermute | solution.py:512
  71.6 13.7 %collective-permute-start.13 = (bf16[256,512]{1,0:T(8,128)(2,1)S(1)}, bf16[256,512]{1,0:T(8,128)(2,1)S(1)}, u32[]{:S(2)}, u32[]{:S(2)}) collective-permute-start(bf16[256,512]{1,0:T(8,128)(2,1)S(1)} %collective-permute-done.10.refs_8_), channel_id=1, source_target_pairs={{0,2},{1,3},{2,0},{3,1},{4,6},{5,7},{6,4},{7,5},{8,10},{9,11},{10,... | collective-permute-start | bytes 786440 | tf_op jit(solution)/shard_map/ppermute | solution.py:512
  78.7 6.6 %collective-permute-start.17 = (bf16[4,2,16,512]{3,2,1,0:T(8,128)(2,1)S(1)}, bf16[4,2,16,512]{3,2,1,0:T(8,128)(2,1)S(1)}, u32[]{:S(2)}, u32[]{:S(2)}) collective-permute-start(bf16[4,2,16,512]{3,2,1,0:T(8,128)(2,1)S(1)} %fusion.5), channel_id=1, source_target_pairs={{0,4},{1,5},{2,6},{3,7},{4,0},{5,1},{6,2},{7,3},{8,12},{9,13},{10,... | collective-permute-start | bytes 393224 | tf_op jit(solution)/shard_map/ppermute | solution.py:512
  86.6 2.7 %collective-permute-start.20 = (f32[2,256,512]{2,1,0:T(8,128)S(1)}, f32[2,256,512]{2,1,0:T(8,128)S(1)}, u32[]{:S(2)}, u32[]{:S(2)}) collective-permute-start(f32[2,256,512]{2,1,0:T(8,128)S(1)} %pad_maximum_fusion), channel_id=1, source_target_pairs={{0,1},{1,0},{2,3},{3,2},{4,5},{5,4},{6,7},{7,6},{8,9},{9,8},{10,11... | collective-permute-start | bytes 3145736 | tf_op jit(solution)/shard_map/ppermute | solution.py:512
  86.7 6.2 %copy-start.6 = (f32[128]{0:T(128)S(1)}, f32[128]{0:T(128)}, u32[]{:S(2)}) copy-start(f32[128]{0:T(128)} %param.17) | copy-start | bytes 1540
  86.7 6.2 %collective-permute-start.24 = (f32[256,512]{1,0:T(8,128)S(1)}, f32[256,512]{1,0:T(8,128)S(1)}, u32[]{:S(2)}, u32[]{:S(2)}) collective-permute-start(f32[256,512]{1,0:T(8,128)S(1)} %slice_bitcast_fusion), channel_id=1, source_target_pairs={{0,1},{1,0},{2,3},{3,2},{4,5},{5,4},{6,7},{7,6},{8,9},{9,8},{10,11... | collective-permute-start | bytes 1572872 | tf_op jit(solution)/shard_map/ppermute | solution.py:512
  87.3 5.5 %collective-permute-start.22 = (bf16[2,4,16,512]{3,2,1,0:T(8,128)(2,1)S(1)}, bf16[2,4,16,512]{3,2,1,0:T(8,128)(2,1)S(1)}, u32[]{:S(2)}, u32[]{:S(2)}) collective-permute-start(bf16[2,4,16,512]{3,2,1,0:T(8,128)(2,1)S(1)} %get-tuple-element.74), channel_id=1, source_target_pairs={{0,2},{1,3},{2,0},{3,1},{4,6},{5,7},{6,4},{7,5},{8,10},{9,11},{10,... | collective-permute-start | bytes 393224 | tf_op jit(solution)/shard_map/ppermute | solution.py:512
  89.4 8.4 %collective-permute-start.21 = (bf16[256,512]{1,0:T(8,128)(2,1)S(1)}, bf16[256,512]{1,0:T(8,128)(2,1)S(1)}, u32[]{:S(2)}, u32[]{:S(2)}) collective-permute-start(bf16[256,512]{1,0:T(8,128)(2,1)S(1)} %fusion.2), channel_id=1, source_target_pairs={{0,16},{1,17},{2,18},{3,19},{4,20},{5,21},{6,22},{7,23},{8,24},{9,... | collective-permute-start | bytes 786440 | tf_op jit(solution)/shard_map/ppermute | solution.py:519
  92.8 1.4 %collective-permute-start.23 = (bf16[1,8,16,512]{3,2,1,0:T(8,128)(2,1)S(1)}, bf16[1,8,16,512]{3,2,1,0:T(8,128)(2,1)S(1)}, u32[]{:S(2)}, u32[]{:S(2)}) collective-permute-start(bf16[1,8,16,512]{3,2,1,0:T(8,128)(2,1)S(1)} %get-tuple-element.72), channel_id=1, source_target_pairs={{0,1},{1,0},{2,3},{3,2},{4,5},{5,4},{6,7},{7,6},{8,9},{9,8},{10,11... | collective-permute-start | bytes 393224 | tf_op jit(solution)/shard_map/ppermute | solution.py:512
  92.9 1.3 %copy-start.5 = (bf16[16,16,512]{2,1,0:T(8,128)(2,1)S(1)}, bf16[16,16,512]{2,1,0:T(8,128)(2,1)}, u32[]{:S(2)}) copy-start(bf16[16,16,512]{2,1,0:T(8,128)(2,1)} %up_ref.1) | copy-start | bytes 786436
  98.2 1.9 %collective-permute-start.25 = (f32[4,40,128]{2,1,0:T(8,128)S(1)}, f32[4,40,128]{2,1,0:T(8,128)S(1)}, u32[]{:S(2)}, u32[]{:S(2)}) collective-permute-start(f32[4,40,128]{2,1,0:T(8,128)S(1)} %get-tuple-element.50), channel_id=1, source_target_pairs={{0,1},{1,0},{2,3},{3,2},{4,5},{5,4},{6,7},{7,6},{8,9},{9,8},{10,11... | collective-permute-start | bytes 245768 | tf_op jit(solution)/shard_map/ppermute | solution.py:512
  98.3 5.3 %collective-permute-start.26 = (f32[4,40,128]{2,1,0:T(8,128)S(1)}, f32[4,40,128]{2,1,0:T(8,128)S(1)}, u32[]{:S(2)}, u32[]{:S(2)}) collective-permute-start(f32[4,40,128]{2,1,0:T(8,128)S(1)} %get-tuple-element.51), channel_id=1, source_target_pairs={{0,2},{1,3},{2,0},{3,1},{4,6},{5,7},{6,4},{7,5},{8,10},{9,11},{10,... | collective-permute-start | bytes 245768 | tf_op jit(solution)/shard_map/ppermute | solution.py:512
  98.9 5.6 %collective-permute-start.27 = (f32[4,40,128]{2,1,0:T(8,128)S(1)}, f32[4,40,128]{2,1,0:T(8,128)S(1)}, u32[]{:S(2)}, u32[]{:S(2)}) collective-permute-start(f32[4,40,128]{2,1,0:T(8,128)S(1)} %get-tuple-element.52), channel_id=1, source_target_pairs={{0,3},{1,2},{2,1},{3,0},{4,7},{5,6},{6,5},{7,4},{8,11},{9,10},{10,... | collective-permute-start | bytes 245768 | tf_op jit(solution)/shard_map/ppermute | solution.py:512
  104.6 5.6 %collective-permute-start.28 = (f32[40,128]{1,0:T(8,128)S(1)}, f32[40,128]{1,0:T(8,128)S(1)}, u32[]{:S(2)}, u32[]{:S(2)}) collective-permute-start(f32[40,128]{1,0:T(8,128)S(1)} %get-tuple-element.54), channel_id=1, source_target_pairs={{0,4},{1,5},{2,6},{3,7},{4,8},{5,9},{6,10},{7,11},{8,12},{9,13},{1... | collective-permute-start | bytes 61448 | tf_op jit(solution)/shard_map/ppermute | solution.py:515
  106.9 4.8 %collective-permute-start.29 = (f32[40,128]{1,0:T(8,128)S(1)}, f32[40,128]{1,0:T(8,128)S(1)}, u32[]{:S(2)}, u32[]{:S(2)}) collective-permute-start(f32[40,128]{1,0:T(8,128)S(1)} %get-tuple-element.55), channel_id=1, source_target_pairs={{0,8},{1,9},{2,10},{3,11},{4,12},{5,13},{6,14},{7,15},{8,0},{9,1},... | collective-permute-start | bytes 61448 | tf_op jit(solution)/shard_map/ppermute | solution.py:515
  106.9 4.8 %collective-permute-start.30 = (f32[40,128]{1,0:T(8,128)S(1)}, f32[40,128]{1,0:T(8,128)S(1)}, u32[]{:S(2)}, u32[]{:S(2)}) collective-permute-start(f32[40,128]{1,0:T(8,128)S(1)} %get-tuple-element.56), channel_id=1, source_target_pairs={{0,12},{1,13},{2,14},{3,15},{4,0},{5,1},{6,2},{7,3},{8,4},{9,5},{1... | collective-permute-start | bytes 61448 | tf_op jit(solution)/shard_map/ppermute | solution.py:515

commit v5 on v4

--- a/solution.py
+++ b/solution.py
@@ -557,15 +557,13 @@
     k_own = across(key_half, CORES)
     k2 = along(after(key_half, k1, k3, k_own), 2)
     kx = across(after(join(k1, k3), k_own), CORES)
-    v_own = across(after(value_half, k_own), CORES)
-    v1, v3 = along(after(value_half, k2, kx), 1), along(after(value_half, k2, kx), 3)
-    kx2 = across(after(k2, kx), CORES)
+    v1, v3 = along(after(value_half, k2, kx, from_core), 1), along(after(value_half, k2, kx, from_core), 3)
+    kx2 = across(after(join(k2, value_half), kx), CORES)
     v2 = along(after(value_half, v1, v3), 2)
     vx = across(after(join(v1, v3), kx2), CORES)
 
     spots = [(d, mirrored) for mirrored in (False, True) for d in (0, 1, 3, 2)]
-    near = join(key_half[half:], k1[half:], k2[half:], k3[half:], k_own[half:], kx[half:step], kx2[half:], kx[step + half :])
-    extras = join(near, across(near, 1))
+    near = join(key_half[half:], k1[half:], k2[half:], k3[half:], k_own[half:], kx[half:step], kx2[half:step], kx[step + half :])
     images = [tokens, from_core, from_pair]
     arrays = [key_half, k_own, k1, k3, k2, kx, kx2]
     pieces = ((0, 0), (2, 0), (3, 0), (4, 0), (1, 0), (5, 0), (5, step), (6, 0))
@@ -575,6 +573,7 @@
     keys_sum = keys_part[2] + across(late[0], 1)
     vx2 = across(after(v2, keys_sum), CORES)
     keys_pair = [swap(keys_sum)]
+    extras = join(near, across(after(near, keys_sum), 1))
     picked = call(
         functools.partial(pick_kernel, devices, steps, rank),
         jax.ShapeDtypeStruct((devices, rank, rows), down_pages.dtype),
@@ -598,10 +597,10 @@
         moved=tokens.size * 2,
     )(extras, tokens, picked, up_pages)
 
-    pieces = ((0, 0), (2, 0), (3, 0), (4, 0), (1, 0), (5, 0), (5, half), (6, 0))
+    pieces = ((0, 0), (2, 0), (3, 0), (4, 0), (1, step), (5, 0), (5, half), (6, 0))
     near_values = after(value_half, keys_sum, pages[0])
     images = images + [from_diagonal]
-    values_part = project(images, 0, [near_values, v_own, v1, v3, v2, vx], pieces[:-1], spots, half, steps)
+    values_part = project(images, 0, [near_values, kx2, v1, v3, v2, vx], pieces[:-1], spots, half, steps)
     values_part = project(images, 0, [after(vx2, keys_pair[0], pages[1])], ((0, 0),), spots[-1:], half, steps, values_part)
     values_core = across(jnp.stack([values_part[1], values_part[3]]), 1)
     values_sum = (values_part[2] + values_core[1]).astype(jnp.bfloat16)

time: 113 us -> 109 us (0.965)
  waiting for transfers between devices: 58.2 us -> 53 us
  starting transfers between devices: 30.3 us -> 32.3 us
    ppermute x18 -> x17, waiting for transfers between devices: 23.2 us -> 17.2 us  [across(): return lax.ppermute(value, 'image', [(i, i ^ bits) for i in everyone])]
    ppermute x9, starting transfers between devices: 13.2 us -> 14.6 us  [along(): lax.ppermute(value, 'image', [(i, (i - PLANE * d) % devices) for i in eve...]
    ppermute x18 -> x17, starting transfers between devices: 11.8 us -> 13.1 us  [across(): return lax.ppermute(value, 'image', [(i, i ^ bits) for i in everyone])]
  transfers between devices with their start and end apart: 31 -> 30, of which waited for: 18 -> 18; matrix products, arithmetic and copies ran while one was open for 0% -> 0% of each run, Pallas kernels for 11% -> 12%
where the time goes in v5:
time: 109 us
  waiting for transfers between devices  53 us (49%)
  starting transfers between devices  32.3 us (30%)
  Pallas kernels  18.8 us (17%)
  local copies, waits for them, and re-layouts  2.4 us (2%)
  between operations  2.29 us (2%)
    ppermute x9, waiting for transfers between devices, along(): lax.ppermute(value, 'image', [(i, (i - PLANE * d) % devices) for i in eve...  33.7 us
    ppermute x17, waiting for transfers between devices, across(): return lax.ppermute(value, 'image', [(i, i ^ bits) for i in everyone])  17.2 us
    ppermute x9, starting transfers between devices, along(): lax.ppermute(value, 'image', [(i, (i - PLANE * d) % devices) for i in eve...  14.6 us
    ppermute x17, starting transfers between devices, across(): return lax.ppermute(value, 'image', [(i, i ^ bits) for i in everyone])  13.1 us
    pallas_call x4, Pallas kernels, project(): call(functools.partial(project_kernel, pieces, spots, number, own, len(ar...  9.08 us
    ppermute x4, starting transfers between devices, swap(): return lax.ppermute(value, ('groups', 'image'), pairs)  4.62 us
    pallas_call x1, Pallas kernels, local(): pl.pallas_call(functools.partial(prepare_kernel, half), out_shape=[jax.Sh...  3.55 us
    pallas_call x1, Pallas kernels, send_columns(): pl.pallas_call(functools.partial(send_kernel, half, targets), out_shape=[...  2.33 us
  transfers between devices with their start and end apart: 30, of which 18 were waited for; matrix products, arithmetic and copies ran while one was open for 0% of the time, Pallas kernels for 12%

profile of v5, /device:TPU:0, one launch (start us, length us, event | category | flops | bytes accessed | tf_op | source)
XLA Modules:
  0.0 109.2 jit_solution(5131058847833857464)
XLA Ops:
  1.9 3.6 %shard_map.119 = (bf16[272,512]{1,0:T(8,128)(2,1)}, bf16[256,512]{1,0:T(8,128)(2,1)}, bf16[256,2048]{1,0:T(8,128)(2,1)}, bf16[256,2048]{1,0:T(8,128)(2,1)}) custom-call(s32[1]{0:T(128)S(6)} %copy.28.text_ref, s32[1,1]{1,0:T(1,128)S(6)} %copy.29.image_ref, s32[1]{0:T(128)S(6)} %copy.30.tiles_ref, s32[8]{0:T(128)} %tenant_ref.1, s32[16]{0:T(128)} %page_ref.1, ...), custom_call_target="tpu_custom_call" | custom-call | tf_op jit(solution)/shard_map/pallas_call | solution.py:526
  5.5 5.1 %collective-permute-start.3 = (bf16[272,512]{1,0:T(8,128)(2,1)}, bf16[272,512]{1,0:T(8,128)(2,1)S(1)}, u32[]{:S(2)}, u32[]{:S(2)}) collective-permute-start(bf16[272,512]{1,0:T(8,128)(2,1)} %get-tuple-element.40.refs_3_.refs_1_), channel_id=1, source_target_pairs={{0,12},{1,13},{2,14},{3,15},{4,0},{5,1},{6,2},{7,3},{8,4},{9,5},{1... | collective-permute-start | bytes 835592 | tf_op jit(solution)/shard_map/ppermute | solution.py:515
  10.6 1.5 %collective-permute-start.5 = (bf16[272,512]{1,0:T(8,128)(2,1)}, bf16[272,512]{1,0:T(8,128)(2,1)S(1)}, u32[]{:S(2)}, u32[]{:S(2)}) collective-permute-start(bf16[272,512]{1,0:T(8,128)(2,1)} %get-tuple-element.40.refs_3_.refs_1_), channel_id=1, source_target_pairs={{0,2},{1,3},{2,0},{3,1},{4,6},{5,7},{6,4},{7,5},{8,10},{9,11},{10,... | collective-permute-start | bytes 835592 | tf_op jit(solution)/shard_map/ppermute | solution.py:512
  12.1 1.5 %collective-permute-start.1 = (bf16[256,2048]{1,0:T(8,128)(2,1)}, bf16[256,2048]{1,0:T(8,128)(2,1)S(1)}, u32[]{:S(2)}, u32[]{:S(2)}) collective-permute-start(bf16[256,2048]{1,0:T(8,128)(2,1)} %get-tuple-element.31), channel_id=1, source_target_pairs={{0,16},{1,17},{2,18},{3,19},{4,20},{5,21},{6,22},{7,23},{8,24},{9,... | collective-permute-start | bytes 3145736 | tf_op jit(solution)/shard_map/ppermute | solution.py:519
  13.6 2.3 %shard_map.118 = bf16[256,2048]{1,0:T(8,128)(2,1)} custom-call(bf16[256,8192]{1,0:T(8,128)(2,1)} %bitcast.18), custom_call_target="tpu_custom_call" | custom-call | bytes 2097152 | tf_op jit(solution)/shard_map/pallas_call | solution.py:200
  16.1 1.9 %collective-permute-done.3.refs_5_.refs_3_ = bf16[272,512]{1,0:T(8,128)(2,1)S(1)} collective-permute-done((bf16[272,512]{1,0:T(8,128)(2,1)}, bf16[272,512]{1,0:T(8,128)(2,1)S(1)}, u32[]{:S(2)}, u32[]{:S(2)}) %collective-permute-start.3) | collective-permute-done | bytes 278560 | tf_op jit(solution)/shard_map/ppermute | solution.py:515
  18.0 5.6 %collective-permute-done.4.refs_6_.refs_4_ = bf16[272,512]{1,0:T(8,128)(2,1)S(1)} collective-permute-done((bf16[272,512]{1,0:T(8,128)(2,1)}, bf16[272,512]{1,0:T(8,128)(2,1)S(1)}, u32[]{:S(2)}, u32[]{:S(2)}) %collective-permute-start.4) | collective-permute-done | bytes 278560 | tf_op jit(solution)/shard_map/ppermute | solution.py:515
  23.6 0.7 collective-permute-start.6
  24.4 1.6 %collective-permute-start.7 = (bf16[544,512]{1,0:T(8,128)(2,1)S(1)}, bf16[544,512]{1,0:T(8,128)(2,1)S(1)}, u32[]{:S(2)}, u32[]{:S(2)}) collective-permute-start(bf16[544,512]{1,0:T(8,128)(2,1)S(1)} %pad_maximum_fusion.1), channel_id=1, source_target_pairs={{0,2},{1,3},{2,0},{3,1},{4,6},{5,7},{6,4},{7,5},{8,10},{9,11},{10,... | collective-permute-start | bytes 1671176 | tf_op jit(solution)/shard_map/ppermute | solution.py:512
  25.9 12.1 %collective-permute-done.6.refs_7_.refs_5_ = bf16[272,512]{1,0:T(8,128)(2,1)S(1)} collective-permute-done((bf16[272,512]{1,0:T(8,128)(2,1)S(1)}, bf16[272,512]{1,0:T(8,128)(2,1)S(1)}, u32[]{:S(2)}, u32[]{:S(2)}) %collective-permute-start.6) | collective-permute-done | bytes 278560 | tf_op jit(solution)/shard_map/ppermute | solution.py:515
  38.1 1.6 %collective-permute-start.11 = (bf16[528,512]{1,0:T(8,128)(2,1)S(1)}, bf16[528,512]{1,0:T(8,128)(2,1)S(1)}, u32[]{:S(2)}, u32[]{:S(2)}) collective-permute-start(bf16[528,512]{1,0:T(8,128)(2,1)S(1)} %pad_maximum_fusion.2), channel_id=1, source_target_pairs={{0,2},{1,3},{2,0},{3,1},{4,6},{5,7},{6,4},{7,5},{8,10},{9,11},{10,... | collective-permute-start | bytes 1622024 | tf_op jit(solution)/shard_map/ppermute | solution.py:512
  39.6 2.8 %collective-permute-start.8 = (bf16[256,512]{1,0:T(8,128)(2,1)S(1)}, bf16[256,512]{1,0:T(8,128)(2,1)S(1)}, u32[]{:S(2)}, u32[]{:S(2)}) collective-permute-start(bf16[256,512]{1,0:T(8,128)(2,1)S(1)} %copy-done.3), channel_id=1, source_target_pairs={{0,12},{1,13},{2,14},{3,15},{4,0},{5,1},{6,2},{7,3},{8,4},{9,5},{1... | collective-permute-start | bytes 786440 | tf_op jit(solution)/shard_map/ppermute | solution.py:515
  42.5 6.8 %collective-permute-done.8.refs_6_ = bf16[256,512]{1,0:T(8,128)(2,1)S(1)} collective-permute-done((bf16[256,512]{1,0:T(8,128)(2,1)S(1)}, bf16[256,512]{1,0:T(8,128)(2,1)S(1)}, u32[]{:S(2)}, u32[]{:S(2)}) %collective-permute-start.8) | collective-permute-done | bytes 262176 | tf_op jit(solution)/shard_map/ppermute | solution.py:515
  49.2 4.0 %collective-permute-done.9.refs_7_ = bf16[256,512]{1,0:T(8,128)(2,1)S(1)} collective-permute-done((bf16[256,512]{1,0:T(8,128)(2,1)S(1)}, bf16[256,512]{1,0:T(8,128)(2,1)S(1)}, u32[]{:S(2)}, u32[]{:S(2)}) %collective-permute-start.9) | collective-permute-done | bytes 262176 | tf_op jit(solution)/shard_map/ppermute | solution.py:515
  53.6 2.2 %copy-done = bf16[1,256,8192]{2,1,0:T(8,128)(2,1)S(1)} copy-done((bf16[1,256,8192]{2,1,0:T(8,128)(2,1)S(1)}, bf16[1,256,8192]{2,1,0:T(8,128)(2,1)}, u32[]{:S(2)}) %copy-start) | copy-done | bytes 4194328
  55.7 3.1 %shard_map.120.mine_ref = f32[3,256,512]{2,1,0:T(8,128)S(1)} custom-call(bf16[256,8192]{1,0:T(8,128)(2,1)S(1)} %bitcast.19, bf16[256,2048]{1,0:T(8,128)(2,1)S(1)} %collective-permute-done.refs_1_, bf16[256,2048]{1,0:T(8,128)(2,1)S(1)} %collective-permute-done.1.refs_2_, bf16[272,512]{1,0:T(8,128)(2,1)S(1)} %copy-done.2, ...), custom_call_target="tpu_custom_call" | custom-call | flops 1610612736 | bytes 5242880 | tf_op jit(solution)/shard_map/pallas_call | solution.py:297
  58.9 1.2 %shard_map.121 = f32[1,256,512]{2,1,0:T(8,128)S(1)} custom-call(bf16[256,2048]{1,0:T(8,128)(2,1)S(1)} %collective-permute-done.2.refs_0_.refs_3_, bf16[272,512]{1,0:T(8,128)(2,1)S(1)} %copy-done.2, bf16[272,512]{1,0:T(8,128)(2,1)S(1)} %collective-permute-done.5.refs_4_.refs_2_, bf16[272,512]{1,0:T(8,128)(2,1)S(1)} %collective-permute-done.3.refs_5_.refs_3_, ...), custom_call_target="tpu_custom_call" | custom-call | flops 536870912 | bytes 3145728 | tf_op jit(solution)/shard_map/pallas_call | solution.py:297
  60.5 0.5 collective-permute-start.18
  61.1 1.1 collective-permute-done.12
  62.6 1.5 %collective-permute-start.14 = (f32[256,512]{1,0:T(8,128)S(1)}, f32[256,512]{1,0:T(8,128)S(1)}, u32[]{:S(2)}, u32[]{:S(2)}) collective-permute-start(f32[256,512]{1,0:T(8,128)S(1)} %fusion.1), channel_id=1, source_target_pairs={{0,16},{1,17},{2,18},{3,19},{4,20},{5,21},{6,22},{7,23},{8,24},{9,... | collective-permute-start | bytes 1572872 | tf_op jit(solution)/shard_map/ppermute | solution.py:519
  64.1 0.4 shard_map.122
  64.6 2.6 %collective-permute-start.16 = (bf16[8,1,16,512]{3,2,1,0:T(8,128)(2,1)S(1)}, bf16[8,1,16,512]{3,2,1,0:T(8,128)(2,1)S(1)}, u32[]{:S(2)}, u32[]{:S(2)}) collective-permute-start(bf16[8,1,16,512]{3,2,1,0:T(8,128)(2,1)S(1)} %get-tuple-element.75), channel_id=1, source_target_pairs={{0,8},{1,9},{2,10},{3,11},{4,12},{5,13},{6,14},{7,15},{8,0},{9,1},... | collective-permute-start | bytes 393224 | tf_op jit(solution)/shard_map/ppermute | solution.py:512
  67.2 0.5 collective-permute-start.13
  67.7 6.0 %collective-permute-done.16 = bf16[8,1,16,512]{3,2,1,0:T(8,128)(2,1)S(1)} collective-permute-done((bf16[8,1,16,512]{3,2,1,0:T(8,128)(2,1)S(1)}, bf16[8,1,16,512]{3,2,1,0:T(8,128)(2,1)S(1)}, u32[]{:S(2)}, u32[]{:S(2)}) %collective-permute-start.16) | collective-permute-done | bytes 131104 | tf_op jit(solution)/shard_map/ppermute | solution.py:512
  73.7 0.8 collective-permute-start.17
  74.5 0.7 collective-permute-done.18.refs_9_
  75.3 3.7 %shard_map.123.refs_5_ = f32[4,256,512]{2,1,0:T(8,128)S(1)} custom-call(bf16[256,8192]{1,0:T(8,128)(2,1)S(1)} %bitcast.20, bf16[256,2048]{1,0:T(8,128)(2,1)S(1)} %collective-permute-done.refs_1_, bf16[256,2048]{1,0:T(8,128)(2,1)S(1)} %collective-permute-done.1.refs_2_, bf16[256,2048]{1,0:T(8,128)(2,1)S(1)} %collective-permute-done.2.refs_0_.refs_3_, ...), custom_call_target="tpu_custom_call" | custom-call | flops 1879048192 | bytes 5505024 | tf_op jit(solution)/shard_map/pallas_call | solution.py:297
  78.9 1.2 %collective-permute-done.13.refs_4_ = bf16[256,512]{1,0:T(8,128)(2,1)S(1)} collective-permute-done((bf16[256,512]{1,0:T(8,128)(2,1)S(1)}, bf16[256,512]{1,0:T(8,128)(2,1)S(1)}, u32[]{:S(2)}, u32[]{:S(2)}) %collective-permute-start.13) | collective-permute-done | bytes 262176 | tf_op jit(solution)/shard_map/ppermute | solution.py:512
  80.2 1.1 shard_map.124.mine_ref
  81.5 0.6 collective-permute-start.23
  82.2 0.6 collective-permute-start.21
  82.8 1.4 %collective-permute-done.19.core_ref = f32[2,256,512]{2,1,0:T(8,128)S(1)} collective-permute-done((f32[2,256,512]{2,1,0:T(8,128)S(1)}, f32[2,256,512]{2,1,0:T(8,128)S(1)}, u32[]{:S(2)}, u32[]{:S(2)}) %collective-permute-start.19) | collective-permute-done | bytes 1048608 | tf_op jit(solution)/shard_map/ppermute | solution.py:512
  84.2 1.6 %collective-permute-start.20 = (bf16[256,512]{1,0:T(8,128)(2,1)S(1)}, bf16[256,512]{1,0:T(8,128)(2,1)S(1)}, u32[]{:S(2)}, u32[]{:S(2)}) collective-permute-start(bf16[256,512]{1,0:T(8,128)(2,1)S(1)} %fusion.2), channel_id=1, source_target_pairs={{0,16},{1,17},{2,18},{3,19},{4,20},{5,21},{6,22},{7,23},{8,24},{9,... | collective-permute-start | bytes 786440 | tf_op jit(solution)/shard_map/ppermute | solution.py:519
  85.8 1.8 %collective-permute-done.21 = bf16[2,4,16,512]{3,2,1,0:T(8,128)(2,1)S(1)} collective-permute-done((bf16[2,4,16,512]{3,2,1,0:T(8,128)(2,1)S(1)}, bf16[2,4,16,512]{3,2,1,0:T(8,128)(2,1)S(1)}, u32[]{:S(2)}, u32[]{:S(2)}) %collective-permute-start.21) | collective-permute-done | bytes 131104 | tf_op jit(solution)/shard_map/ppermute | solution.py:512
  87.8 0.7 shard_map.126
  88.5 0.6 collective-permute-done.22
  89.1 1.5 %shard_map.125.lowrank_ref = f32[256,512]{1,0:T(8,128)S(1)} custom-call(bf16[256,512]{1,0:T(8,128)(2,1)S(1)} %constant_dynamic-update-slice_fusion.8.extras_ref, bf16[256,8192]{1,0:T(8,128)(2,1)S(1)} %bitcast.22, bf16[16,16,512]{2,1,0:T(8,128)(2,1)S(1)} %maximum_bitcast_fusion.down_ref, bf16[16,16,512]{2,1,0:T(8,128)(2,1)S(1)} %copy-done.5), custom_call_target="tpu_custom_call" | custom-call | bytes 4194304 | tf_op jit(solution)/shard_map/pallas_call | solution.py:592
  90.6 2.0 %collective-permute-done.20.pair_ref = bf16[256,512]{1,0:T(8,128)(2,1)S(1)} collective-permute-done((bf16[256,512]{1,0:T(8,128)(2,1)S(1)}, bf16[256,512]{1,0:T(8,128)(2,1)S(1)}, u32[]{:S(2)}, u32[]{:S(2)}) %collective-permute-start.20) | collective-permute-done | bytes 262176 | tf_op jit(solution)/shard_map/ppermute | solution.py:519
  93.1 0.6 collective-permute-start.25
  93.7 1.3 %collective-permute-start.26 = (f32[4,40,128]{2,1,0:T(8,128)S(1)}, f32[4,40,128]{2,1,0:T(8,128)S(1)}, u32[]{:S(2)}, u32[]{:S(2)}) collective-permute-start(f32[4,40,128]{2,1,0:T(8,128)S(1)} %get-tuple-element.52), channel_id=1, source_target_pairs={{0,3},{1,2},{2,1},{3,0},{4,7},{5,6},{6,5},{7,4},{8,11},{9,10},{10,... | collective-permute-start | bytes 245768 | tf_op jit(solution)/shard_map/ppermute | solution.py:512
  95.0 3.4 %collective-permute-done.25.refs_2_ = f32[4,40,128]{2,1,0:T(8,128)S(1)} collective-permute-done((f32[4,40,128]{2,1,0:T(8,128)S(1)}, f32[4,40,128]{2,1,0:T(8,128)S(1)}, u32[]{:S(2)}, u32[]{:S(2)}) %collective-permute-start.25) | collective-permute-done | bytes 81952 | tf_op jit(solution)/shard_map/ppermute | solution.py:512
  98.4 0.8 collective-permute-done.26.refs_3_
  99.4 2.3 %collective-permute-start.27 = (f32[40,128]{1,0:T(8,128)S(1)}, f32[40,128]{1,0:T(8,128)S(1)}, u32[]{:S(2)}, u32[]{:S(2)}) collective-permute-start(f32[40,128]{1,0:T(8,128)S(1)} %get-tuple-element.54), channel_id=1, source_target_pairs={{0,4},{1,5},{2,6},{3,7},{4,8},{5,9},{6,10},{7,11},{8,12},{9,13},{1... | collective-permute-start | bytes 61448 | tf_op jit(solution)/shard_map/ppermute | solution.py:515
  101.7 2.9 %collective-permute-start.28 = (f32[40,128]{1,0:T(8,128)S(1)}, f32[40,128]{1,0:T(8,128)S(1)}, u32[]{:S(2)}, u32[]{:S(2)}) collective-permute-start(f32[40,128]{1,0:T(8,128)S(1)} %get-tuple-element.55), channel_id=1, source_target_pairs={{0,8},{1,9},{2,10},{3,11},{4,12},{5,13},{6,14},{7,15},{8,0},{9,1},... | collective-permute-start | bytes 61448 | tf_op jit(solution)/shard_map/ppermute | solution.py:515
  104.7 0.4 collective-permute-start.29
  105.1 1.0 collective-permute-done.27.refs_1_
  106.4 2.0 %collective-permute-done.29.refs_3_ = f32[40,128]{1,0:T(8,128)S(1)} collective-permute-done((f32[40,128]{1,0:T(8,128)S(1)}, f32[40,128]{1,0:T(8,128)S(1)}, u32[]{:S(2)}, u32[]{:S(2)}) %collective-permute-start.29) | collective-permute-done | bytes 20512 | tf_op jit(solution)/shard_map/ppermute | solution.py:515
  108.4 0.7 shard_map.129
  (63 shorter events, 2.8 us)
Async XLA Ops:
  5.5 12.5 %collective-permute-start.3 = (bf16[272,512]{1,0:T(8,128)(2,1)}, bf16[272,512]{1,0:T(8,128)(2,1)S(1)}, u32[]{:S(2)}, u32[]{:S(2)}) collective-permute-start(bf16[272,512]{1,0:T(8,128)(2,1)} %get-tuple-element.40.refs_3_.refs_1_), channel_id=1, source_target_pairs={{0,12},{1,13},{2,14},{3,15},{4,0},{5,1},{6,2},{7,3},{8,4},{9,5},{1... | collective-permute-start | bytes 835592 | tf_op jit(solution)/shard_map/ppermute | solution.py:515
  10.6 13.0 %collective-permute-start.4 = (bf16[272,512]{1,0:T(8,128)(2,1)}, bf16[272,512]{1,0:T(8,128)(2,1)S(1)}, u32[]{:S(2)}, u32[]{:S(2)}) collective-permute-start(bf16[272,512]{1,0:T(8,128)(2,1)} %get-tuple-element.40.refs_3_.refs_1_), channel_id=1, source_target_pairs={{0,4},{1,5},{2,6},{3,7},{4,8},{5,9},{6,10},{7,11},{8,12},{9,13},{1... | collective-permute-start | bytes 835592 | tf_op jit(solution)/shard_map/ppermute | solution.py:515
  10.6 13.0 %collective-permute-start.5 = (bf16[272,512]{1,0:T(8,128)(2,1)}, bf16[272,512]{1,0:T(8,128)(2,1)S(1)}, u32[]{:S(2)}, u32[]{:S(2)}) collective-permute-start(bf16[272,512]{1,0:T(8,128)(2,1)} %get-tuple-element.40.refs_3_.refs_1_), channel_id=1, source_target_pairs={{0,2},{1,3},{2,0},{3,1},{4,6},{5,7},{6,4},{7,5},{8,10},{9,11},{10,... | collective-permute-start | bytes 835592 | tf_op jit(solution)/shard_map/ppermute | solution.py:512
  12.1 3.9 %copy-start.2 = (bf16[272,512]{1,0:T(8,128)(2,1)S(1)}, bf16[272,512]{1,0:T(8,128)(2,1)}, u32[]{:S(2)}) copy-start(bf16[272,512]{1,0:T(8,128)(2,1)} %get-tuple-element.40.refs_3_.refs_1_) | copy-start | bytes 835588
  12.1 25.9 %copy-start.3 = (bf16[256,512]{1,0:T(8,128)(2,1)S(1)}, bf16[256,512]{1,0:T(8,128)(2,1)}, u32[]{:S(2)}) copy-start(bf16[256,512]{1,0:T(8,128)(2,1)} %get-tuple-element.45.refs_4_) | copy-start | bytes 786436
  12.1 41.4 %collective-permute-start.1 = (bf16[256,2048]{1,0:T(8,128)(2,1)}, bf16[256,2048]{1,0:T(8,128)(2,1)S(1)}, u32[]{:S(2)}, u32[]{:S(2)}) collective-permute-start(bf16[256,2048]{1,0:T(8,128)(2,1)} %get-tuple-element.31), channel_id=1, source_target_pairs={{0,16},{1,17},{2,18},{3,19},{4,20},{5,21},{6,22},{7,23},{8,24},{9,... | collective-permute-start | bytes 3145736 | tf_op jit(solution)/shard_map/ppermute | solution.py:519
  16.0 23.7 %collective-permute-start = (bf16[256,2048]{1,0:T(8,128)(2,1)}, bf16[256,2048]{1,0:T(8,128)(2,1)S(1)}, u32[]{:S(2)}, u32[]{:S(2)}) collective-permute-start(bf16[256,2048]{1,0:T(8,128)(2,1)} %shard_map.118), channel_id=1, source_target_pairs={{0,1},{1,0},{2,3},{3,2},{4,5},{5,4},{6,7},{7,6},{8,9},{9,8},{10,11... | collective-permute-start | bytes 3145736 | tf_op jit(solution)/shard_map/ppermute | solution.py:512
  18.0 40.9 %collective-permute-start.2 = (bf16[256,2048]{1,0:T(8,128)(2,1)}, bf16[256,2048]{1,0:T(8,128)(2,1)S(1)}, u32[]{:S(2)}, u32[]{:S(2)}) collective-permute-start(bf16[256,2048]{1,0:T(8,128)(2,1)} %get-tuple-element.32), channel_id=1, source_target_pairs={{0,17},{1,16},{2,19},{3,18},{4,21},{5,20},{6,23},{7,22},{8,25},{9,... | collective-permute-start | bytes 3145736 | tf_op jit(solution)/shard_map/ppermute | solution.py:519
  23.6 14.4 %collective-permute-start.6 = (bf16[272,512]{1,0:T(8,128)(2,1)S(1)}, bf16[272,512]{1,0:T(8,128)(2,1)S(1)}, u32[]{:S(2)}, u32[]{:S(2)}) collective-permute-start(bf16[272,512]{1,0:T(8,128)(2,1)S(1)} %copy-done.2), channel_id=1, source_target_pairs={{0,8},{1,9},{2,10},{3,11},{4,12},{5,13},{6,14},{7,15},{8,0},{9,1},... | collective-permute-start | bytes 835592 | tf_op jit(solution)/shard_map/ppermute | solution.py:515
  24.4 13.7 %collective-permute-start.7 = (bf16[544,512]{1,0:T(8,128)(2,1)S(1)}, bf16[544,512]{1,0:T(8,128)(2,1)S(1)}, u32[]{:S(2)}, u32[]{:S(2)}) collective-permute-start(bf16[544,512]{1,0:T(8,128)(2,1)S(1)} %pad_maximum_fusion.1), channel_id=1, source_target_pairs={{0,2},{1,3},{2,0},{3,1},{4,6},{5,7},{6,4},{7,5},{8,10},{9,11},{10,... | collective-permute-start | bytes 1671176 | tf_op jit(solution)/shard_map/ppermute | solution.py:512
  38.1 15.5 %collective-permute-start.11 = (bf16[528,512]{1,0:T(8,128)(2,1)S(1)}, bf16[528,512]{1,0:T(8,128)(2,1)S(1)}, u32[]{:S(2)}, u32[]{:S(2)}) collective-permute-start(bf16[528,512]{1,0:T(8,128)(2,1)S(1)} %pad_maximum_fusion.2), channel_id=1, source_target_pairs={{0,2},{1,3},{2,0},{3,1},{4,6},{5,7},{6,4},{7,5},{8,10},{9,11},{10,... | collective-permute-start | bytes 1622024 | tf_op jit(solution)/shard_map/ppermute | solution.py:512
  39.6 9.6 %collective-permute-start.8 = (bf16[256,512]{1,0:T(8,128)(2,1)S(1)}, bf16[256,512]{1,0:T(8,128)(2,1)S(1)}, u32[]{:S(2)}, u32[]{:S(2)}) collective-permute-start(bf16[256,512]{1,0:T(8,128)(2,1)S(1)} %copy-done.3), channel_id=1, source_target_pairs={{0,12},{1,13},{2,14},{3,15},{4,0},{5,1},{6,2},{7,3},{8,4},{9,5},{1... | collective-permute-start | bytes 786440 | tf_op jit(solution)/shard_map/ppermute | solution.py:515
  42.5 10.8 %collective-permute-start.9 = (bf16[256,512]{1,0:T(8,128)(2,1)S(1)}, bf16[256,512]{1,0:T(8,128)(2,1)S(1)}, u32[]{:S(2)}, u32[]{:S(2)}) collective-permute-start(bf16[256,512]{1,0:T(8,128)(2,1)S(1)} %copy-done.3), channel_id=1, source_target_pairs={{0,4},{1,5},{2,6},{3,7},{4,8},{5,9},{6,10},{7,11},{8,12},{9,13},{1... | collective-permute-start | bytes 786440 | tf_op jit(solution)/shard_map/ppermute | solution.py:515
  53.2 13.9 %collective-permute-start.10 = (bf16[256,512]{1,0:T(8,128)(2,1)S(1)}, bf16[256,512]{1,0:T(8,128)(2,1)S(1)}, u32[]{:S(2)}, u32[]{:S(2)}) collective-permute-start(bf16[256,512]{1,0:T(8,128)(2,1)S(1)} %copy-done.3), channel_id=1, source_target_pairs={{0,8},{1,9},{2,10},{3,11},{4,12},{5,13},{6,14},{7,15},{8,0},{9,1},... | collective-permute-start | bytes 786440 | tf_op jit(solution)/shard_map/ppermute | solution.py:515
  53.6 2.2 %copy-start = (bf16[1,256,8192]{2,1,0:T(8,128)(2,1)S(1)}, bf16[1,256,8192]{2,1,0:T(8,128)(2,1)}, u32[]{:S(2)}) copy-start(bf16[1,256,8192]{2,1,0:T(8,128)(2,1)} %param.12) | copy-start | bytes 12582916
  58.9 16.4 %copy-start.1 = (bf16[1,256,8192]{2,1,0:T(8,128)(2,1)S(1)}, bf16[1,256,8192]{2,1,0:T(8,128)(2,1)}, u32[]{:S(2)}) copy-start(bf16[1,256,8192]{2,1,0:T(8,128)(2,1)} %param.12) | copy-start | bytes 12582916
  60.1 4.0 %copy-start.4 = (bf16[512,256]{1,0:T(8,128)(2,1)S(1)}, bf16[512,256]{1,0:T(8,128)(2,1)}, u32[]{:S(2)}) copy-start(bf16[512,256]{1,0:T(8,128)(2,1)} %down_ref.1) | copy-start | bytes 786436
  60.1 2.0 %collective-permute-start.12 = (f32[256,512]{1,0:T(8,128)S(1)}, f32[256,512]{1,0:T(8,128)S(1)}, u32[]{:S(2)}, u32[]{:S(2)}) collective-permute-start(f32[256,512]{1,0:T(8,128)S(1)} %bitcast.23), channel_id=1, source_target_pairs={{0,1},{1,0},{2,3},{3,2},{4,5},{5,4},{6,7},{7,6},{8,9},{9,8},{10,11... | collective-permute-start | bytes 1572872 | tf_op jit(solution)/shard_map/ppermute | solution.py:512
  60.5 14.8 %collective-permute-start.18 = (bf16[512,512]{1,0:T(8,128)(2,1)S(1)}, bf16[512,512]{1,0:T(8,128)(2,1)S(1)}, u32[]{:S(2)}, u32[]{:S(2)}) collective-permute-start(bf16[512,512]{1,0:T(8,128)(2,1)S(1)} %pad_maximum_fusion.3), channel_id=1, source_target_pairs={{0,2},{1,3},{2,0},{3,1},{4,6},{5,7},{6,4},{7,5},{8,10},{9,11},{10,... | collective-permute-start | bytes 1572872 | tf_op jit(solution)/shard_map/ppermute | solution.py:512
  62.2 1.9 %collective-permute-start.15 = (bf16[128,512]{1,0:T(8,128)(2,1)S(1)}, bf16[128,512]{1,0:T(8,128)(2,1)S(1)}, u32[]{:S(2)}, u32[]{:S(2)}) collective-permute-start(bf16[128,512]{1,0:T(8,128)(2,1)S(1)} %get-tuple-element.42), channel_id=1, source_target_pairs={{0,1},{1,0},{2,3},{3,2},{4,5},{5,4},{6,7},{7,6},{8,9},{9,8},{10,11... | collective-permute-start | bytes 393224 | tf_op jit(solution)/shard_map/ppermute | solution.py:512
  62.6 17.6 %collective-permute-start.14 = (f32[256,512]{1,0:T(8,128)S(1)}, f32[256,512]{1,0:T(8,128)S(1)}, u32[]{:S(2)}, u32[]{:S(2)}) collective-permute-start(f32[256,512]{1,0:T(8,128)S(1)} %fusion.1), channel_id=1, source_target_pairs={{0,16},{1,17},{2,18},{3,19},{4,20},{5,21},{6,22},{7,23},{8,24},{9,... | collective-permute-start | bytes 1572872 | tf_op jit(solution)/shard_map/ppermute | solution.py:519
  64.6 9.2 %collective-permute-start.16 = (bf16[8,1,16,512]{3,2,1,0:T(8,128)(2,1)S(1)}, bf16[8,1,16,512]{3,2,1,0:T(8,128)(2,1)S(1)}, u32[]{:S(2)}, u32[]{:S(2)}) collective-permute-start(bf16[8,1,16,512]{3,2,1,0:T(8,128)(2,1)S(1)} %get-tuple-element.75), channel_id=1, source_target_pairs={{0,8},{1,9},{2,10},{3,11},{4,12},{5,13},{6,14},{7,15},{8,0},{9,1},... | collective-permute-start | bytes 393224 | tf_op jit(solution)/shard_map/ppermute | solution.py:512
  67.2 13.0 %collective-permute-start.13 = (bf16[256,512]{1,0:T(8,128)(2,1)S(1)}, bf16[256,512]{1,0:T(8,128)(2,1)S(1)}, u32[]{:S(2)}, u32[]{:S(2)}) collective-permute-start(bf16[256,512]{1,0:T(8,128)(2,1)S(1)} %collective-permute-done.10.refs_8_), channel_id=1, source_target_pairs={{0,2},{1,3},{2,0},{3,1},{4,6},{5,7},{6,4},{7,5},{8,10},{9,11},{10,... | collective-permute-start | bytes 786440 | tf_op jit(solution)/shard_map/ppermute | solution.py:512
  73.7 6.4 %collective-permute-start.17 = (bf16[4,2,16,512]{3,2,1,0:T(8,128)(2,1)S(1)}, bf16[4,2,16,512]{3,2,1,0:T(8,128)(2,1)S(1)}, u32[]{:S(2)}, u32[]{:S(2)}) collective-permute-start(bf16[4,2,16,512]{3,2,1,0:T(8,128)(2,1)S(1)} %fusion.5), channel_id=1, source_target_pairs={{0,4},{1,5},{2,6},{3,7},{4,0},{5,1},{6,2},{7,3},{8,12},{9,13},{10,... | collective-permute-start | bytes 393224 | tf_op jit(solution)/shard_map/ppermute | solution.py:512
  81.4 2.7 %collective-permute-start.19 = (f32[2,256,512]{2,1,0:T(8,128)S(1)}, f32[2,256,512]{2,1,0:T(8,128)S(1)}, u32[]{:S(2)}, u32[]{:S(2)}) collective-permute-start(f32[2,256,512]{2,1,0:T(8,128)S(1)} %pad_maximum_fusion), channel_id=1, source_target_pairs={{0,1},{1,0},{2,3},{3,2},{4,5},{5,4},{6,7},{7,6},{8,9},{9,8},{10,11... | collective-permute-start | bytes 3145736 | tf_op jit(solution)/shard_map/ppermute | solution.py:512
  81.5 6.2 %copy-start.6 = (f32[128]{0:T(128)S(1)}, f32[128]{0:T(128)}, u32[]{:S(2)}) copy-start(f32[128]{0:T(128)} %param.17) | copy-start | bytes 1540
  81.5 6.2 %collective-permute-start.23 = (f32[256,512]{1,0:T(8,128)S(1)}, f32[256,512]{1,0:T(8,128)S(1)}, u32[]{:S(2)}, u32[]{:S(2)}) collective-permute-start(f32[256,512]{1,0:T(8,128)S(1)} %slice_bitcast_fusion), channel_id=1, source_target_pairs={{0,1},{1,0},{2,3},{3,2},{4,5},{5,4},{6,7},{7,6},{8,9},{9,8},{10,11... | collective-permute-start | bytes 1572872 | tf_op jit(solution)/shard_map/ppermute | solution.py:512
  82.2 5.5 %collective-permute-start.21 = (bf16[2,4,16,512]{3,2,1,0:T(8,128)(2,1)S(1)}, bf16[2,4,16,512]{3,2,1,0:T(8,128)(2,1)S(1)}, u32[]{:S(2)}, u32[]{:S(2)}) collective-permute-start(bf16[2,4,16,512]{3,2,1,0:T(8,128)(2,1)S(1)} %get-tuple-element.74), channel_id=1, source_target_pairs={{0,2},{1,3},{2,0},{3,1},{4,6},{5,7},{6,4},{7,5},{8,10},{9,11},{10,... | collective-permute-start | bytes 393224 | tf_op jit(solution)/shard_map/ppermute | solution.py:512
  84.2 8.4 %collective-permute-start.20 = (bf16[256,512]{1,0:T(8,128)(2,1)S(1)}, bf16[256,512]{1,0:T(8,128)(2,1)S(1)}, u32[]{:S(2)}, u32[]{:S(2)}) collective-permute-start(bf16[256,512]{1,0:T(8,128)(2,1)S(1)} %fusion.2), channel_id=1, source_target_pairs={{0,16},{1,17},{2,18},{3,19},{4,20},{5,21},{6,22},{7,23},{8,24},{9,... | collective-permute-start | bytes 786440 | tf_op jit(solution)/shard_map/ppermute | solution.py:519
  87.7 1.4 %collective-permute-start.22 = (bf16[1,8,16,512]{3,2,1,0:T(8,128)(2,1)S(1)}, bf16[1,8,16,512]{3,2,1,0:T(8,128)(2,1)S(1)}, u32[]{:S(2)}, u32[]{:S(2)}) collective-permute-start(bf16[1,8,16,512]{3,2,1,0:T(8,128)(2,1)S(1)} %get-tuple-element.72), channel_id=1, source_target_pairs={{0,1},{1,0},{2,3},{3,2},{4,5},{5,4},{6,7},{7,6},{8,9},{9,8},{10,11... | collective-permute-start | bytes 393224 | tf_op jit(solution)/shard_map/ppermute | solution.py:512
  87.8 1.3 %copy-start.5 = (bf16[16,16,512]{2,1,0:T(8,128)(2,1)S(1)}, bf16[16,16,512]{2,1,0:T(8,128)(2,1)}, u32[]{:S(2)}) copy-start(bf16[16,16,512]{2,1,0:T(8,128)(2,1)} %up_ref.1) | copy-start | bytes 786436
  93.0 1.9 %collective-permute-start.24 = (f32[4,40,128]{2,1,0:T(8,128)S(1)}, f32[4,40,128]{2,1,0:T(8,128)S(1)}, u32[]{:S(2)}, u32[]{:S(2)}) collective-permute-start(f32[4,40,128]{2,1,0:T(8,128)S(1)} %get-tuple-element.50), channel_id=1, source_target_pairs={{0,1},{1,0},{2,3},{3,2},{4,5},{5,4},{6,7},{7,6},{8,9},{9,8},{10,11... | collective-permute-start | bytes 245768 | tf_op jit(solution)/shard_map/ppermute | solution.py:512
  93.1 5.3 %collective-permute-start.25 = (f32[4,40,128]{2,1,0:T(8,128)S(1)}, f32[4,40,128]{2,1,0:T(8,128)S(1)}, u32[]{:S(2)}, u32[]{:S(2)}) collective-permute-start(f32[4,40,128]{2,1,0:T(8,128)S(1)} %get-tuple-element.51), channel_id=1, source_target_pairs={{0,2},{1,3},{2,0},{3,1},{4,6},{5,7},{6,4},{7,5},{8,10},{9,11},{10,... | collective-permute-start | bytes 245768 | tf_op jit(solution)/shard_map/ppermute | solution.py:512
  93.7 5.6 %collective-permute-start.26 = (f32[4,40,128]{2,1,0:T(8,128)S(1)}, f32[4,40,128]{2,1,0:T(8,128)S(1)}, u32[]{:S(2)}, u32[]{:S(2)}) collective-permute-start(f32[4,40,128]{2,1,0:T(8,128)S(1)} %get-tuple-element.52), channel_id=1, source_target_pairs={{0,3},{1,2},{2,1},{3,0},{4,7},{5,6},{6,5},{7,4},{8,11},{9,10},{10,... | collective-permute-start | bytes 245768 | tf_op jit(solution)/shard_map/ppermute | solution.py:512
  99.4 6.7 %collective-permute-start.27 = (f32[40,128]{1,0:T(8,128)S(1)}, f32[40,128]{1,0:T(8,128)S(1)}, u32[]{:S(2)}, u32[]{:S(2)}) collective-permute-start(f32[40,128]{1,0:T(8,128)S(1)} %get-tuple-element.54), channel_id=1, source_target_pairs={{0,4},{1,5},{2,6},{3,7},{4,8},{5,9},{6,10},{7,11},{8,12},{9,13},{1... | collective-permute-start | bytes 61448 | tf_op jit(solution)/shard_map/ppermute | solution.py:515
  101.7 4.7 %collective-permute-start.28 = (f32[40,128]{1,0:T(8,128)S(1)}, f32[40,128]{1,0:T(8,128)S(1)}, u32[]{:S(2)}, u32[]{:S(2)}) collective-permute-start(f32[40,128]{1,0:T(8,128)S(1)} %get-tuple-element.55), channel_id=1, source_target_pairs={{0,8},{1,9},{2,10},{3,11},{4,12},{5,13},{6,14},{7,15},{8,0},{9,1},... | collective-permute-start | bytes 61448 | tf_op jit(solution)/shard_map/ppermute | solution.py:515
  104.7 3.8 %collective-permute-start.29 = (f32[40,128]{1,0:T(8,128)S(1)}, f32[40,128]{1,0:T(8,128)S(1)}, u32[]{:S(2)}, u32[]{:S(2)}) collective-permute-start(f32[40,128]{1,0:T(8,128)S(1)} %get-tuple-element.56), channel_id=1, source_target_pairs={{0,12},{1,13},{2,14},{3,15},{4,0},{5,1},{6,2},{7,3},{8,4},{9,5},{1... | collective-permute-start | bytes 61448 | tf_op jit(solution)/shard_map/ppermute | solution.py:515

commit v6 on v5

--- a/solution.py
+++ b/solution.py
@@ -141,6 +141,7 @@
 EXTRA = 16
 WINDOW = 4
 MESSAGE = 40
+NARROW = 48
 IMAGES = 4
 
 
@@ -443,7 +444,20 @@
             for j in range(1, WINDOW):
                 good = jnp.where(s == j, match[j], jnp.where(good, 1.0, 0.0)) > 0.5
             good = inside & good
-            out_ref[z] = jnp.where(good, numerators[s], empty)
+            block = jnp.where(good, numerators[s], empty)
+            if k == 0:
+                out_ref[z] = block
+                continue
+            out_ref[z, 0:rows, :] = block[0:rows].astype(jnp.bfloat16)
+            thirds = jnp.zeros((NARROW - rows, HEAD), jnp.float32)
+            at = lax.broadcasted_iota(jnp.int32, thirds.shape, 0)
+            for j in range(2):
+                rest = block[rows + j : rows + j + 1]
+                for i in range(3):
+                    part = rest.astype(jnp.bfloat16).astype(jnp.float32)
+                    thirds = jnp.where(at == 3 * j + i, part, thirds)
+                    rest = rest - part
+            out_ref[z, rows:NARROW, :] = thirds.astype(jnp.bfloat16)
 
 
 def merge(blocks):
@@ -460,12 +474,24 @@
     return numerator, top, total, eye
 
 
+def widen(block):
+    rows = 8 * KV_HEADS
+    if block.shape[0] == MESSAGE:
+        return block
+    terms = block[rows:NARROW].astype(jnp.float32)
+    line = lax.broadcasted_iota(jnp.int32, (8, HEAD), 0)
+    top = terms[0:1] + terms[1:2] + terms[2:3]
+    total = terms[3:4] + terms[4:5] + terms[5:6]
+    stats = jnp.where(line == 0, top, jnp.where(line == 1, total, 0.0))
+    return jnp.concatenate([block[0:rows].astype(jnp.float32), stats], axis=0)
+
+
 def plane_kernel(steps, *refs):
     in_refs, out_refs, merged = refs[:PLANE], refs[PLANE : PLANE + steps], refs[-1]
     rows = 8 * KV_HEADS
     line = lax.broadcasted_iota(jnp.int32, (8, HEAD), 0)
     for z in range(steps):
-        numerator, top, total, _ = merge([ref[z] for ref in in_refs])
+        numerator, top, total, _ = merge([widen(ref[z]) for ref in in_refs])
         merged[z, 0:rows, :] = numerator
         merged[z, rows:MESSAGE, :] = jnp.where(line == 0, top, jnp.where(line == 1, total, 0.0))
     for d, out_ref in enumerate(out_refs):
@@ -617,9 +643,10 @@
     )(keys_part, keys_core, *keys_pair, key_gain.reshape(1, HEAD), extras)
 
     message = jax.ShapeDtypeStruct((steps, MESSAGE, HEAD), jnp.float32)
+    narrow = jax.ShapeDtypeStruct((steps, NARROW, HEAD), jnp.bfloat16)
     messages = call(
         functools.partial(value_kernel, steps),
-        [message] * PLANE,
+        [message] + [narrow] * (PLANE - 1),
         whole(6),
         scratch=[pltpu.VMEM((WINDOW, MESSAGE, HEAD), jnp.float32)],
     )(values_part, values_core, values_pair, lowrank, weights, stats)

time: 109 us -> 108 us (level)
  waiting for transfers between devices: 53 us -> 51.6 us
    ppermute x17, waiting for transfers between devices: 17.2 us -> 15.8 us  [across(): return lax.ppermute(value, 'image', [(i, i ^ bits) for i in everyone])]
where the time goes in v6:
time: 108 us
  waiting for transfers between devices  51.6 us (48%)
  starting transfers between devices  32.3 us (30%)
  Pallas kernels  18.8 us (17%)
  local copies, waits for them, and re-layouts  2.4 us (2%)
  between operations  2.28 us (2%)
    ppermute x9, waiting for transfers between devices, along(): lax.ppermute(value, 'image', [(i, (i - PLANE * d) % devices) for i in eve...  33.7 us
    ppermute x17, waiting for transfers between devices, across(): return lax.ppermute(value, 'image', [(i, i ^ bits) for i in everyone])  15.8 us
    ppermute x9, starting transfers between devices, along(): lax.ppermute(value, 'image', [(i, (i - PLANE * d) % devices) for i in eve...  14.6 us
    ppermute x17, starting transfers between devices, across(): return lax.ppermute(value, 'image', [(i, i ^ bits) for i in everyone])  13.1 us
    pallas_call x4, Pallas kernels, project(): call(functools.partial(project_kernel, pieces, spots, number, own, len(ar...  9.08 us
    ppermute x4, starting transfers between devices, swap(): return lax.ppermute(value, ('groups', 'image'), pairs)  4.62 us
    pallas_call x1, Pallas kernels, local(): pl.pallas_call(functools.partial(prepare_kernel, half), out_shape=[jax.Sh...  3.55 us
    pallas_call x1, Pallas kernels, send_columns(): pl.pallas_call(functools.partial(send_kernel, half, targets), out_shape=[...  2.33 us
  transfers between devices with their start and end apart: 30, of which 18 were waited for; matrix products, arithmetic and copies ran while one was open for 0% of the time, Pallas kernels for 12%

profile of v6, /device:TPU:0, one launch (start us, length us, event | category | flops | bytes accessed | tf_op | source)
XLA Modules:
  0.0 107.8 jit_solution(3078782705440410676)
XLA Ops:
  1.9 3.6 %shard_map.119 = (bf16[272,512]{1,0:T(8,128)(2,1)}, bf16[256,512]{1,0:T(8,128)(2,1)}, bf16[256,2048]{1,0:T(8,128)(2,1)}, bf16[256,2048]{1,0:T(8,128)(2,1)}) custom-call(s32[1]{0:T(128)S(6)} %copy.28.text_ref, s32[1,1]{1,0:T(1,128)S(6)} %copy.29.image_ref, s32[1]{0:T(128)S(6)} %copy.30.tiles_ref, s32[8]{0:T(128)} %tenant_ref.1, s32[16]{0:T(128)} %page_ref.1, ...), custom_call_target="tpu_custom_call" | custom-call | tf_op jit(solution)/shard_map/pallas_call | solution.py:552
  5.5 5.1 %collective-permute-start.3 = (bf16[272,512]{1,0:T(8,128)(2,1)}, bf16[272,512]{1,0:T(8,128)(2,1)S(1)}, u32[]{:S(2)}, u32[]{:S(2)}) collective-permute-start(bf16[272,512]{1,0:T(8,128)(2,1)} %get-tuple-element.40.refs_3_.refs_1_), channel_id=1, source_target_pairs={{0,12},{1,13},{2,14},{3,15},{4,0},{5,1},{6,2},{7,3},{8,4},{9,5},{1... | collective-permute-start | bytes 835592 | tf_op jit(solution)/shard_map/ppermute | solution.py:541
  10.6 1.5 %collective-permute-start.5 = (bf16[272,512]{1,0:T(8,128)(2,1)}, bf16[272,512]{1,0:T(8,128)(2,1)S(1)}, u32[]{:S(2)}, u32[]{:S(2)}) collective-permute-start(bf16[272,512]{1,0:T(8,128)(2,1)} %get-tuple-element.40.refs_3_.refs_1_), channel_id=1, source_target_pairs={{0,2},{1,3},{2,0},{3,1},{4,6},{5,7},{6,4},{7,5},{8,10},{9,11},{10,... | collective-permute-start | bytes 835592 | tf_op jit(solution)/shard_map/ppermute | solution.py:538
  12.1 1.5 %collective-permute-start.1 = (bf16[256,2048]{1,0:T(8,128)(2,1)}, bf16[256,2048]{1,0:T(8,128)(2,1)S(1)}, u32[]{:S(2)}, u32[]{:S(2)}) collective-permute-start(bf16[256,2048]{1,0:T(8,128)(2,1)} %get-tuple-element.31), channel_id=1, source_target_pairs={{0,16},{1,17},{2,18},{3,19},{4,20},{5,21},{6,22},{7,23},{8,24},{9,... | collective-permute-start | bytes 3145736 | tf_op jit(solution)/shard_map/ppermute | solution.py:545
  13.6 2.3 %shard_map.118 = bf16[256,2048]{1,0:T(8,128)(2,1)} custom-call(bf16[256,8192]{1,0:T(8,128)(2,1)} %bitcast.18), custom_call_target="tpu_custom_call" | custom-call | bytes 2097152 | tf_op jit(solution)/shard_map/pallas_call | solution.py:201
  16.1 1.9 %collective-permute-done.3.refs_5_.refs_3_ = bf16[272,512]{1,0:T(8,128)(2,1)S(1)} collective-permute-done((bf16[272,512]{1,0:T(8,128)(2,1)}, bf16[272,512]{1,0:T(8,128)(2,1)S(1)}, u32[]{:S(2)}, u32[]{:S(2)}) %collective-permute-start.3) | collective-permute-done | bytes 278560 | tf_op jit(solution)/shard_map/ppermute | solution.py:541
  18.0 5.6 %collective-permute-done.4.refs_6_.refs_4_ = bf16[272,512]{1,0:T(8,128)(2,1)S(1)} collective-permute-done((bf16[272,512]{1,0:T(8,128)(2,1)}, bf16[272,512]{1,0:T(8,128)(2,1)S(1)}, u32[]{:S(2)}, u32[]{:S(2)}) %collective-permute-start.4) | collective-permute-done | bytes 278560 | tf_op jit(solution)/shard_map/ppermute | solution.py:541
  23.6 0.7 collective-permute-start.6
  24.4 1.6 %collective-permute-start.7 = (bf16[544,512]{1,0:T(8,128)(2,1)S(1)}, bf16[544,512]{1,0:T(8,128)(2,1)S(1)}, u32[]{:S(2)}, u32[]{:S(2)}) collective-permute-start(bf16[544,512]{1,0:T(8,128)(2,1)S(1)} %pad_maximum_fusion.1), channel_id=1, source_target_pairs={{0,2},{1,3},{2,0},{3,1},{4,6},{5,7},{6,4},{7,5},{8,10},{9,11},{10,... | collective-permute-start | bytes 1671176 | tf_op jit(solution)/shard_map/ppermute | solution.py:538
  25.9 12.1 %collective-permute-done.6.refs_7_.refs_5_ = bf16[272,512]{1,0:T(8,128)(2,1)S(1)} collective-permute-done((bf16[272,512]{1,0:T(8,128)(2,1)S(1)}, bf16[272,512]{1,0:T(8,128)(2,1)S(1)}, u32[]{:S(2)}, u32[]{:S(2)}) %collective-permute-start.6) | collective-permute-done | bytes 278560 | tf_op jit(solution)/shard_map/ppermute | solution.py:541
  38.1 1.6 %collective-permute-start.11 = (bf16[528,512]{1,0:T(8,128)(2,1)S(1)}, bf16[528,512]{1,0:T(8,128)(2,1)S(1)}, u32[]{:S(2)}, u32[]{:S(2)}) collective-permute-start(bf16[528,512]{1,0:T(8,128)(2,1)S(1)} %pad_maximum_fusion.2), channel_id=1, source_target_pairs={{0,2},{1,3},{2,0},{3,1},{4,6},{5,7},{6,4},{7,5},{8,10},{9,11},{10,... | collective-permute-start | bytes 1622024 | tf_op jit(solution)/shard_map/ppermute | solution.py:538
  39.6 2.8 %collective-permute-start.8 = (bf16[256,512]{1,0:T(8,128)(2,1)S(1)}, bf16[256,512]{1,0:T(8,128)(2,1)S(1)}, u32[]{:S(2)}, u32[]{:S(2)}) collective-permute-start(bf16[256,512]{1,0:T(8,128)(2,1)S(1)} %copy-done.3), channel_id=1, source_target_pairs={{0,12},{1,13},{2,14},{3,15},{4,0},{5,1},{6,2},{7,3},{8,4},{9,5},{1... | collective-permute-start | bytes 786440 | tf_op jit(solution)/shard_map/ppermute | solution.py:541
  42.5 6.8 %collective-permute-done.8.refs_6_ = bf16[256,512]{1,0:T(8,128)(2,1)S(1)} collective-permute-done((bf16[256,512]{1,0:T(8,128)(2,1)S(1)}, bf16[256,512]{1,0:T(8,128)(2,1)S(1)}, u32[]{:S(2)}, u32[]{:S(2)}) %collective-permute-start.8) | collective-permute-done | bytes 262176 | tf_op jit(solution)/shard_map/ppermute | solution.py:541
  49.2 4.0 %collective-permute-done.9.refs_7_ = bf16[256,512]{1,0:T(8,128)(2,1)S(1)} collective-permute-done((bf16[256,512]{1,0:T(8,128)(2,1)S(1)}, bf16[256,512]{1,0:T(8,128)(2,1)S(1)}, u32[]{:S(2)}, u32[]{:S(2)}) %collective-permute-start.9) | collective-permute-done | bytes 262176 | tf_op jit(solution)/shard_map/ppermute | solution.py:541
  53.6 2.2 %copy-done = bf16[1,256,8192]{2,1,0:T(8,128)(2,1)S(1)} copy-done((bf16[1,256,8192]{2,1,0:T(8,128)(2,1)S(1)}, bf16[1,256,8192]{2,1,0:T(8,128)(2,1)}, u32[]{:S(2)}) %copy-start) | copy-done | bytes 4194328
  55.7 3.1 %shard_map.120.mine_ref = f32[3,256,512]{2,1,0:T(8,128)S(1)} custom-call(bf16[256,8192]{1,0:T(8,128)(2,1)S(1)} %bitcast.19, bf16[256,2048]{1,0:T(8,128)(2,1)S(1)} %collective-permute-done.refs_1_, bf16[256,2048]{1,0:T(8,128)(2,1)S(1)} %collective-permute-done.1.refs_2_, bf16[272,512]{1,0:T(8,128)(2,1)S(1)} %copy-done.2, ...), custom_call_target="tpu_custom_call" | custom-call | flops 1610612736 | bytes 5242880 | tf_op jit(solution)/shard_map/pallas_call | solution.py:298
  58.9 1.2 %shard_map.121 = f32[1,256,512]{2,1,0:T(8,128)S(1)} custom-call(bf16[256,2048]{1,0:T(8,128)(2,1)S(1)} %collective-permute-done.2.refs_0_.refs_3_, bf16[272,512]{1,0:T(8,128)(2,1)S(1)} %copy-done.2, bf16[272,512]{1,0:T(8,128)(2,1)S(1)} %collective-permute-done.5.refs_4_.refs_2_, bf16[272,512]{1,0:T(8,128)(2,1)S(1)} %collective-permute-done.3.refs_5_.refs_3_, ...), custom_call_target="tpu_custom_call" | custom-call | flops 536870912 | bytes 3145728 | tf_op jit(solution)/shard_map/pallas_call | solution.py:298
  60.5 0.5 collective-permute-start.18
  61.1 1.1 collective-permute-done.12
  62.6 1.5 %collective-permute-start.14 = (f32[256,512]{1,0:T(8,128)S(1)}, f32[256,512]{1,0:T(8,128)S(1)}, u32[]{:S(2)}, u32[]{:S(2)}) collective-permute-start(f32[256,512]{1,0:T(8,128)S(1)} %fusion.1), channel_id=1, source_target_pairs={{0,16},{1,17},{2,18},{3,19},{4,20},{5,21},{6,22},{7,23},{8,24},{9,... | collective-permute-start | bytes 1572872 | tf_op jit(solution)/shard_map/ppermute | solution.py:545
  64.1 0.4 shard_map.122
  64.6 2.6 %collective-permute-start.16 = (bf16[8,1,16,512]{3,2,1,0:T(8,128)(2,1)S(1)}, bf16[8,1,16,512]{3,2,1,0:T(8,128)(2,1)S(1)}, u32[]{:S(2)}, u32[]{:S(2)}) collective-permute-start(bf16[8,1,16,512]{3,2,1,0:T(8,128)(2,1)S(1)} %get-tuple-element.75), channel_id=1, source_target_pairs={{0,8},{1,9},{2,10},{3,11},{4,12},{5,13},{6,14},{7,15},{8,0},{9,1},... | collective-permute-start | bytes 393224 | tf_op jit(solution)/shard_map/ppermute | solution.py:538
  67.2 0.5 collective-permute-start.13
  67.7 6.0 %collective-permute-done.16 = bf16[8,1,16,512]{3,2,1,0:T(8,128)(2,1)S(1)} collective-permute-done((bf16[8,1,16,512]{3,2,1,0:T(8,128)(2,1)S(1)}, bf16[8,1,16,512]{3,2,1,0:T(8,128)(2,1)S(1)}, u32[]{:S(2)}, u32[]{:S(2)}) %collective-permute-start.16) | collective-permute-done | bytes 131104 | tf_op jit(solution)/shard_map/ppermute | solution.py:538
  73.7 0.8 collective-permute-start.17
  74.5 0.7 collective-permute-done.18.refs_9_
  75.3 3.7 %shard_map.123.refs_5_ = f32[4,256,512]{2,1,0:T(8,128)S(1)} custom-call(bf16[256,8192]{1,0:T(8,128)(2,1)S(1)} %bitcast.20, bf16[256,2048]{1,0:T(8,128)(2,1)S(1)} %collective-permute-done.refs_1_, bf16[256,2048]{1,0:T(8,128)(2,1)S(1)} %collective-permute-done.1.refs_2_, bf16[256,2048]{1,0:T(8,128)(2,1)S(1)} %collective-permute-done.2.refs_0_.refs_3_, ...), custom_call_target="tpu_custom_call" | custom-call | flops 1879048192 | bytes 5505024 | tf_op jit(solution)/shard_map/pallas_call | solution.py:298
  78.9 1.2 %collective-permute-done.13.refs_4_ = bf16[256,512]{1,0:T(8,128)(2,1)S(1)} collective-permute-done((bf16[256,512]{1,0:T(8,128)(2,1)S(1)}, bf16[256,512]{1,0:T(8,128)(2,1)S(1)}, u32[]{:S(2)}, u32[]{:S(2)}) %collective-permute-start.13) | collective-permute-done | bytes 262176 | tf_op jit(solution)/shard_map/ppermute | solution.py:538
  80.2 1.1 shard_map.124.mine_ref
  81.5 0.6 collective-permute-start.23
  82.2 0.6 collective-permute-start.21
  82.8 1.4 %collective-permute-done.19.core_ref = f32[2,256,512]{2,1,0:T(8,128)S(1)} collective-permute-done((f32[2,256,512]{2,1,0:T(8,128)S(1)}, f32[2,256,512]{2,1,0:T(8,128)S(1)}, u32[]{:S(2)}, u32[]{:S(2)}) %collective-permute-start.19) | collective-permute-done | bytes 1048608 | tf_op jit(solution)/shard_map/ppermute | solution.py:538
  84.2 1.6 %collective-permute-start.20 = (bf16[256,512]{1,0:T(8,128)(2,1)S(1)}, bf16[256,512]{1,0:T(8,128)(2,1)S(1)}, u32[]{:S(2)}, u32[]{:S(2)}) collective-permute-start(bf16[256,512]{1,0:T(8,128)(2,1)S(1)} %fusion.2), channel_id=1, source_target_pairs={{0,16},{1,17},{2,18},{3,19},{4,20},{5,21},{6,22},{7,23},{8,24},{9,... | collective-permute-start | bytes 786440 | tf_op jit(solution)/shard_map/ppermute | solution.py:545
  85.8 1.8 %collective-permute-done.21 = bf16[2,4,16,512]{3,2,1,0:T(8,128)(2,1)S(1)} collective-permute-done((bf16[2,4,16,512]{3,2,1,0:T(8,128)(2,1)S(1)}, bf16[2,4,16,512]{3,2,1,0:T(8,128)(2,1)S(1)}, u32[]{:S(2)}, u32[]{:S(2)}) %collective-permute-start.21) | collective-permute-done | bytes 131104 | tf_op jit(solution)/shard_map/ppermute | solution.py:538
  87.8 0.7 shard_map.126
  88.5 0.6 collective-permute-done.22
  89.1 1.5 %shard_map.125.lowrank_ref = f32[256,512]{1,0:T(8,128)S(1)} custom-call(bf16[256,512]{1,0:T(8,128)(2,1)S(1)} %constant_dynamic-update-slice_fusion.8.extras_ref, bf16[256,8192]{1,0:T(8,128)(2,1)S(1)} %bitcast.22, bf16[16,16,512]{2,1,0:T(8,128)(2,1)S(1)} %maximum_bitcast_fusion.down_ref, bf16[16,16,512]{2,1,0:T(8,128)(2,1)S(1)} %copy-done.5), custom_call_target="tpu_custom_call" | custom-call | bytes 4194304 | tf_op jit(solution)/shard_map/pallas_call | solution.py:618
  90.6 2.0 %collective-permute-done.20.pair_ref = bf16[256,512]{1,0:T(8,128)(2,1)S(1)} collective-permute-done((bf16[256,512]{1,0:T(8,128)(2,1)S(1)}, bf16[256,512]{1,0:T(8,128)(2,1)S(1)}, u32[]{:S(2)}, u32[]{:S(2)}) %collective-permute-start.20) | collective-permute-done | bytes 262176 | tf_op jit(solution)/shard_map/ppermute | solution.py:545
  92.6 0.4 shard_map.127
  93.1 0.6 collective-permute-start.25
  93.7 1.3 %collective-permute-start.26 = (bf16[4,48,128]{2,1,0:T(8,128)(2,1)S(1)}, bf16[4,48,128]{2,1,0:T(8,128)(2,1)S(1)}, u32[]{:S(2)}, u32[]{:S(2)}) collective-permute-start(bf16[4,48,128]{2,1,0:T(8,128)(2,1)S(1)} %get-tuple-element.52), channel_id=1, source_target_pairs={{0,3},{1,2},{2,1},{3,0},{4,7},{5,6},{6,5},{7,4},{8,11},{9,10},{10,... | collective-permute-start | bytes 147464 | tf_op jit(solution)/shard_map/ppermute | solution.py:538
  95.0 2.7 %collective-permute-done.25.refs_2_ = bf16[4,48,128]{2,1,0:T(8,128)(2,1)S(1)} collective-permute-done((bf16[4,48,128]{2,1,0:T(8,128)(2,1)S(1)}, bf16[4,48,128]{2,1,0:T(8,128)(2,1)S(1)}, u32[]{:S(2)}, u32[]{:S(2)}) %collective-permute-start.25) | collective-permute-done | bytes 49184 | tf_op jit(solution)/shard_map/ppermute | solution.py:538
  98.0 2.3 %collective-permute-start.27 = (f32[40,128]{1,0:T(8,128)S(1)}, f32[40,128]{1,0:T(8,128)S(1)}, u32[]{:S(2)}, u32[]{:S(2)}) collective-permute-start(f32[40,128]{1,0:T(8,128)S(1)} %get-tuple-element.54), channel_id=1, source_target_pairs={{0,4},{1,5},{2,6},{3,7},{4,8},{5,9},{6,10},{7,11},{8,12},{9,13},{1... | collective-permute-start | bytes 61448 | tf_op jit(solution)/shard_map/ppermute | solution.py:541
  100.4 2.9 %collective-permute-start.28 = (f32[40,128]{1,0:T(8,128)S(1)}, f32[40,128]{1,0:T(8,128)S(1)}, u32[]{:S(2)}, u32[]{:S(2)}) collective-permute-start(f32[40,128]{1,0:T(8,128)S(1)} %get-tuple-element.55), channel_id=1, source_target_pairs={{0,8},{1,9},{2,10},{3,11},{4,12},{5,13},{6,14},{7,15},{8,0},{9,1},... | collective-permute-start | bytes 61448 | tf_op jit(solution)/shard_map/ppermute | solution.py:541
  103.3 0.4 collective-permute-start.29
  103.7 1.0 collective-permute-done.27.refs_1_
  105.0 2.0 %collective-permute-done.29.refs_3_ = f32[40,128]{1,0:T(8,128)S(1)} collective-permute-done((f32[40,128]{1,0:T(8,128)S(1)}, f32[40,128]{1,0:T(8,128)S(1)}, u32[]{:S(2)}, u32[]{:S(2)}) %collective-permute-start.29) | collective-permute-done | bytes 20512 | tf_op jit(solution)/shard_map/ppermute | solution.py:541
  107.1 0.7 shard_map.129
  (63 shorter events, 2.6 us)
Async XLA Ops:
  5.5 12.5 %collective-permute-start.3 = (bf16[272,512]{1,0:T(8,128)(2,1)}, bf16[272,512]{1,0:T(8,128)(2,1)S(1)}, u32[]{:S(2)}, u32[]{:S(2)}) collective-permute-start(bf16[272,512]{1,0:T(8,128)(2,1)} %get-tuple-element.40.refs_3_.refs_1_), channel_id=1, source_target_pairs={{0,12},{1,13},{2,14},{3,15},{4,0},{5,1},{6,2},{7,3},{8,4},{9,5},{1... | collective-permute-start | bytes 835592 | tf_op jit(solution)/shard_map/ppermute | solution.py:541
  10.6 13.0 %collective-permute-start.4 = (bf16[272,512]{1,0:T(8,128)(2,1)}, bf16[272,512]{1,0:T(8,128)(2,1)S(1)}, u32[]{:S(2)}, u32[]{:S(2)}) collective-permute-start(bf16[272,512]{1,0:T(8,128)(2,1)} %get-tuple-element.40.refs_3_.refs_1_), channel_id=1, source_target_pairs={{0,4},{1,5},{2,6},{3,7},{4,8},{5,9},{6,10},{7,11},{8,12},{9,13},{1... | collective-permute-start | bytes 835592 | tf_op jit(solution)/shard_map/ppermute | solution.py:541
  10.6 13.0 %collective-permute-start.5 = (bf16[272,512]{1,0:T(8,128)(2,1)}, bf16[272,512]{1,0:T(8,128)(2,1)S(1)}, u32[]{:S(2)}, u32[]{:S(2)}) collective-permute-start(bf16[272,512]{1,0:T(8,128)(2,1)} %get-tuple-element.40.refs_3_.refs_1_), channel_id=1, source_target_pairs={{0,2},{1,3},{2,0},{3,1},{4,6},{5,7},{6,4},{7,5},{8,10},{9,11},{10,... | collective-permute-start | bytes 835592 | tf_op jit(solution)/shard_map/ppermute | solution.py:538
  12.1 3.9 %copy-start.2 = (bf16[272,512]{1,0:T(8,128)(2,1)S(1)}, bf16[272,512]{1,0:T(8,128)(2,1)}, u32[]{:S(2)}) copy-start(bf16[272,512]{1,0:T(8,128)(2,1)} %get-tuple-element.40.refs_3_.refs_1_) | copy-start | bytes 835588
  12.1 25.9 %copy-start.3 = (bf16[256,512]{1,0:T(8,128)(2,1)S(1)}, bf16[256,512]{1,0:T(8,128)(2,1)}, u32[]{:S(2)}) copy-start(bf16[256,512]{1,0:T(8,128)(2,1)} %get-tuple-element.45.refs_4_) | copy-start | bytes 786436
  12.1 41.4 %collective-permute-start.1 = (bf16[256,2048]{1,0:T(8,128)(2,1)}, bf16[256,2048]{1,0:T(8,128)(2,1)S(1)}, u32[]{:S(2)}, u32[]{:S(2)}) collective-permute-start(bf16[256,2048]{1,0:T(8,128)(2,1)} %get-tuple-element.31), channel_id=1, source_target_pairs={{0,16},{1,17},{2,18},{3,19},{4,20},{5,21},{6,22},{7,23},{8,24},{9,... | collective-permute-start | bytes 3145736 | tf_op jit(solution)/shard_map/ppermute | solution.py:545
  16.0 23.7 %collective-permute-start = (bf16[256,2048]{1,0:T(8,128)(2,1)}, bf16[256,2048]{1,0:T(8,128)(2,1)S(1)}, u32[]{:S(2)}, u32[]{:S(2)}) collective-permute-start(bf16[256,2048]{1,0:T(8,128)(2,1)} %shard_map.118), channel_id=1, source_target_pairs={{0,1},{1,0},{2,3},{3,2},{4,5},{5,4},{6,7},{7,6},{8,9},{9,8},{10,11... | collective-permute-start | bytes 3145736 | tf_op jit(solution)/shard_map/ppermute | solution.py:538
  18.0 40.9 %collective-permute-start.2 = (bf16[256,2048]{1,0:T(8,128)(2,1)}, bf16[256,2048]{1,0:T(8,128)(2,1)S(1)}, u32[]{:S(2)}, u32[]{:S(2)}) collective-permute-start(bf16[256,2048]{1,0:T(8,128)(2,1)} %get-tuple-element.32), channel_id=1, source_target_pairs={{0,17},{1,16},{2,19},{3,18},{4,21},{5,20},{6,23},{7,22},{8,25},{9,... | collective-permute-start | bytes 3145736 | tf_op jit(solution)/shard_map/ppermute | solution.py:545
  23.6 14.4 %collective-permute-start.6 = (bf16[272,512]{1,0:T(8,128)(2,1)S(1)}, bf16[272,512]{1,0:T(8,128)(2,1)S(1)}, u32[]{:S(2)}, u32[]{:S(2)}) collective-permute-start(bf16[272,512]{1,0:T(8,128)(2,1)S(1)} %copy-done.2), channel_id=1, source_target_pairs={{0,8},{1,9},{2,10},{3,11},{4,12},{5,13},{6,14},{7,15},{8,0},{9,1},... | collective-permute-start | bytes 835592 | tf_op jit(solution)/shard_map/ppermute | solution.py:541
  24.4 13.7 %collective-permute-start.7 = (bf16[544,512]{1,0:T(8,128)(2,1)S(1)}, bf16[544,512]{1,0:T(8,128)(2,1)S(1)}, u32[]{:S(2)}, u32[]{:S(2)}) collective-permute-start(bf16[544,512]{1,0:T(8,128)(2,1)S(1)} %pad_maximum_fusion.1), channel_id=1, source_target_pairs={{0,2},{1,3},{2,0},{3,1},{4,6},{5,7},{6,4},{7,5},{8,10},{9,11},{10,... | collective-permute-start | bytes 1671176 | tf_op jit(solution)/shard_map/ppermute | solution.py:538
  38.1 15.5 %collective-permute-start.11 = (bf16[528,512]{1,0:T(8,128)(2,1)S(1)}, bf16[528,512]{1,0:T(8,128)(2,1)S(1)}, u32[]{:S(2)}, u32[]{:S(2)}) collective-permute-start(bf16[528,512]{1,0:T(8,128)(2,1)S(1)} %pad_maximum_fusion.2), channel_id=1, source_target_pairs={{0,2},{1,3},{2,0},{3,1},{4,6},{5,7},{6,4},{7,5},{8,10},{9,11},{10,... | collective-permute-start | bytes 1622024 | tf_op jit(solution)/shard_map/ppermute | solution.py:538
  39.6 9.6 %collective-permute-start.8 = (bf16[256,512]{1,0:T(8,128)(2,1)S(1)}, bf16[256,512]{1,0:T(8,128)(2,1)S(1)}, u32[]{:S(2)}, u32[]{:S(2)}) collective-permute-start(bf16[256,512]{1,0:T(8,128)(2,1)S(1)} %copy-done.3), channel_id=1, source_target_pairs={{0,12},{1,13},{2,14},{3,15},{4,0},{5,1},{6,2},{7,3},{8,4},{9,5},{1... | collective-permute-start | bytes 786440 | tf_op jit(solution)/shard_map/ppermute | solution.py:541
  42.5 10.8 %collective-permute-start.9 = (bf16[256,512]{1,0:T(8,128)(2,1)S(1)}, bf16[256,512]{1,0:T(8,128)(2,1)S(1)}, u32[]{:S(2)}, u32[]{:S(2)}) collective-permute-start(bf16[256,512]{1,0:T(8,128)(2,1)S(1)} %copy-done.3), channel_id=1, source_target_pairs={{0,4},{1,5},{2,6},{3,7},{4,8},{5,9},{6,10},{7,11},{8,12},{9,13},{1... | collective-permute-start | bytes 786440 | tf_op jit(solution)/shard_map/ppermute | solution.py:541
  53.2 13.9 %collective-permute-start.10 = (bf16[256,512]{1,0:T(8,128)(2,1)S(1)}, bf16[256,512]{1,0:T(8,128)(2,1)S(1)}, u32[]{:S(2)}, u32[]{:S(2)}) collective-permute-start(bf16[256,512]{1,0:T(8,128)(2,1)S(1)} %copy-done.3), channel_id=1, source_target_pairs={{0,8},{1,9},{2,10},{3,11},{4,12},{5,13},{6,14},{7,15},{8,0},{9,1},... | collective-permute-start | bytes 786440 | tf_op jit(solution)/shard_map/ppermute | solution.py:541
  53.6 2.2 %copy-start = (bf16[1,256,8192]{2,1,0:T(8,128)(2,1)S(1)}, bf16[1,256,8192]{2,1,0:T(8,128)(2,1)}, u32[]{:S(2)}) copy-start(bf16[1,256,8192]{2,1,0:T(8,128)(2,1)} %param.12) | copy-start | bytes 12582916
  58.9 16.4 %copy-start.1 = (bf16[1,256,8192]{2,1,0:T(8,128)(2,1)S(1)}, bf16[1,256,8192]{2,1,0:T(8,128)(2,1)}, u32[]{:S(2)}) copy-start(bf16[1,256,8192]{2,1,0:T(8,128)(2,1)} %param.12) | copy-start | bytes 12582916
  60.1 4.0 %copy-start.4 = (bf16[512,256]{1,0:T(8,128)(2,1)S(1)}, bf16[512,256]{1,0:T(8,128)(2,1)}, u32[]{:S(2)}) copy-start(bf16[512,256]{1,0:T(8,128)(2,1)} %down_ref.1) | copy-start | bytes 786436
  60.1 2.0 %collective-permute-start.12 = (f32[256,512]{1,0:T(8,128)S(1)}, f32[256,512]{1,0:T(8,128)S(1)}, u32[]{:S(2)}, u32[]{:S(2)}) collective-permute-start(f32[256,512]{1,0:T(8,128)S(1)} %bitcast.23), channel_id=1, source_target_pairs={{0,1},{1,0},{2,3},{3,2},{4,5},{5,4},{6,7},{7,6},{8,9},{9,8},{10,11... | collective-permute-start | bytes 1572872 | tf_op jit(solution)/shard_map/ppermute | solution.py:538
  60.5 14.8 %collective-permute-start.18 = (bf16[512,512]{1,0:T(8,128)(2,1)S(1)}, bf16[512,512]{1,0:T(8,128)(2,1)S(1)}, u32[]{:S(2)}, u32[]{:S(2)}) collective-permute-start(bf16[512,512]{1,0:T(8,128)(2,1)S(1)} %pad_maximum_fusion.3), channel_id=1, source_target_pairs={{0,2},{1,3},{2,0},{3,1},{4,6},{5,7},{6,4},{7,5},{8,10},{9,11},{10,... | collective-permute-start | bytes 1572872 | tf_op jit(solution)/shard_map/ppermute | solution.py:538
  62.2 1.9 %collective-permute-start.15 = (bf16[128,512]{1,0:T(8,128)(2,1)S(1)}, bf16[128,512]{1,0:T(8,128)(2,1)S(1)}, u32[]{:S(2)}, u32[]{:S(2)}) collective-permute-start(bf16[128,512]{1,0:T(8,128)(2,1)S(1)} %get-tuple-element.42), channel_id=1, source_target_pairs={{0,1},{1,0},{2,3},{3,2},{4,5},{5,4},{6,7},{7,6},{8,9},{9,8},{10,11... | collective-permute-start | bytes 393224 | tf_op jit(solution)/shard_map/ppermute | solution.py:538
  62.6 17.6 %collective-permute-start.14 = (f32[256,512]{1,0:T(8,128)S(1)}, f32[256,512]{1,0:T(8,128)S(1)}, u32[]{:S(2)}, u32[]{:S(2)}) collective-permute-start(f32[256,512]{1,0:T(8,128)S(1)} %fusion.1), channel_id=1, source_target_pairs={{0,16},{1,17},{2,18},{3,19},{4,20},{5,21},{6,22},{7,23},{8,24},{9,... | collective-permute-start | bytes 1572872 | tf_op jit(solution)/shard_map/ppermute | solution.py:545
  64.6 9.2 %collective-permute-start.16 = (bf16[8,1,16,512]{3,2,1,0:T(8,128)(2,1)S(1)}, bf16[8,1,16,512]{3,2,1,0:T(8,128)(2,1)S(1)}, u32[]{:S(2)}, u32[]{:S(2)}) collective-permute-start(bf16[8,1,16,512]{3,2,1,0:T(8,128)(2,1)S(1)} %get-tuple-element.75), channel_id=1, source_target_pairs={{0,8},{1,9},{2,10},{3,11},{4,12},{5,13},{6,14},{7,15},{8,0},{9,1},... | collective-permute-start | bytes 393224 | tf_op jit(solution)/shard_map/ppermute | solution.py:538
  67.2 13.0 %collective-permute-start.13 = (bf16[256,512]{1,0:T(8,128)(2,1)S(1)}, bf16[256,512]{1,0:T(8,128)(2,1)S(1)}, u32[]{:S(2)}, u32[]{:S(2)}) collective-permute-start(bf16[256,512]{1,0:T(8,128)(2,1)S(1)} %collective-permute-done.10.refs_8_), channel_id=1, source_target_pairs={{0,2},{1,3},{2,0},{3,1},{4,6},{5,7},{6,4},{7,5},{8,10},{9,11},{10,... | collective-permute-start | bytes 786440 | tf_op jit(solution)/shard_map/ppermute | solution.py:538
  73.7 6.4 %collective-permute-start.17 = (bf16[4,2,16,512]{3,2,1,0:T(8,128)(2,1)S(1)}, bf16[4,2,16,512]{3,2,1,0:T(8,128)(2,1)S(1)}, u32[]{:S(2)}, u32[]{:S(2)}) collective-permute-start(bf16[4,2,16,512]{3,2,1,0:T(8,128)(2,1)S(1)} %fusion.5), channel_id=1, source_target_pairs={{0,4},{1,5},{2,6},{3,7},{4,0},{5,1},{6,2},{7,3},{8,12},{9,13},{10,... | collective-permute-start | bytes 393224 | tf_op jit(solution)/shard_map/ppermute | solution.py:538
  81.4 2.7 %collective-permute-start.19 = (f32[2,256,512]{2,1,0:T(8,128)S(1)}, f32[2,256,512]{2,1,0:T(8,128)S(1)}, u32[]{:S(2)}, u32[]{:S(2)}) collective-permute-start(f32[2,256,512]{2,1,0:T(8,128)S(1)} %pad_maximum_fusion), channel_id=1, source_target_pairs={{0,1},{1,0},{2,3},{3,2},{4,5},{5,4},{6,7},{7,6},{8,9},{9,8},{10,11... | collective-permute-start | bytes 3145736 | tf_op jit(solution)/shard_map/ppermute | solution.py:538
  81.5 6.2 %copy-start.6 = (f32[128]{0:T(128)S(1)}, f32[128]{0:T(128)}, u32[]{:S(2)}) copy-start(f32[128]{0:T(128)} %param.17) | copy-start | bytes 1540
  81.5 6.2 %collective-permute-start.23 = (f32[256,512]{1,0:T(8,128)S(1)}, f32[256,512]{1,0:T(8,128)S(1)}, u32[]{:S(2)}, u32[]{:S(2)}) collective-permute-start(f32[256,512]{1,0:T(8,128)S(1)} %slice_bitcast_fusion), channel_id=1, source_target_pairs={{0,1},{1,0},{2,3},{3,2},{4,5},{5,4},{6,7},{7,6},{8,9},{9,8},{10,11... | collective-permute-start | bytes 1572872 | tf_op jit(solution)/shard_map/ppermute | solution.py:538
  82.2 5.5 %collective-permute-start.21 = (bf16[2,4,16,512]{3,2,1,0:T(8,128)(2,1)S(1)}, bf16[2,4,16,512]{3,2,1,0:T(8,128)(2,1)S(1)}, u32[]{:S(2)}, u32[]{:S(2)}) collective-permute-start(bf16[2,4,16,512]{3,2,1,0:T(8,128)(2,1)S(1)} %get-tuple-element.74), channel_id=1, source_target_pairs={{0,2},{1,3},{2,0},{3,1},{4,6},{5,7},{6,4},{7,5},{8,10},{9,11},{10,... | collective-permute-start | bytes 393224 | tf_op jit(solution)/shard_map/ppermute | solution.py:538
  84.2 8.4 %collective-permute-start.20 = (bf16[256,512]{1,0:T(8,128)(2,1)S(1)}, bf16[256,512]{1,0:T(8,128)(2,1)S(1)}, u32[]{:S(2)}, u32[]{:S(2)}) collective-permute-start(bf16[256,512]{1,0:T(8,128)(2,1)S(1)} %fusion.2), channel_id=1, source_target_pairs={{0,16},{1,17},{2,18},{3,19},{4,20},{5,21},{6,22},{7,23},{8,24},{9,... | collective-permute-start | bytes 786440 | tf_op jit(solution)/shard_map/ppermute | solution.py:545
  87.7 1.4 %collective-permute-start.22 = (bf16[1,8,16,512]{3,2,1,0:T(8,128)(2,1)S(1)}, bf16[1,8,16,512]{3,2,1,0:T(8,128)(2,1)S(1)}, u32[]{:S(2)}, u32[]{:S(2)}) collective-permute-start(bf16[1,8,16,512]{3,2,1,0:T(8,128)(2,1)S(1)} %get-tuple-element.72), channel_id=1, source_target_pairs={{0,1},{1,0},{2,3},{3,2},{4,5},{5,4},{6,7},{7,6},{8,9},{9,8},{10,11... | collective-permute-start | bytes 393224 | tf_op jit(solution)/shard_map/ppermute | solution.py:538
  87.8 1.3 %copy-start.5 = (bf16[16,16,512]{2,1,0:T(8,128)(2,1)S(1)}, bf16[16,16,512]{2,1,0:T(8,128)(2,1)}, u32[]{:S(2)}) copy-start(bf16[16,16,512]{2,1,0:T(8,128)(2,1)} %up_ref.1) | copy-start | bytes 786436
  93.0 1.9 %collective-permute-start.24 = (bf16[4,48,128]{2,1,0:T(8,128)(2,1)S(1)}, bf16[4,48,128]{2,1,0:T(8,128)(2,1)S(1)}, u32[]{:S(2)}, u32[]{:S(2)}) collective-permute-start(bf16[4,48,128]{2,1,0:T(8,128)(2,1)S(1)} %get-tuple-element.50), channel_id=1, source_target_pairs={{0,1},{1,0},{2,3},{3,2},{4,5},{5,4},{6,7},{7,6},{8,9},{9,8},{10,11... | collective-permute-start | bytes 147464 | tf_op jit(solution)/shard_map/ppermute | solution.py:538
  93.1 4.6 %collective-permute-start.25 = (bf16[4,48,128]{2,1,0:T(8,128)(2,1)S(1)}, bf16[4,48,128]{2,1,0:T(8,128)(2,1)S(1)}, u32[]{:S(2)}, u32[]{:S(2)}) collective-permute-start(bf16[4,48,128]{2,1,0:T(8,128)(2,1)S(1)} %get-tuple-element.51), channel_id=1, source_target_pairs={{0,2},{1,3},{2,0},{3,1},{4,6},{5,7},{6,4},{7,5},{8,10},{9,11},{10,... | collective-permute-start | bytes 147464 | tf_op jit(solution)/shard_map/ppermute | solution.py:538
  93.7 4.2 %collective-permute-start.26 = (bf16[4,48,128]{2,1,0:T(8,128)(2,1)S(1)}, bf16[4,48,128]{2,1,0:T(8,128)(2,1)S(1)}, u32[]{:S(2)}, u32[]{:S(2)}) collective-permute-start(bf16[4,48,128]{2,1,0:T(8,128)(2,1)S(1)} %get-tuple-element.52), channel_id=1, source_target_pairs={{0,3},{1,2},{2,1},{3,0},{4,7},{5,6},{6,5},{7,4},{8,11},{9,10},{10,... | collective-permute-start | bytes 147464 | tf_op jit(solution)/shard_map/ppermute | solution.py:538
  98.0 6.7 %collective-permute-start.27 = (f32[40,128]{1,0:T(8,128)S(1)}, f32[40,128]{1,0:T(8,128)S(1)}, u32[]{:S(2)}, u32[]{:S(2)}) collective-permute-start(f32[40,128]{1,0:T(8,128)S(1)} %get-tuple-element.54), channel_id=1, source_target_pairs={{0,4},{1,5},{2,6},{3,7},{4,8},{5,9},{6,10},{7,11},{8,12},{9,13},{1... | collective-permute-start | bytes 61448 | tf_op jit(solution)/shard_map/ppermute | solution.py:541
  100.4 4.7 %collective-permute-start.28 = (f32[40,128]{1,0:T(8,128)S(1)}, f32[40,128]{1,0:T(8,128)S(1)}, u32[]{:S(2)}, u32[]{:S(2)}) collective-permute-start(f32[40,128]{1,0:T(8,128)S(1)} %get-tuple-element.55), channel_id=1, source_target_pairs={{0,8},{1,9},{2,10},{3,11},{4,12},{5,13},{6,14},{7,15},{8,0},{9,1},... | collective-permute-start | bytes 61448 | tf_op jit(solution)/shard_map/ppermute | solution.py:541
  103.3 3.8 %collective-permute-start.29 = (f32[40,128]{1,0:T(8,128)S(1)}, f32[40,128]{1,0:T(8,128)S(1)}, u32[]{:S(2)}, u32[]{:S(2)}) collective-permute-start(f32[40,128]{1,0:T(8,128)S(1)} %get-tuple-element.56), channel_id=1, source_target_pairs={{0,12},{1,13},{2,14},{3,15},{4,0},{5,1},{6,2},{7,3},{8,4},{9,5},{1... | collective-permute-start | bytes 61448 | tf_op jit(solution)/shard_map/ppermute | solution.py:541

commit v7 on v6

--- a/solution.py
+++ b/solution.py
@@ -298,7 +298,9 @@
     return call(
         functools.partial(project_kernel, pieces, spots, number, own, len(arrays), len(before), half, steps),
         jax.ShapeDtypeStruct((number, keys, width), jnp.float32),
-        whole(number + len(arrays), pl.ANY) + whole(len(before)),
+        [pl.BlockSpec(memory_space=pltpu.HBM if i == own else pl.ANY) for i in range(number)]
+        + whole(len(arrays), pl.ANY)
+        + whole(len(before)),
         scratch=[
             pltpu.VMEM((number, keys, count * half), images[0].dtype),
             pltpu.VMEM((count * half, width), arrays[0].dtype),

time: 108 us -> 108 us (level)
  no operation moved by 1% of the time
where the time goes in v7:
time: 108 us
  waiting for transfers between devices  51.6 us (48%)
  starting transfers between devices  32.3 us (30%)
  Pallas kernels  18.8 us (17%)
  local copies, waits for them, and re-layouts  2.4 us (2%)
  between operations  2.28 us (2%)
    ppermute x9, waiting for transfers between devices, along(): lax.ppermute(value, 'image', [(i, (i - PLANE * d) % devices) for i in eve...  33.7 us
    ppermute x17, waiting for transfers between devices, across(): return lax.ppermute(value, 'image', [(i, i ^ bits) for i in everyone])  15.8 us
    ppermute x9, starting transfers between devices, along(): lax.ppermute(value, 'image', [(i, (i - PLANE * d) % devices) for i in eve...  14.6 us
    ppermute x17, starting transfers between devices, across(): return lax.ppermute(value, 'image', [(i, i ^ bits) for i in everyone])  13.1 us
    pallas_call x4, Pallas kernels, project(): call(functools.partial(project_kernel, pieces, spots, number, own, len(ar...  9.08 us
    ppermute x4, starting transfers between devices, swap(): return lax.ppermute(value, ('groups', 'image'), pairs)  4.62 us
    pallas_call x1, Pallas kernels, local(): pl.pallas_call(functools.partial(prepare_kernel, half), out_shape=[jax.Sh...  3.55 us
    pallas_call x1, Pallas kernels, send_columns(): pl.pallas_call(functools.partial(send_kernel, half, targets), out_shape=[...  2.33 us
  transfers between devices with their start and end apart: 30, of which 18 were waited for; matrix products, arithmetic and copies ran while one was open for 0% of the time, Pallas kernels for 12%

profile of v7, /device:TPU:0, one launch (start us, length us, event | category | flops | bytes accessed | tf_op | source)
XLA Modules:
  0.0 107.8 jit_solution(3078782705440410676)
XLA Ops:
  1.9 3.6 %shard_map.119 = (bf16[272,512]{1,0:T(8,128)(2,1)}, bf16[256,512]{1,0:T(8,128)(2,1)}, bf16[256,2048]{1,0:T(8,128)(2,1)}, bf16[256,2048]{1,0:T(8,128)(2,1)}) custom-call(s32[1]{0:T(128)S(6)} %copy.28.text_ref, s32[1,1]{1,0:T(1,128)S(6)} %copy.29.image_ref, s32[1]{0:T(128)S(6)} %copy.30.tiles_ref, s32[8]{0:T(128)} %tenant_ref.1, s32[16]{0:T(128)} %page_ref.1, ...), custom_call_target="tpu_custom_call" | custom-call | tf_op jit(solution)/shard_map/pallas_call | solution.py:554
  5.5 5.1 %collective-permute-start.3 = (bf16[272,512]{1,0:T(8,128)(2,1)}, bf16[272,512]{1,0:T(8,128)(2,1)S(1)}, u32[]{:S(2)}, u32[]{:S(2)}) collective-permute-start(bf16[272,512]{1,0:T(8,128)(2,1)} %get-tuple-element.40.refs_3_.refs_1_), channel_id=1, source_target_pairs={{0,12},{1,13},{2,14},{3,15},{4,0},{5,1},{6,2},{7,3},{8,4},{9,5},{1... | collective-permute-start | bytes 835592 | tf_op jit(solution)/shard_map/ppermute | solution.py:543
  10.6 1.5 %collective-permute-start.5 = (bf16[272,512]{1,0:T(8,128)(2,1)}, bf16[272,512]{1,0:T(8,128)(2,1)S(1)}, u32[]{:S(2)}, u32[]{:S(2)}) collective-permute-start(bf16[272,512]{1,0:T(8,128)(2,1)} %get-tuple-element.40.refs_3_.refs_1_), channel_id=1, source_target_pairs={{0,2},{1,3},{2,0},{3,1},{4,6},{5,7},{6,4},{7,5},{8,10},{9,11},{10,... | collective-permute-start | bytes 835592 | tf_op jit(solution)/shard_map/ppermute | solution.py:540
  12.1 1.5 %collective-permute-start.1 = (bf16[256,2048]{1,0:T(8,128)(2,1)}, bf16[256,2048]{1,0:T(8,128)(2,1)S(1)}, u32[]{:S(2)}, u32[]{:S(2)}) collective-permute-start(bf16[256,2048]{1,0:T(8,128)(2,1)} %get-tuple-element.31), channel_id=1, source_target_pairs={{0,16},{1,17},{2,18},{3,19},{4,20},{5,21},{6,22},{7,23},{8,24},{9,... | collective-permute-start | bytes 3145736 | tf_op jit(solution)/shard_map/ppermute | solution.py:547
  13.6 2.3 %shard_map.118 = bf16[256,2048]{1,0:T(8,128)(2,1)} custom-call(bf16[256,8192]{1,0:T(8,128)(2,1)} %bitcast.18), custom_call_target="tpu_custom_call" | custom-call | bytes 2097152 | tf_op jit(solution)/shard_map/pallas_call | solution.py:201
  16.1 1.9 %collective-permute-done.3.refs_5_.refs_3_ = bf16[272,512]{1,0:T(8,128)(2,1)S(1)} collective-permute-done((bf16[272,512]{1,0:T(8,128)(2,1)}, bf16[272,512]{1,0:T(8,128)(2,1)S(1)}, u32[]{:S(2)}, u32[]{:S(2)}) %collective-permute-start.3) | collective-permute-done | bytes 278560 | tf_op jit(solution)/shard_map/ppermute | solution.py:543
  18.0 5.6 %collective-permute-done.4.refs_6_.refs_4_ = bf16[272,512]{1,0:T(8,128)(2,1)S(1)} collective-permute-done((bf16[272,512]{1,0:T(8,128)(2,1)}, bf16[272,512]{1,0:T(8,128)(2,1)S(1)}, u32[]{:S(2)}, u32[]{:S(2)}) %collective-permute-start.4) | collective-permute-done | bytes 278560 | tf_op jit(solution)/shard_map/ppermute | solution.py:543
  23.6 0.7 collective-permute-start.6
  24.4 1.6 %collective-permute-start.7 = (bf16[544,512]{1,0:T(8,128)(2,1)S(1)}, bf16[544,512]{1,0:T(8,128)(2,1)S(1)}, u32[]{:S(2)}, u32[]{:S(2)}) collective-permute-start(bf16[544,512]{1,0:T(8,128)(2,1)S(1)} %pad_maximum_fusion.1), channel_id=1, source_target_pairs={{0,2},{1,3},{2,0},{3,1},{4,6},{5,7},{6,4},{7,5},{8,10},{9,11},{10,... | collective-permute-start | bytes 1671176 | tf_op jit(solution)/shard_map/ppermute | solution.py:540
  25.9 12.1 %collective-permute-done.6.refs_7_.refs_5_ = bf16[272,512]{1,0:T(8,128)(2,1)S(1)} collective-permute-done((bf16[272,512]{1,0:T(8,128)(2,1)S(1)}, bf16[272,512]{1,0:T(8,128)(2,1)S(1)}, u32[]{:S(2)}, u32[]{:S(2)}) %collective-permute-start.6) | collective-permute-done | bytes 278560 | tf_op jit(solution)/shard_map/ppermute | solution.py:543
  38.1 1.6 %collective-permute-start.11 = (bf16[528,512]{1,0:T(8,128)(2,1)S(1)}, bf16[528,512]{1,0:T(8,128)(2,1)S(1)}, u32[]{:S(2)}, u32[]{:S(2)}) collective-permute-start(bf16[528,512]{1,0:T(8,128)(2,1)S(1)} %pad_maximum_fusion.2), channel_id=1, source_target_pairs={{0,2},{1,3},{2,0},{3,1},{4,6},{5,7},{6,4},{7,5},{8,10},{9,11},{10,... | collective-permute-start | bytes 1622024 | tf_op jit(solution)/shard_map/ppermute | solution.py:540
  39.6 2.8 %collective-permute-start.8 = (bf16[256,512]{1,0:T(8,128)(2,1)S(1)}, bf16[256,512]{1,0:T(8,128)(2,1)S(1)}, u32[]{:S(2)}, u32[]{:S(2)}) collective-permute-start(bf16[256,512]{1,0:T(8,128)(2,1)S(1)} %copy-done.3), channel_id=1, source_target_pairs={{0,12},{1,13},{2,14},{3,15},{4,0},{5,1},{6,2},{7,3},{8,4},{9,5},{1... | collective-permute-start | bytes 786440 | tf_op jit(solution)/shard_map/ppermute | solution.py:543
  42.5 6.8 %collective-permute-done.8.refs_6_ = bf16[256,512]{1,0:T(8,128)(2,1)S(1)} collective-permute-done((bf16[256,512]{1,0:T(8,128)(2,1)S(1)}, bf16[256,512]{1,0:T(8,128)(2,1)S(1)}, u32[]{:S(2)}, u32[]{:S(2)}) %collective-permute-start.8) | collective-permute-done | bytes 262176 | tf_op jit(solution)/shard_map/ppermute | solution.py:543
  49.2 4.0 %collective-permute-done.9.refs_7_ = bf16[256,512]{1,0:T(8,128)(2,1)S(1)} collective-permute-done((bf16[256,512]{1,0:T(8,128)(2,1)S(1)}, bf16[256,512]{1,0:T(8,128)(2,1)S(1)}, u32[]{:S(2)}, u32[]{:S(2)}) %collective-permute-start.9) | collective-permute-done | bytes 262176 | tf_op jit(solution)/shard_map/ppermute | solution.py:543
  53.6 2.2 %copy-done = bf16[1,256,8192]{2,1,0:T(8,128)(2,1)S(1)} copy-done((bf16[1,256,8192]{2,1,0:T(8,128)(2,1)S(1)}, bf16[1,256,8192]{2,1,0:T(8,128)(2,1)}, u32[]{:S(2)}) %copy-start) | copy-done | bytes 4194328
  55.7 3.1 %shard_map.120.mine_ref = f32[3,256,512]{2,1,0:T(8,128)S(1)} custom-call(bf16[256,8192]{1,0:T(8,128)(2,1)S(1)} %bitcast.19, bf16[256,2048]{1,0:T(8,128)(2,1)S(1)} %collective-permute-done.refs_1_, bf16[256,2048]{1,0:T(8,128)(2,1)S(1)} %collective-permute-done.1.refs_2_, bf16[272,512]{1,0:T(8,128)(2,1)S(1)} %copy-done.2, ...), custom_call_target="tpu_custom_call" | custom-call | flops 1610612736 | bytes 5242880 | tf_op jit(solution)/shard_map/pallas_call | solution.py:298
  58.9 1.2 %shard_map.121 = f32[1,256,512]{2,1,0:T(8,128)S(1)} custom-call(bf16[256,2048]{1,0:T(8,128)(2,1)S(1)} %collective-permute-done.2.refs_0_.refs_3_, bf16[272,512]{1,0:T(8,128)(2,1)S(1)} %copy-done.2, bf16[272,512]{1,0:T(8,128)(2,1)S(1)} %collective-permute-done.5.refs_4_.refs_2_, bf16[272,512]{1,0:T(8,128)(2,1)S(1)} %collective-permute-done.3.refs_5_.refs_3_, ...), custom_call_target="tpu_custom_call" | custom-call | flops 536870912 | bytes 3145728 | tf_op jit(solution)/shard_map/pallas_call | solution.py:298
  60.5 0.5 collective-permute-start.18
  61.1 1.1 collective-permute-done.12
  62.6 1.5 %collective-permute-start.14 = (f32[256,512]{1,0:T(8,128)S(1)}, f32[256,512]{1,0:T(8,128)S(1)}, u32[]{:S(2)}, u32[]{:S(2)}) collective-permute-start(f32[256,512]{1,0:T(8,128)S(1)} %fusion.1), channel_id=1, source_target_pairs={{0,16},{1,17},{2,18},{3,19},{4,20},{5,21},{6,22},{7,23},{8,24},{9,... | collective-permute-start | bytes 1572872 | tf_op jit(solution)/shard_map/ppermute | solution.py:547
  64.1 0.4 shard_map.122
  64.6 2.6 %collective-permute-start.16 = (bf16[8,1,16,512]{3,2,1,0:T(8,128)(2,1)S(1)}, bf16[8,1,16,512]{3,2,1,0:T(8,128)(2,1)S(1)}, u32[]{:S(2)}, u32[]{:S(2)}) collective-permute-start(bf16[8,1,16,512]{3,2,1,0:T(8,128)(2,1)S(1)} %get-tuple-element.75), channel_id=1, source_target_pairs={{0,8},{1,9},{2,10},{3,11},{4,12},{5,13},{6,14},{7,15},{8,0},{9,1},... | collective-permute-start | bytes 393224 | tf_op jit(solution)/shard_map/ppermute | solution.py:540
  67.2 0.5 collective-permute-start.13
  67.7 6.0 %collective-permute-done.16 = bf16[8,1,16,512]{3,2,1,0:T(8,128)(2,1)S(1)} collective-permute-done((bf16[8,1,16,512]{3,2,1,0:T(8,128)(2,1)S(1)}, bf16[8,1,16,512]{3,2,1,0:T(8,128)(2,1)S(1)}, u32[]{:S(2)}, u32[]{:S(2)}) %collective-permute-start.16) | collective-permute-done | bytes 131104 | tf_op jit(solution)/shard_map/ppermute | solution.py:540
  73.7 0.8 collective-permute-start.17
  74.5 0.7 collective-permute-done.18.refs_9_
  75.3 3.7 %shard_map.123.refs_5_ = f32[4,256,512]{2,1,0:T(8,128)S(1)} custom-call(bf16[256,8192]{1,0:T(8,128)(2,1)S(1)} %bitcast.20, bf16[256,2048]{1,0:T(8,128)(2,1)S(1)} %collective-permute-done.refs_1_, bf16[256,2048]{1,0:T(8,128)(2,1)S(1)} %collective-permute-done.1.refs_2_, bf16[256,2048]{1,0:T(8,128)(2,1)S(1)} %collective-permute-done.2.refs_0_.refs_3_, ...), custom_call_target="tpu_custom_call" | custom-call | flops 1879048192 | bytes 5505024 | tf_op jit(solution)/shard_map/pallas_call | solution.py:298
  78.9 1.2 %collective-permute-done.13.refs_4_ = bf16[256,512]{1,0:T(8,128)(2,1)S(1)} collective-permute-done((bf16[256,512]{1,0:T(8,128)(2,1)S(1)}, bf16[256,512]{1,0:T(8,128)(2,1)S(1)}, u32[]{:S(2)}, u32[]{:S(2)}) %collective-permute-start.13) | collective-permute-done | bytes 262176 | tf_op jit(solution)/shard_map/ppermute | solution.py:540
  80.2 1.1 shard_map.124.mine_ref
  81.5 0.6 collective-permute-start.23
  82.2 0.6 collective-permute-start.21
  82.8 1.4 %collective-permute-done.19.core_ref = f32[2,256,512]{2,1,0:T(8,128)S(1)} collective-permute-done((f32[2,256,512]{2,1,0:T(8,128)S(1)}, f32[2,256,512]{2,1,0:T(8,128)S(1)}, u32[]{:S(2)}, u32[]{:S(2)}) %collective-permute-start.19) | collective-permute-done | bytes 1048608 | tf_op jit(solution)/shard_map/ppermute | solution.py:540
  84.2 1.6 %collective-permute-start.20 = (bf16[256,512]{1,0:T(8,128)(2,1)S(1)}, bf16[256,512]{1,0:T(8,128)(2,1)S(1)}, u32[]{:S(2)}, u32[]{:S(2)}) collective-permute-start(bf16[256,512]{1,0:T(8,128)(2,1)S(1)} %fusion.2), channel_id=1, source_target_pairs={{0,16},{1,17},{2,18},{3,19},{4,20},{5,21},{6,22},{7,23},{8,24},{9,... | collective-permute-start | bytes 786440 | tf_op jit(solution)/shard_map/ppermute | solution.py:547
  85.8 1.8 %collective-permute-done.21 = bf16[2,4,16,512]{3,2,1,0:T(8,128)(2,1)S(1)} collective-permute-done((bf16[2,4,16,512]{3,2,1,0:T(8,128)(2,1)S(1)}, bf16[2,4,16,512]{3,2,1,0:T(8,128)(2,1)S(1)}, u32[]{:S(2)}, u32[]{:S(2)}) %collective-permute-start.21) | collective-permute-done | bytes 131104 | tf_op jit(solution)/shard_map/ppermute | solution.py:540
  87.8 0.7 shard_map.126
  88.5 0.6 collective-permute-done.22
  89.1 1.5 %shard_map.125.lowrank_ref = f32[256,512]{1,0:T(8,128)S(1)} custom-call(bf16[256,512]{1,0:T(8,128)(2,1)S(1)} %constant_dynamic-update-slice_fusion.8.extras_ref, bf16[256,8192]{1,0:T(8,128)(2,1)S(1)} %bitcast.22, bf16[16,16,512]{2,1,0:T(8,128)(2,1)S(1)} %maximum_bitcast_fusion.down_ref, bf16[16,16,512]{2,1,0:T(8,128)(2,1)S(1)} %copy-done.5), custom_call_target="tpu_custom_call" | custom-call | bytes 4194304 | tf_op jit(solution)/shard_map/pallas_call | solution.py:620
  90.6 2.0 %collective-permute-done.20.pair_ref = bf16[256,512]{1,0:T(8,128)(2,1)S(1)} collective-permute-done((bf16[256,512]{1,0:T(8,128)(2,1)S(1)}, bf16[256,512]{1,0:T(8,128)(2,1)S(1)}, u32[]{:S(2)}, u32[]{:S(2)}) %collective-permute-start.20) | collective-permute-done | bytes 262176 | tf_op jit(solution)/shard_map/ppermute | solution.py:547
  92.6 0.4 shard_map.127
  93.1 0.6 collective-permute-start.25
  93.7 1.3 %collective-permute-start.26 = (bf16[4,48,128]{2,1,0:T(8,128)(2,1)S(1)}, bf16[4,48,128]{2,1,0:T(8,128)(2,1)S(1)}, u32[]{:S(2)}, u32[]{:S(2)}) collective-permute-start(bf16[4,48,128]{2,1,0:T(8,128)(2,1)S(1)} %get-tuple-element.52), channel_id=1, source_target_pairs={{0,3},{1,2},{2,1},{3,0},{4,7},{5,6},{6,5},{7,4},{8,11},{9,10},{10,... | collective-permute-start | bytes 147464 | tf_op jit(solution)/shard_map/ppermute | solution.py:540
  95.0 2.7 %collective-permute-done.25.refs_2_ = bf16[4,48,128]{2,1,0:T(8,128)(2,1)S(1)} collective-permute-done((bf16[4,48,128]{2,1,0:T(8,128)(2,1)S(1)}, bf16[4,48,128]{2,1,0:T(8,128)(2,1)S(1)}, u32[]{:S(2)}, u32[]{:S(2)}) %collective-permute-start.25) | collective-permute-done | bytes 49184 | tf_op jit(solution)/shard_map/ppermute | solution.py:540
  98.0 2.3 %collective-permute-start.27 = (f32[40,128]{1,0:T(8,128)S(1)}, f32[40,128]{1,0:T(8,128)S(1)}, u32[]{:S(2)}, u32[]{:S(2)}) collective-permute-start(f32[40,128]{1,0:T(8,128)S(1)} %get-tuple-element.54), channel_id=1, source_target_pairs={{0,4},{1,5},{2,6},{3,7},{4,8},{5,9},{6,10},{7,11},{8,12},{9,13},{1... | collective-permute-start | bytes 61448 | tf_op jit(solution)/shard_map/ppermute | solution.py:543
  100.4 2.9 %collective-permute-start.28 = (f32[40,128]{1,0:T(8,128)S(1)}, f32[40,128]{1,0:T(8,128)S(1)}, u32[]{:S(2)}, u32[]{:S(2)}) collective-permute-start(f32[40,128]{1,0:T(8,128)S(1)} %get-tuple-element.55), channel_id=1, source_target_pairs={{0,8},{1,9},{2,10},{3,11},{4,12},{5,13},{6,14},{7,15},{8,0},{9,1},... | collective-permute-start | bytes 61448 | tf_op jit(solution)/shard_map/ppermute | solution.py:543
  103.3 0.4 collective-permute-start.29
  103.7 1.0 collective-permute-done.27.refs_1_
  105.0 2.0 %collective-permute-done.29.refs_3_ = f32[40,128]{1,0:T(8,128)S(1)} collective-permute-done((f32[40,128]{1,0:T(8,128)S(1)}, f32[40,128]{1,0:T(8,128)S(1)}, u32[]{:S(2)}, u32[]{:S(2)}) %collective-permute-start.29) | collective-permute-done | bytes 20512 | tf_op jit(solution)/shard_map/ppermute | solution.py:543
  107.1 0.7 shard_map.129
  (63 shorter events, 2.6 us)
Async XLA Ops:
  5.5 12.5 %collective-permute-start.3 = (bf16[272,512]{1,0:T(8,128)(2,1)}, bf16[272,512]{1,0:T(8,128)(2,1)S(1)}, u32[]{:S(2)}, u32[]{:S(2)}) collective-permute-start(bf16[272,512]{1,0:T(8,128)(2,1)} %get-tuple-element.40.refs_3_.refs_1_), channel_id=1, source_target_pairs={{0,12},{1,13},{2,14},{3,15},{4,0},{5,1},{6,2},{7,3},{8,4},{9,5},{1... | collective-permute-start | bytes 835592 | tf_op jit(solution)/shard_map/ppermute | solution.py:543
  10.6 13.0 %collective-permute-start.4 = (bf16[272,512]{1,0:T(8,128)(2,1)}, bf16[272,512]{1,0:T(8,128)(2,1)S(1)}, u32[]{:S(2)}, u32[]{:S(2)}) collective-permute-start(bf16[272,512]{1,0:T(8,128)(2,1)} %get-tuple-element.40.refs_3_.refs_1_), channel_id=1, source_target_pairs={{0,4},{1,5},{2,6},{3,7},{4,8},{5,9},{6,10},{7,11},{8,12},{9,13},{1... | collective-permute-start | bytes 835592 | tf_op jit(solution)/shard_map/ppermute | solution.py:543
  10.6 13.0 %collective-permute-start.5 = (bf16[272,512]{1,0:T(8,128)(2,1)}, bf16[272,512]{1,0:T(8,128)(2,1)S(1)}, u32[]{:S(2)}, u32[]{:S(2)}) collective-permute-start(bf16[272,512]{1,0:T(8,128)(2,1)} %get-tuple-element.40.refs_3_.refs_1_), channel_id=1, source_target_pairs={{0,2},{1,3},{2,0},{3,1},{4,6},{5,7},{6,4},{7,5},{8,10},{9,11},{10,... | collective-permute-start | bytes 835592 | tf_op jit(solution)/shard_map/ppermute | solution.py:540
  12.1 3.9 %copy-start.2 = (bf16[272,512]{1,0:T(8,128)(2,1)S(1)}, bf16[272,512]{1,0:T(8,128)(2,1)}, u32[]{:S(2)}) copy-start(bf16[272,512]{1,0:T(8,128)(2,1)} %get-tuple-element.40.refs_3_.refs_1_) | copy-start | bytes 835588
  12.1 25.9 %copy-start.3 = (bf16[256,512]{1,0:T(8,128)(2,1)S(1)}, bf16[256,512]{1,0:T(8,128)(2,1)}, u32[]{:S(2)}) copy-start(bf16[256,512]{1,0:T(8,128)(2,1)} %get-tuple-element.45.refs_4_) | copy-start | bytes 786436
  12.1 41.4 %collective-permute-start.1 = (bf16[256,2048]{1,0:T(8,128)(2,1)}, bf16[256,2048]{1,0:T(8,128)(2,1)S(1)}, u32[]{:S(2)}, u32[]{:S(2)}) collective-permute-start(bf16[256,2048]{1,0:T(8,128)(2,1)} %get-tuple-element.31), channel_id=1, source_target_pairs={{0,16},{1,17},{2,18},{3,19},{4,20},{5,21},{6,22},{7,23},{8,24},{9,... | collective-permute-start | bytes 3145736 | tf_op jit(solution)/shard_map/ppermute | solution.py:547
  16.0 23.7 %collective-permute-start = (bf16[256,2048]{1,0:T(8,128)(2,1)}, bf16[256,2048]{1,0:T(8,128)(2,1)S(1)}, u32[]{:S(2)}, u32[]{:S(2)}) collective-permute-start(bf16[256,2048]{1,0:T(8,128)(2,1)} %shard_map.118), channel_id=1, source_target_pairs={{0,1},{1,0},{2,3},{3,2},{4,5},{5,4},{6,7},{7,6},{8,9},{9,8},{10,11... | collective-permute-start | bytes 3145736 | tf_op jit(solution)/shard_map/ppermute | solution.py:540
  18.0 40.9 %collective-permute-start.2 = (bf16[256,2048]{1,0:T(8,128)(2,1)}, bf16[256,2048]{1,0:T(8,128)(2,1)S(1)}, u32[]{:S(2)}, u32[]{:S(2)}) collective-permute-start(bf16[256,2048]{1,0:T(8,128)(2,1)} %get-tuple-element.32), channel_id=1, source_target_pairs={{0,17},{1,16},{2,19},{3,18},{4,21},{5,20},{6,23},{7,22},{8,25},{9,... | collective-permute-start | bytes 3145736 | tf_op jit(solution)/shard_map/ppermute | solution.py:547
  23.6 14.4 %collective-permute-start.6 = (bf16[272,512]{1,0:T(8,128)(2,1)S(1)}, bf16[272,512]{1,0:T(8,128)(2,1)S(1)}, u32[]{:S(2)}, u32[]{:S(2)}) collective-permute-start(bf16[272,512]{1,0:T(8,128)(2,1)S(1)} %copy-done.2), channel_id=1, source_target_pairs={{0,8},{1,9},{2,10},{3,11},{4,12},{5,13},{6,14},{7,15},{8,0},{9,1},... | collective-permute-start | bytes 835592 | tf_op jit(solution)/shard_map/ppermute | solution.py:543
  24.4 13.7 %collective-permute-start.7 = (bf16[544,512]{1,0:T(8,128)(2,1)S(1)}, bf16[544,512]{1,0:T(8,128)(2,1)S(1)}, u32[]{:S(2)}, u32[]{:S(2)}) collective-permute-start(bf16[544,512]{1,0:T(8,128)(2,1)S(1)} %pad_maximum_fusion.1), channel_id=1, source_target_pairs={{0,2},{1,3},{2,0},{3,1},{4,6},{5,7},{6,4},{7,5},{8,10},{9,11},{10,... | collective-permute-start | bytes 1671176 | tf_op jit(solution)/shard_map/ppermute | solution.py:540
  38.1 15.5 %collective-permute-start.11 = (bf16[528,512]{1,0:T(8,128)(2,1)S(1)}, bf16[528,512]{1,0:T(8,128)(2,1)S(1)}, u32[]{:S(2)}, u32[]{:S(2)}) collective-permute-start(bf16[528,512]{1,0:T(8,128)(2,1)S(1)} %pad_maximum_fusion.2), channel_id=1, source_target_pairs={{0,2},{1,3},{2,0},{3,1},{4,6},{5,7},{6,4},{7,5},{8,10},{9,11},{10,... | collective-permute-start | bytes 1622024 | tf_op jit(solution)/shard_map/ppermute | solution.py:540
  39.6 9.6 %collective-permute-start.8 = (bf16[256,512]{1,0:T(8,128)(2,1)S(1)}, bf16[256,512]{1,0:T(8,128)(2,1)S(1)}, u32[]{:S(2)}, u32[]{:S(2)}) collective-permute-start(bf16[256,512]{1,0:T(8,128)(2,1)S(1)} %copy-done.3), channel_id=1, source_target_pairs={{0,12},{1,13},{2,14},{3,15},{4,0},{5,1},{6,2},{7,3},{8,4},{9,5},{1... | collective-permute-start | bytes 786440 | tf_op jit(solution)/shard_map/ppermute | solution.py:543
  42.5 10.8 %collective-permute-start.9 = (bf16[256,512]{1,0:T(8,128)(2,1)S(1)}, bf16[256,512]{1,0:T(8,128)(2,1)S(1)}, u32[]{:S(2)}, u32[]{:S(2)}) collective-permute-start(bf16[256,512]{1,0:T(8,128)(2,1)S(1)} %copy-done.3), channel_id=1, source_target_pairs={{0,4},{1,5},{2,6},{3,7},{4,8},{5,9},{6,10},{7,11},{8,12},{9,13},{1... | collective-permute-start | bytes 786440 | tf_op jit(solution)/shard_map/ppermute | solution.py:543
  53.2 13.9 %collective-permute-start.10 = (bf16[256,512]{1,0:T(8,128)(2,1)S(1)}, bf16[256,512]{1,0:T(8,128)(2,1)S(1)}, u32[]{:S(2)}, u32[]{:S(2)}) collective-permute-start(bf16[256,512]{1,0:T(8,128)(2,1)S(1)} %copy-done.3), channel_id=1, source_target_pairs={{0,8},{1,9},{2,10},{3,11},{4,12},{5,13},{6,14},{7,15},{8,0},{9,1},... | collective-permute-start | bytes 786440 | tf_op jit(solution)/shard_map/ppermute | solution.py:543
  53.6 2.2 %copy-start = (bf16[1,256,8192]{2,1,0:T(8,128)(2,1)S(1)}, bf16[1,256,8192]{2,1,0:T(8,128)(2,1)}, u32[]{:S(2)}) copy-start(bf16[1,256,8192]{2,1,0:T(8,128)(2,1)} %param.12) | copy-start | bytes 12582916
  58.9 16.4 %copy-start.1 = (bf16[1,256,8192]{2,1,0:T(8,128)(2,1)S(1)}, bf16[1,256,8192]{2,1,0:T(8,128)(2,1)}, u32[]{:S(2)}) copy-start(bf16[1,256,8192]{2,1,0:T(8,128)(2,1)} %param.12) | copy-start | bytes 12582916
  60.1 4.0 %copy-start.4 = (bf16[512,256]{1,0:T(8,128)(2,1)S(1)}, bf16[512,256]{1,0:T(8,128)(2,1)}, u32[]{:S(2)}) copy-start(bf16[512,256]{1,0:T(8,128)(2,1)} %down_ref.1) | copy-start | bytes 786436
  60.1 2.0 %collective-permute-start.12 = (f32[256,512]{1,0:T(8,128)S(1)}, f32[256,512]{1,0:T(8,128)S(1)}, u32[]{:S(2)}, u32[]{:S(2)}) collective-permute-start(f32[256,512]{1,0:T(8,128)S(1)} %bitcast.23), channel_id=1, source_target_pairs={{0,1},{1,0},{2,3},{3,2},{4,5},{5,4},{6,7},{7,6},{8,9},{9,8},{10,11... | collective-permute-start | bytes 1572872 | tf_op jit(solution)/shard_map/ppermute | solution.py:540
  60.5 14.8 %collective-permute-start.18 = (bf16[512,512]{1,0:T(8,128)(2,1)S(1)}, bf16[512,512]{1,0:T(8,128)(2,1)S(1)}, u32[]{:S(2)}, u32[]{:S(2)}) collective-permute-start(bf16[512,512]{1,0:T(8,128)(2,1)S(1)} %pad_maximum_fusion.3), channel_id=1, source_target_pairs={{0,2},{1,3},{2,0},{3,1},{4,6},{5,7},{6,4},{7,5},{8,10},{9,11},{10,... | collective-permute-start | bytes 1572872 | tf_op jit(solution)/shard_map/ppermute | solution.py:540
  62.2 1.9 %collective-permute-start.15 = (bf16[128,512]{1,0:T(8,128)(2,1)S(1)}, bf16[128,512]{1,0:T(8,128)(2,1)S(1)}, u32[]{:S(2)}, u32[]{:S(2)}) collective-permute-start(bf16[128,512]{1,0:T(8,128)(2,1)S(1)} %get-tuple-element.42), channel_id=1, source_target_pairs={{0,1},{1,0},{2,3},{3,2},{4,5},{5,4},{6,7},{7,6},{8,9},{9,8},{10,11... | collective-permute-start | bytes 393224 | tf_op jit(solution)/shard_map/ppermute | solution.py:540
  62.6 17.6 %collective-permute-start.14 = (f32[256,512]{1,0:T(8,128)S(1)}, f32[256,512]{1,0:T(8,128)S(1)}, u32[]{:S(2)}, u32[]{:S(2)}) collective-permute-start(f32[256,512]{1,0:T(8,128)S(1)} %fusion.1), channel_id=1, source_target_pairs={{0,16},{1,17},{2,18},{3,19},{4,20},{5,21},{6,22},{7,23},{8,24},{9,... | collective-permute-start | bytes 1572872 | tf_op jit(solution)/shard_map/ppermute | solution.py:547
  64.6 9.2 %collective-permute-start.16 = (bf16[8,1,16,512]{3,2,1,0:T(8,128)(2,1)S(1)}, bf16[8,1,16,512]{3,2,1,0:T(8,128)(2,1)S(1)}, u32[]{:S(2)}, u32[]{:S(2)}) collective-permute-start(bf16[8,1,16,512]{3,2,1,0:T(8,128)(2,1)S(1)} %get-tuple-element.75), channel_id=1, source_target_pairs={{0,8},{1,9},{2,10},{3,11},{4,12},{5,13},{6,14},{7,15},{8,0},{9,1},... | collective-permute-start | bytes 393224 | tf_op jit(solution)/shard_map/ppermute | solution.py:540
  67.2 13.0 %collective-permute-start.13 = (bf16[256,512]{1,0:T(8,128)(2,1)S(1)}, bf16[256,512]{1,0:T(8,128)(2,1)S(1)}, u32[]{:S(2)}, u32[]{:S(2)}) collective-permute-start(bf16[256,512]{1,0:T(8,128)(2,1)S(1)} %collective-permute-done.10.refs_8_), channel_id=1, source_target_pairs={{0,2},{1,3},{2,0},{3,1},{4,6},{5,7},{6,4},{7,5},{8,10},{9,11},{10,... | collective-permute-start | bytes 786440 | tf_op jit(solution)/shard_map/ppermute | solution.py:540
  73.7 6.4 %collective-permute-start.17 = (bf16[4,2,16,512]{3,2,1,0:T(8,128)(2,1)S(1)}, bf16[4,2,16,512]{3,2,1,0:T(8,128)(2,1)S(1)}, u32[]{:S(2)}, u32[]{:S(2)}) collective-permute-start(bf16[4,2,16,512]{3,2,1,0:T(8,128)(2,1)S(1)} %fusion.5), channel_id=1, source_target_pairs={{0,4},{1,5},{2,6},{3,7},{4,0},{5,1},{6,2},{7,3},{8,12},{9,13},{10,... | collective-permute-start | bytes 393224 | tf_op jit(solution)/shard_map/ppermute | solution.py:540
  81.4 2.7 %collective-permute-start.19 = (f32[2,256,512]{2,1,0:T(8,128)S(1)}, f32[2,256,512]{2,1,0:T(8,128)S(1)}, u32[]{:S(2)}, u32[]{:S(2)}) collective-permute-start(f32[2,256,512]{2,1,0:T(8,128)S(1)} %pad_maximum_fusion), channel_id=1, source_target_pairs={{0,1},{1,0},{2,3},{3,2},{4,5},{5,4},{6,7},{7,6},{8,9},{9,8},{10,11... | collective-permute-start | bytes 3145736 | tf_op jit(solution)/shard_map/ppermute | solution.py:540
  81.5 6.2 %copy-start.6 = (f32[128]{0:T(128)S(1)}, f32[128]{0:T(128)}, u32[]{:S(2)}) copy-start(f32[128]{0:T(128)} %param.17) | copy-start | bytes 1540
  81.5 6.2 %collective-permute-start.23 = (f32[256,512]{1,0:T(8,128)S(1)}, f32[256,512]{1,0:T(8,128)S(1)}, u32[]{:S(2)}, u32[]{:S(2)}) collective-permute-start(f32[256,512]{1,0:T(8,128)S(1)} %slice_bitcast_fusion), channel_id=1, source_target_pairs={{0,1},{1,0},{2,3},{3,2},{4,5},{5,4},{6,7},{7,6},{8,9},{9,8},{10,11... | collective-permute-start | bytes 1572872 | tf_op jit(solution)/shard_map/ppermute | solution.py:540
  82.2 5.5 %collective-permute-start.21 = (bf16[2,4,16,512]{3,2,1,0:T(8,128)(2,1)S(1)}, bf16[2,4,16,512]{3,2,1,0:T(8,128)(2,1)S(1)}, u32[]{:S(2)}, u32[]{:S(2)}) collective-permute-start(bf16[2,4,16,512]{3,2,1,0:T(8,128)(2,1)S(1)} %get-tuple-element.74), channel_id=1, source_target_pairs={{0,2},{1,3},{2,0},{3,1},{4,6},{5,7},{6,4},{7,5},{8,10},{9,11},{10,... | collective-permute-start | bytes 393224 | tf_op jit(solution)/shard_map/ppermute | solution.py:540
  84.2 8.4 %collective-permute-start.20 = (bf16[256,512]{1,0:T(8,128)(2,1)S(1)}, bf16[256,512]{1,0:T(8,128)(2,1)S(1)}, u32[]{:S(2)}, u32[]{:S(2)}) collective-permute-start(bf16[256,512]{1,0:T(8,128)(2,1)S(1)} %fusion.2), channel_id=1, source_target_pairs={{0,16},{1,17},{2,18},{3,19},{4,20},{5,21},{6,22},{7,23},{8,24},{9,... | collective-permute-start | bytes 786440 | tf_op jit(solution)/shard_map/ppermute | solution.py:547
  87.7 1.4 %collective-permute-start.22 = (bf16[1,8,16,512]{3,2,1,0:T(8,128)(2,1)S(1)}, bf16[1,8,16,512]{3,2,1,0:T(8,128)(2,1)S(1)}, u32[]{:S(2)}, u32[]{:S(2)}) collective-permute-start(bf16[1,8,16,512]{3,2,1,0:T(8,128)(2,1)S(1)} %get-tuple-element.72), channel_id=1, source_target_pairs={{0,1},{1,0},{2,3},{3,2},{4,5},{5,4},{6,7},{7,6},{8,9},{9,8},{10,11... | collective-permute-start | bytes 393224 | tf_op jit(solution)/shard_map/ppermute | solution.py:540
  87.8 1.3 %copy-start.5 = (bf16[16,16,512]{2,1,0:T(8,128)(2,1)S(1)}, bf16[16,16,512]{2,1,0:T(8,128)(2,1)}, u32[]{:S(2)}) copy-start(bf16[16,16,512]{2,1,0:T(8,128)(2,1)} %up_ref.1) | copy-start | bytes 786436
  93.0 1.9 %collective-permute-start.24 = (bf16[4,48,128]{2,1,0:T(8,128)(2,1)S(1)}, bf16[4,48,128]{2,1,0:T(8,128)(2,1)S(1)}, u32[]{:S(2)}, u32[]{:S(2)}) collective-permute-start(bf16[4,48,128]{2,1,0:T(8,128)(2,1)S(1)} %get-tuple-element.50), channel_id=1, source_target_pairs={{0,1},{1,0},{2,3},{3,2},{4,5},{5,4},{6,7},{7,6},{8,9},{9,8},{10,11... | collective-permute-start | bytes 147464 | tf_op jit(solution)/shard_map/ppermute | solution.py:540
  93.1 4.6 %collective-permute-start.25 = (bf16[4,48,128]{2,1,0:T(8,128)(2,1)S(1)}, bf16[4,48,128]{2,1,0:T(8,128)(2,1)S(1)}, u32[]{:S(2)}, u32[]{:S(2)}) collective-permute-start(bf16[4,48,128]{2,1,0:T(8,128)(2,1)S(1)} %get-tuple-element.51), channel_id=1, source_target_pairs={{0,2},{1,3},{2,0},{3,1},{4,6},{5,7},{6,4},{7,5},{8,10},{9,11},{10,... | collective-permute-start | bytes 147464 | tf_op jit(solution)/shard_map/ppermute | solution.py:540
  93.7 4.2 %collective-permute-start.26 = (bf16[4,48,128]{2,1,0:T(8,128)(2,1)S(1)}, bf16[4,48,128]{2,1,0:T(8,128)(2,1)S(1)}, u32[]{:S(2)}, u32[]{:S(2)}) collective-permute-start(bf16[4,48,128]{2,1,0:T(8,128)(2,1)S(1)} %get-tuple-element.52), channel_id=1, source_target_pairs={{0,3},{1,2},{2,1},{3,0},{4,7},{5,6},{6,5},{7,4},{8,11},{9,10},{10,... | collective-permute-start | bytes 147464 | tf_op jit(solution)/shard_map/ppermute | solution.py:540
  98.0 6.7 %collective-permute-start.27 = (f32[40,128]{1,0:T(8,128)S(1)}, f32[40,128]{1,0:T(8,128)S(1)}, u32[]{:S(2)}, u32[]{:S(2)}) collective-permute-start(f32[40,128]{1,0:T(8,128)S(1)} %get-tuple-element.54), channel_id=1, source_target_pairs={{0,4},{1,5},{2,6},{3,7},{4,8},{5,9},{6,10},{7,11},{8,12},{9,13},{1... | collective-permute-start | bytes 61448 | tf_op jit(solution)/shard_map/ppermute | solution.py:543
  100.4 4.7 %collective-permute-start.28 = (f32[40,128]{1,0:T(8,128)S(1)}, f32[40,128]{1,0:T(8,128)S(1)}, u32[]{:S(2)}, u32[]{:S(2)}) collective-permute-start(f32[40,128]{1,0:T(8,128)S(1)} %get-tuple-element.55), channel_id=1, source_target_pairs={{0,8},{1,9},{2,10},{3,11},{4,12},{5,13},{6,14},{7,15},{8,0},{9,1},... | collective-permute-start | bytes 61448 | tf_op jit(solution)/shard_map/ppermute | solution.py:543
  103.3 3.8 %collective-permute-start.29 = (f32[40,128]{1,0:T(8,128)S(1)}, f32[40,128]{1,0:T(8,128)S(1)}, u32[]{:S(2)}, u32[]{:S(2)}) collective-permute-start(f32[40,128]{1,0:T(8,128)S(1)} %get-tuple-element.56), channel_id=1, source_target_pairs={{0,12},{1,13},{2,14},{3,15},{4,0},{5,1},{6,2},{7,3},{8,4},{9,5},{1... | collective-permute-start | bytes 61448 | tf_op jit(solution)/shard_map/ppermute | solution.py:543
